TPU v7x, 32 devices: a whole 2x2x4 slice. The times are simulated.
32 devices in a mesh: ha: 8 (over y, x, core), wa: 4 (over z).
Axes of the slice: x: 2, y: 2, z: 4, core: 2. Of those that a mesh axis runs over, the one named last changes fastest.
Arguments:
- features: bfloat16 [4, 208, 20, 2048], P(None, 'ha', 'wa'), may hold values from -6 to 6
- row_image: int32 [4, 208], replicated, may hold values from 0 to 15, never falling along the last dimension, each value on 1 to 33 neighbouring positions
- cotangent: bfloat16 [4, 208, 20, 256], P(None, 'ha', 'wa'), may hold values from -6 to 6
- w_one: bfloat16 [2048, 256], P('ha', 'wa'), may hold values from -0.125 to 0.125
- dilated_weight: bfloat16 [3, 9, 2048, 256], P(None, None, 'ha', 'wa'), may hold values from -0.046875 to 0.046875
- w_pool: bfloat16 [2048, 256], P('ha', 'wa'), may hold values from -0.125 to 0.125
- w_proj: bfloat16 [1280, 256], P('ha', 'wa'), may hold values from -0.15625 to 0.15625
- scales: float32 [5, 256], replicated, may hold values from 0.5 to 1.5
- shifts: float32 [5, 256], replicated, may hold values from -3 to 3
- out_scale: float32 [256], replicated, may hold values from 0.5 to 1.5
- out_shift: float32 [256], replicated, may hold values from -3 to 3
Outputs:
- activations: bfloat16 [4, 208, 20, 256], P(None, 'ha', 'wa')
- feature_grad: bfloat16 [4, 208, 20, 2048], P(None, 'ha', 'wa')
- w_one_grad: float32 [2048, 256], P('ha', 'wa')
- w_atrous_grad: float32 [3, 9, 2048, 256], P(None, None, 'ha', 'wa')
- w_pool_grad: float32 [2048, 256], P('ha', 'wa')
- w_proj_grad: float32 [1280, 256], P('ha', 'wa')
- scales_grad: float32 [5, 256], replicated
- shifts_grad: float32 [5, 256], replicated
- out_scale_grad: float32 [256], replicated
- out_shift_grad: float32 [256], replicated
Inputs may be any that keep to these rules, and one draw needn't show every extreme that they name: In each micro-batch, row_image never falls along the height and each of the 16 images holds 1 to 33 whole rows, one of them exactly 33.
All inputs are finite; a program needn't handle non-finite values.
Results may differ from a plain program's by a relative error of at most 0.015.
Values may be sent and summed in bfloat16 or wider, within the bound.
No kernel may reach another device: no remote copies, remote signals or barrier semaphores. Data moves between devices by JAX's collectives and lax.ppermute only.
A program may use at most 896 MiB of HBM per device.

v0:
```python
import jax
import jax.numpy as jnp
from jax import lax
from jax.sharding import PartitionSpec as P

IMG_DEV = 2
REACH = 18
PADC = 7


dilation_rates = (6, 12, 18)
epsilon = 1e-05
highest = lax.Precision.HIGHEST


def with_halo(array, sides, width):
    for axis, dim in sides:
        count, length = (lax.axis_size(axis), array.shape[dim])
        up = [(i, (i + 1) % count) for i in range(count - 1)]
        down = [(j, i) for i, j in up]
        last = lax.slice_in_dim(array, length - width, length, axis=dim)
        leading = lax.slice_in_dim(array, 0, width, axis=dim)
        before = lax.ppermute(last, axis, up)
        after = lax.ppermute(leading, axis, down)
        array = jnp.concatenate([before, array, after], axis=dim)
    return array


def smooth_gate(inputs):
    return inputs * jax.nn.sigmoid(inputs)


def gate_slope(inputs):
    sigmoid_part = jax.nn.sigmoid(inputs)
    return sigmoid_part * (1.0 + inputs * (1.0 - sigmoid_part))


def fetch_each(w_one, dilated_weight, w_pool, w_proj):
    row_full = (
        lax.all_gather(w_one, "ha", axis=0, tiled=True),
        lax.all_gather(dilated_weight, "ha", axis=2, tiled=True),
        lax.all_gather(w_pool, "ha", axis=0, tiled=True),
        lax.all_gather(w_proj, "ha", axis=0, tiled=True),
    )
    return (
        lax.all_gather(row_full[0], "wa", axis=1, tiled=True),
        lax.all_gather(row_full[1], "wa", axis=3, tiled=True),
        lax.all_gather(row_full[2], "wa", axis=1, tiled=True),
        lax.all_gather(row_full[3], "wa", axis=1, tiled=True),
    )


def tap_stack(
    padded_input,
    padded_row_labels,
    start_row,
    start_col,
    rate_value,
    direction,
    row_count,
    col_count,
    reach_rows,
):
    own_ids = lax.dynamic_slice_in_dim(padded_row_labels, reach_rows + start_row, row_count)
    windows = []
    for step_row in (-1, 0, 1):
        for step_col in (-1, 0, 1):
            offset_row = direction * step_row * rate_value
            offset_col = direction * step_col * rate_value
            window = lax.dynamic_slice(
                padded_input,
                (reach_rows + offset_row, reach_rows + offset_col + start_col, 0),
                (row_count, col_count, padded_input.shape[2]),
            )
            source_ids = lax.dynamic_slice_in_dim(
                padded_row_labels, reach_rows + start_row + offset_row, row_count
            )
            row_match = (source_ids == own_ids).astype(padded_input.dtype)
            windows.append(window * row_match[:, None, None])
    return jnp.stack(windows)


def local(
    features,
    row_image,
    cotangent,
    w_one,
    dilated_weight,
    w_pool,
    w_proj,
    scales,
    shifts,
    out_scale,
    out_shift,
):
    count_mb, row_count, col_count, channel_count = features.shape
    output_width = w_one.shape[1] * lax.axis_size("wa")
    height = row_count * lax.axis_size("ha")
    width = col_count * lax.axis_size("wa")
    valid = width - PADC
    pixel_total = float(height * valid)
    image_count = IMG_DEV * lax.axis_size("ha")
    reach_rows = REACH
    start_row = lax.axis_index("ha") * row_count
    start_col = lax.axis_index("wa") * col_count
    col_mask = (start_col + jnp.arange(col_count, dtype=jnp.int32) < valid).astype(jnp.float32)
    col_weight = col_mask[None, :, None]
    mask_low = col_mask.astype(jnp.bfloat16)[None, :, None]
    labels = jnp.arange(image_count, dtype=jnp.int32)
    pool_rows0 = lax.axis_index("ha") * w_pool.shape[0]
    pool_cols0 = lax.axis_index("wa") * w_pool.shape[1]
    grad_one = jnp.zeros((channel_count, output_width), jnp.float32)
    dilated_gradient = [
        jnp.zeros((9, channel_count, output_width), jnp.float32) for dilation_index in range(3)
    ]
    grad_proj = jnp.zeros((5 * output_width, output_width), jnp.float32)
    grad_pool = jnp.zeros(w_pool.shape, jnp.float32)
    grad_scales = jnp.zeros((5, output_width), jnp.float32)
    grad_shifts = jnp.zeros((5, output_width), jnp.float32)
    grad_out_scale = jnp.zeros((output_width,), jnp.float32)
    grad_out_shift = jnp.zeros((output_width,), jnp.float32)
    act_outputs = []
    feature_grads = []
    for batch_index in range(count_mb):
        full_one, whole_dilated_conv, full_pool, full_proj = fetch_each(
            w_one, dilated_weight, w_pool, w_proj
        )
        row_labels = row_image[batch_index]
        padded_row_labels = jnp.pad(row_labels, (reach_rows, reach_rows), constant_values=-1)
        own_ids = lax.dynamic_slice_in_dim(padded_row_labels, reach_rows + start_row, row_count)
        images = (own_ids[:, None] == labels[None, :]).astype(jnp.float32)
        counts = (
            jnp.sum((row_labels[:, None] == labels[None, :]).astype(jnp.float32), axis=0) * valid
        )
        masked = features[batch_index] * mask_low
        rim_rows = with_halo(masked, (("ha", 0),), reach_rows)
        wide_rows = lax.all_gather(rim_rows, "wa", axis=1, tiled=True)
        padded_input = jnp.pad(wide_rows, ((0, 0), (reach_rows, reach_rows), (0, 0)))
        branch_list = [
            jnp.einsum("rcd,de->rce", masked, full_one, preferred_element_type=jnp.float32)
        ]
        stacked_taps = []
        for dilation_index in range(3):
            stack_fwd = tap_stack(
                padded_input,
                padded_row_labels,
                start_row,
                start_col,
                dilation_rates[dilation_index],
                1,
                row_count,
                col_count,
                reach_rows,
            )
            stacked_taps.append(stack_fwd)
            branch_list.append(
                jnp.einsum(
                    "trcd,tde->rce",
                    stack_fwd,
                    whole_dilated_conv[dilation_index],
                    preferred_element_type=jnp.float32,
                )
            )
        stacked = jnp.stack(branch_list)
        row_sums = jnp.sum(masked, axis=1, dtype=jnp.float32)
        partial_pool = jnp.dot(images.T, row_sums, precision=highest)
        first_part = jnp.sum(stacked * col_weight[None], axis=(1, 2))
        second_part = jnp.sum(stacked * stacked * col_weight[None], axis=(1, 2))
        pool_sums, first_sum, second_sum = lax.psum(
            (partial_pool, first_part, second_part), ("ha", "wa")
        )
        branch_mean = first_sum / pixel_total
        branch_rstd = lax.rsqrt(second_sum / pixel_total - branch_mean * branch_mean + epsilon)
        norm_branch = (stacked - branch_mean[:, None, None, :]) * branch_rstd[:, None, None, :]
        hid_branch = norm_branch * scales[:4, None, None, :] + shifts[:4, None, None, :]
        act_branch = smooth_gate(hid_branch)
        pooled = (pool_sums / counts[:, None]).astype(jnp.bfloat16)
        pool_out = jnp.dot(pooled, full_pool, preferred_element_type=jnp.float32)
        weighted = counts[:, None]
        pool_first = jnp.sum(weighted * pool_out, axis=0) / pixel_total
        pool_second = jnp.sum(weighted * pool_out * pool_out, axis=0) / pixel_total
        pool_rstd = lax.rsqrt(pool_second - pool_first * pool_first + epsilon)
        pool_norm = (pool_out - pool_first) * pool_rstd
        pool_hid = pool_norm * scales[4] + shifts[4]
        pool_act = smooth_gate(pool_hid)
        spread = jnp.dot(images, pool_act, precision=highest)
        spread_wide = jnp.broadcast_to(spread[:, None, :], (row_count, col_count, output_width))
        joined = jnp.concatenate(
            [act_branch[0], act_branch[1], act_branch[2], act_branch[3], spread_wide], axis=-1
        ).astype(jnp.bfloat16)
        projected = jnp.einsum("rck,ke->rce", joined, full_proj, preferred_element_type=jnp.float32)
        proj_first, proj_second = lax.psum(
            (
                jnp.sum(projected * col_weight, axis=(0, 1)),
                jnp.sum(projected * projected * col_weight, axis=(0, 1)),
            ),
            ("ha", "wa"),
        )
        proj_mean = proj_first / pixel_total
        proj_rstd = lax.rsqrt(proj_second / pixel_total - proj_mean * proj_mean + epsilon)
        proj_norm = (projected - proj_mean) * proj_rstd
        proj_hid = proj_norm * out_scale + out_shift
        act_outputs.append((smooth_gate(proj_hid) * col_weight).astype(jnp.bfloat16))
        dproj_hid = cotangent[batch_index].astype(jnp.float32) * col_weight * gate_slope(proj_hid)
        shift_sum, scale_sum = lax.psum(
            (jnp.sum(dproj_hid, axis=(0, 1)), jnp.sum(dproj_hid * proj_norm, axis=(0, 1))),
            ("ha", "wa"),
        )
        grad_out_shift = grad_out_shift + shift_sum
        grad_out_scale = grad_out_scale + scale_sum
        dproj = (
            out_scale
            * proj_rstd
            * (dproj_hid - (shift_sum + proj_norm * scale_sum) / pixel_total)
            * col_weight
        ).astype(jnp.bfloat16)
        djoined = jnp.einsum("rce,ke->rck", dproj, full_proj, preferred_element_type=jnp.float32)
        grad_proj = grad_proj + jnp.einsum(
            "rck,rce->ke", joined, dproj, preferred_element_type=jnp.float32
        )
        dact_branch = jnp.moveaxis(
            djoined[..., : 4 * output_width].reshape(row_count, col_count, 4, output_width), 2, 0
        )
        dact_pool = djoined[..., 4 * output_width :]
        pool_part = jnp.dot(images.T, jnp.sum(dact_pool, axis=1), precision=highest)
        dhid_branch = dact_branch * gate_slope(hid_branch) * col_weight[None]
        branch_shift, branch_scale, pool_total = lax.psum(
            (
                jnp.sum(dhid_branch, axis=(1, 2)),
                jnp.sum(dhid_branch * norm_branch, axis=(1, 2)),
                pool_part,
            ),
            ("ha", "wa"),
        )
        branch_gradient = (
            scales[:4, None, None, :]
            * branch_rstd[:, None, None, :]
            * (
                dhid_branch
                - (branch_shift[:, None, None, :] + norm_branch * branch_scale[:, None, None, :])
                / pixel_total
            )
            * col_weight[None]
        ).astype(jnp.bfloat16)
        dpool_hid = gate_slope(pool_hid) * pool_total
        pool_shift = jnp.sum(dpool_hid, axis=0)
        pool_scale = jnp.sum(dpool_hid * pool_norm, axis=0)
        dpool = (
            scales[4]
            * pool_rstd
            * (dpool_hid - weighted * (pool_shift + pool_norm * pool_scale) / pixel_total)
        ).astype(jnp.bfloat16)
        grad_scales = grad_scales + jnp.concatenate([branch_scale, pool_scale[None]], axis=0)
        grad_shifts = grad_shifts + jnp.concatenate([branch_shift, pool_shift[None]], axis=0)
        dpooled = jnp.dot(dpool, full_pool.T, preferred_element_type=jnp.float32)
        pooled_slice = lax.dynamic_slice_in_dim(pooled, pool_rows0, w_pool.shape[0], 1)
        dpool_slice = lax.dynamic_slice_in_dim(dpool, pool_cols0, w_pool.shape[1], 1)
        grad_pool = grad_pool + jnp.dot(
            pooled_slice.T, dpool_slice, preferred_element_type=jnp.float32
        )
        grad_one = grad_one + jnp.einsum(
            "rcd,rce->de", masked, branch_gradient[0], preferred_element_type=jnp.float32
        )
        for dilation_index in range(3):
            dilated_gradient[dilation_index] = dilated_gradient[dilation_index] + jnp.einsum(
                "trcd,rce->tde",
                stacked_taps[dilation_index],
                branch_gradient[dilation_index + 1],
                preferred_element_type=jnp.float32,
            )
        grad_send = jnp.concatenate(
            [branch_gradient[1], branch_gradient[2], branch_gradient[3]], axis=-1
        )
        grad_rows = with_halo(grad_send, (("ha", 0),), reach_rows)
        grad_wide = lax.all_gather(grad_rows, "wa", axis=1, tiled=True)
        padded_gradient = jnp.pad(grad_wide, ((0, 0), (reach_rows, reach_rows), (0, 0)))
        input_grad = jnp.einsum(
            "rce,de->rcd", branch_gradient[0], full_one, preferred_element_type=jnp.float32
        )
        for dilation_index in range(3):
            channel_section = padded_gradient[
                ..., dilation_index * output_width : (dilation_index + 1) * output_width
            ]
            stack_back = tap_stack(
                channel_section,
                padded_row_labels,
                start_row,
                start_col,
                dilation_rates[dilation_index],
                -1,
                row_count,
                col_count,
                reach_rows,
            )
            input_grad = input_grad + jnp.einsum(
                "trce,tde->rcd",
                stack_back,
                whole_dilated_conv[dilation_index],
                preferred_element_type=jnp.float32,
            )
        pool_rows = jnp.dot(images, dpooled / counts[:, None], precision=highest)
        feature_grads.append(
            ((input_grad + pool_rows[:, None, :]) * col_weight).astype(jnp.bfloat16)
        )
    col_parts = (
        lax.psum_scatter(
            grad_one.astype(jnp.bfloat16), "wa", scatter_dimension=1, tiled=True
        ).astype(jnp.float32),
        lax.psum_scatter(
            jnp.stack(dilated_gradient).astype(jnp.bfloat16), "wa", scatter_dimension=3, tiled=True
        ).astype(jnp.float32),
        lax.psum_scatter(
            grad_proj.astype(jnp.bfloat16), "wa", scatter_dimension=1, tiled=True
        ).astype(jnp.float32),
    )
    final_parts = (
        lax.psum_scatter(
            col_parts[0].astype(jnp.bfloat16), "ha", scatter_dimension=0, tiled=True
        ).astype(jnp.float32),
        lax.psum_scatter(
            col_parts[1].astype(jnp.bfloat16), "ha", scatter_dimension=2, tiled=True
        ).astype(jnp.float32),
        lax.psum_scatter(
            col_parts[2].astype(jnp.bfloat16), "ha", scatter_dimension=0, tiled=True
        ).astype(jnp.float32),
    )
    one_out, atrous_out, proj_out = (final_parts[0], final_parts[1], final_parts[2])
    return (
        jnp.stack(act_outputs),
        jnp.stack(feature_grads),
        one_out,
        atrous_out,
        grad_pool,
        proj_out,
        grad_scales,
        grad_shifts,
        grad_out_scale,
        grad_out_shift,
    )


def solution(mesh):
    in_specs = (
        P(None, "ha", "wa", None),
        P(),
        P(None, "ha", "wa", None),
        P("ha", "wa"),
        P(None, None, "ha", "wa"),
        P("ha", "wa"),
        P("ha", "wa"),
        P(),
        P(),
        P(),
        P(),
    )
    out_specs = (
        P(None, "ha", "wa", None),
        P(None, "ha", "wa", None),
        P("ha", "wa"),
        P(None, None, "ha", "wa"),
        P("ha", "wa"),
        P("ha", "wa"),
        P(),
        P(),
        P(),
        P(),
    )
    return jax.shard_map(local, mesh=mesh, in_specs=in_specs, out_specs=out_specs, check_vma=False)
```

profile of v0, /device:TPU:8, one launch (start us, length us, event | category | flops | bytes accessed | tf_op | source)
XLA Modules:
  0.0 3874.3 jit_solution(9421331998077910542)
XLA Ops:
  29.7 11.3 all_gather.32
  41.0 13.6 all_gather.37
  62.4 12.3 collective-permute-start.6
  80.2 11.5 collective-permute-start.4
  114.3 15.2 all-gather
  135.5 26.6 all_gather.80
  162.1 184.7 %all-reduce.26.cloned.1.call-done = (f32[16,2048]{1,0:T(8,128)}, f32[16,2048]{1,0:T(8,128)}, f32[16,2048]{1,0:T(8,128)}, f32[16,2048]{1,0:T(8,128)}) async-done(((f32[16,2048]{1,0:T(8,128)}, f32[16,2048]{1,0:T(8,128)}, f32[16,2048]{1,0:T(8,128)}, f32[16,2048]{1,0:T(8,128)}), (f32[16,2048]{1,0:T(8,128)}, f32[16,2048]{1,0:T(8,128)}, f32[16,2048]{1,0:T(8,128)}, ...) | async-done | bytes 524304 | tf_op jit(solution)/shard_map/psum | solution.py:169
  393.2 34.0 all-gather.26.cloned.1.call-done
  435.6 90.1 %all-gather.24.cloned.1.call-done = bf16[62,20,2048]{2,0,1:T(8,128)(2,1)} async-done(((bf16[62,5,2048]{2,0,1:T(8,128)(2,1)}), bf16[62,20,2048]{2,0,1:T(8,128)(2,1)}) %all-gather.24.cloned.1.call-update) | async-done | bytes 5079056 | tf_op jit(solution)/shard_map/all_gather | solution.py:137
  587.0 414.7 %all-gather.20.cloned.1.call-done = bf16[3,9,2048,256]{2,3,1,0:T(8,128)(2,1)} async-done(((bf16[3,9,2048,64]{2,3,1,0:T(8,128)(2,1)}), bf16[3,9,2048,256]{2,3,1,0:T(8,128)(2,1)}) %all-gather.20.cloned.1.call-update) | async-done | bytes 28311568 | tf_op jit(solution)/shard_map/all_gather | solution.py:47
  1098.7 43.1 %all-reduce.16 = (f32[4,256]{1,0:T(4,128)S(1)}, f32[4,256]{1,0:T(4,128)S(1)}, f32[4,256]{1,0:T(4,128)S(1)}, f32[4,256]{1,0:T(4,128)S(1)}, f32[4,256]{1,0:T(4,128...) all-reduce(f32[4,256]{1,0:T(4,128)S(1)} %get-tuple-element.373, ...), channel_id=1, replica_groups=mesh['ha'=8,'wa'=4] {'ha','wa'}, use_global_device_ids=true, to_apply=%region_29.30 | all-reduce | flops 8192 | bytes 65536 | tf_op jit(solution)/shard_map/psum | solution.py:169
  1147.0 38.6 all-reduce.15
  1190.1 41.7 %all-reduce.14 = (f32[256]{0:T(256)S(1)}, f32[256]{0:T(256)S(1)}, f32[256]{0:T(256)}, f32[256]{0:T(256)}, f32[256]{0:T(256)}, /*index=5*/f32[256]{0:T(256)}, f32[256]{0:T(256)S(1)}, f32[256]{0:T(256)S(1)}) all-reduce(f32[256]{0:T(256)S(1)} %get-tuple-element.309, ...), channel_id=1, replica_groups=mesh['ha'=8,'wa'=4] {'ha','wa'}, use_global_device_ids=true, to_apply=%region_79.80 | all-reduce | flops 2048 | bytes 16384 | tf_op jit(solution)/shard_map/psum | solution.py:205
  1266.2 128.9 %all-reduce.24.cloned.1.call-done = (f32[4,256]{1,0:T(4,128)}, f32[4,256]{1,0:T(4,128)}, f32[4,256]{1,0:T(4,128)}, f32[4,256]{1,0:T(4,128)}, f32[4,256]{1,0:T(4,...) async-done(((f32[4,256]{1,0:T(4,128)}, f32[4,256]{1,0:T(4,128)}, ...) | async-done | bytes 98320 | tf_op jit(solution)/shard_map/psum | solution.py:227
  1410.0 11.8 fusion.141
  1421.9 11.7 fusion.143
  1433.6 11.8 fusion.145
  1457.6 24.7 fusion.5
  1482.3 11.8 fusion.155
  1494.1 11.8 fusion.157
  1508.2 11.8 fusion.138
  1520.0 24.8 fusion.3
  1547.0 11.8 fusion.148
  1560.4 11.9 fusion.150
  1582.2 24.7 fusion.4
  1607.0 20.0 pad_maximum_fusion
  1626.9 59.8 %copy.185 = bf16[3,9,2048,256]{2,0,1,3:T(4,128)(2,1)} copy(bf16[3,9,2048,256]{3,2,1,0:T(8,128)(2,1)} %pad_maximum_fusion) | data formatting | bytes 56623104 | tf_op jit(solution)/shard_map/stack | solution.py:310
  1788.2 1148.2 %all-reduce.22.cloned.1.call-done = bf16[3,9,2048,256]{2,0,1,3:T(4,128)(2,1)} async-done(((bf16[3,9,2048,256]{2,0,1,3:T(4,128)(2,1)}), bf16[3,9,2048,256]{2,0,1,3:T(4,128)(2,1)}) %all-reduce.22.cloned.1.call-update) | async-done | bytes 28311568
  2945.3 358.0 %copy.205 = bf16[3,9,2048,64]{0,1,3,2:T(8,128)(2,1)} copy(bf16[3,9,2048,64]{2,0,1,3:T(4,128)(2,1)} %constant_dynamic-slice_fusion.16) | data formatting | bytes 14155776
  3303.4 381.3 %reshape.390 = bf16[2048,1728]{1,0:T(8,128)(2,1)} reshape(bf16[2048,64,9,3]{3,2,1,0:T(8,128)(2,1)} %bitcast.392) | data formatting | bytes 14155776
  3765.7 40.0 %reshape.391 = bf16[256,64,9,3]{3,2,1,0:T(8,128)(2,1)} reshape(bf16[256,1728]{1,0:T(8,128)(2,1)} %reduce-scatter.16.cloned.1.call-done) | data formatting | bytes 1769472
  3805.8 59.3 %copy.206 = bf16[3,9,256,64]{2,0,1,3:T(4,128)(2,1)S(1)} copy(bf16[3,9,256,64]{0,1,3,2:T(8,128)(2,1)} %bitcast.393) | data formatting | bytes 1769472
  (1029 shorter events, 551.1 us)
Async XLA Ops:
  8.0 104.4 %all-gather.18.cloned.1.call-start = ((), (), s32[]{:S(2)}) async-start(), calls=%async_computation.7 | async-start | bytes 7962624 | tf_op jit(solution)/shard_map/all_gather | solution.py:41
  8.7 338.1 %all-reduce.26.cloned.1.call-start = ((), (), s32[]{:S(2)}) async-start(), calls=%async_computation.24 | async-start | bytes 1048576 | tf_op jit(solution)/shard_map/psum | solution.py:169
  29.6 320.4 %all-gather.14.cloned.1.call-start = ((), (), s32[]{:S(2)}) async-start(), calls=%async_computation.5 | async-start | bytes 1310720 | tf_op jit(solution)/shard_map/all_gather | solution.py:46
  40.9 318.6 %all-gather.22.cloned.1.call-start = ((), (), s32[]{:S(2)}) async-start(), calls=%async_computation.9 | async-start | bytes 1310720 | tf_op jit(solution)/shard_map/all_gather | solution.py:48
  54.6 318.9 %all-gather.16.cloned.1.call-start = ((), (), s32[]{:S(2)}) async-start(), calls=%async_computation.6 | async-start | bytes 6553600 | tf_op jit(solution)/shard_map/all_gather | solution.py:137
  62.3 322.4 %all-gather.28.cloned.1.call-start = ((), (), s32[]{:S(2)}) async-start(), calls=%async_computation.12 | async-start | bytes 6553600 | tf_op jit(solution)/shard_map/all_gather | solution.py:137
  62.4 13.8 collective-permute-start.6
  80.0 347.2 %all-gather.26.cloned.1.call-start = ((), (), s32[]{:S(2)}) async-start(), calls=%async_computation.11 | async-start | bytes 6553600 | tf_op jit(solution)/shard_map/all_gather | solution.py:137
  80.2 13.0 collective-permute-start.4
  96.9 428.7 %all-gather.24.cloned.1.call-start = ((), (), s32[]{:S(2)}) async-start(), calls=%async_computation.10 | async-start | bytes 6553600 | tf_op jit(solution)/shard_map/all_gather | solution.py:137
  97.1 10.8 collective-permute-start.2
  106.5 3.9 collective-permute-start.3
  111.8 889.8 %all-gather.20.cloned.1.call-start = ((), (), s32[]{:S(2)}) async-start(), calls=%async_computation.8 | async-start | bytes 35389440 | tf_op jit(solution)/shard_map/all_gather | solution.py:47
  112.6 1282.5 %all-reduce.24.cloned.1.call-start = ((), (), s32[]{:S(2)}) async-start(), calls=%async_computation.23 | async-start | bytes 196608 | tf_op jit(solution)/shard_map/psum | solution.py:227
  1263.4 182.1 %reduce-scatter.14.cloned.1.call-start = ((), (), s32[]{:S(2)}) async-start(), calls=%async_computation.19 | async-start | bytes 819200 | tf_op jit(solution)/shard_map/reduce_scatter | solution.py:312
  1265.7 184.3 %reduce-scatter.10.cloned.1.call-start = ((), (), s32[]{:S(2)}) async-start(), calls=%async_computation.17 | async-start | bytes 1310720 | tf_op jit(solution)/shard_map/reduce_scatter | solution.py:306
  1400.5 179.8 %collective-permute-start.12 = (bf16[18,5,768]{2,0,1:T(8,128)(2,1)}, bf16[18,5,768]{2,0,1:T(8,128)(2,1)}, u32[]{:S(2)}, u32[]{:S(2)}) collective-permute-start(bf16[18,5,768]{2,0,1:T(8,128)(2,1)} %get-tuple-element.264), channel_id=1, source_target_pairs={{0,4},{4,8},{8,12},{12,16},{16,20},{20,24},{24,28},{1,5},{5,9},{9,... | collective-permute-start | bytes 414728 | tf_op jit(solution)/shard_map/ppermute | solution.py:23
  1403.2 141.7 %collective-permute-start.10 = (bf16[18,5,768]{2,0,1:T(8,128)(2,1)}, bf16[18,5,768]{2,0,1:T(8,128)(2,1)}, u32[]{:S(2)}, u32[]{:S(2)}) collective-permute-start(bf16[18,5,768]{2,0,1:T(8,128)(2,1)} %get-tuple-element.262), channel_id=1, source_target_pairs={{0,4},{4,8},{8,12},{12,16},{16,20},{20,24},{24,28},{1,5},{5,9},{9,... | collective-permute-start | bytes 414728 | tf_op jit(solution)/shard_map/ppermute | solution.py:23
  1421.8 288.6 %reduce-scatter.18.cloned.1.call-start = ((), (), s32[]{:S(2)}) async-start(), calls=%async_computation.21 | async-start | bytes 368640
  1447.3 264.6 %reduce-scatter.12.cloned.1.call-start = ((), (), s32[]{:S(2)}) async-start(), calls=%async_computation.18 | async-start | bytes 294912 | tf_op jit(solution)/shard_map/reduce_scatter | solution.py:317
  1447.4 6.9 collective-permute-start.14
  1448.7 6.9 collective-permute-start.15
  1450.1 263.2 %all-gather.36.cloned.1.call-start = ((), (), s32[]{:S(2)}) async-start(), calls=%async_computation.16 | async-start | bytes 2457600 | tf_op jit(solution)/shard_map/all_gather | solution.py:275
  1450.2 57.0 %collective-permute-start.8 = (bf16[18,5,768]{2,0,1:T(8,128)(2,1)S(1)}, bf16[18,5,768]{2,0,1:T(8,128)(2,1)S(1)}, u32[]{:S(2)}, u32[]{:S(2)}) collective-permute-start(bf16[18,5,768]{2,0,1:T(8,128)(2,1)S(1)} %get-tuple-element.260), channel_id=1, source_target_pairs={{0,4},{4,8},{8,12},{12,16},{16,20},{20,24},{24,28},{1,5},{5,9},{9,... | collective-permute-start | bytes 414728 | tf_op jit(solution)/shard_map/ppermute | solution.py:23
  1454.3 52.9 %collective-permute-start.9 = (bf16[18,5,768]{2,0,1:T(8,128)(2,1)S(1)}, bf16[18,5,768]{2,0,1:T(8,128)(2,1)S(1)}, u32[]{:S(2)}, u32[]{:S(2)}) collective-permute-start(bf16[18,5,768]{2,0,1:T(8,128)(2,1)S(1)} %get-tuple-element.261), channel_id=1, source_target_pairs={{4,0},{8,4},{12,8},{16,12},{20,16},{24,20},{28,24},{5,1},{9,5},{13... | collective-permute-start | bytes 414728 | tf_op jit(solution)/shard_map/ppermute | solution.py:24
  1457.5 266.6 %all-gather.30.cloned.1.call-start = ((), (), s32[]{:S(2)}) async-start(), calls=%async_computation.13 | async-start | bytes 2457600 | tf_op jit(solution)/shard_map/all_gather | solution.py:275
  1505.9 39.0 %collective-permute-start.11 = (bf16[18,5,768]{2,0,1:T(8,128)(2,1)S(1)}, bf16[18,5,768]{2,0,1:T(8,128)(2,1)S(1)}, u32[]{:S(2)}, u32[]{:S(2)}) collective-permute-start(bf16[18,5,768]{2,0,1:T(8,128)(2,1)S(1)} %copy-done.87), channel_id=1, source_target_pairs={{4,0},{8,4},{12,8},{16,12},{20,16},{24,20},{28,24},{5,1},{9,5},{13... | collective-permute-start | bytes 414728 | tf_op jit(solution)/shard_map/ppermute | solution.py:24
  1508.2 224.6 %all-gather.32.cloned.1.call-start = ((), (), s32[]{:S(2)}) async-start(), calls=%async_computation.14 | async-start | bytes 2457600 | tf_op jit(solution)/shard_map/all_gather | solution.py:275
  1546.8 194.4 %all-gather.34.cloned.1.call-start = ((), (), s32[]{:S(2)}) async-start(), calls=%async_computation.15 | async-start | bytes 2457600 | tf_op jit(solution)/shard_map/all_gather | solution.py:275
  1558.9 21.4 collective-permute-start.13
  1582.1 1354.3 %all-reduce.22.cloned.1.call-start = ((), (), s32[]{:S(2)}) async-start(), calls=%async_computation.22 | async-start | bytes 75497472
  1687.2 2078.6 %reduce-scatter.16.cloned.1.call-start = ((), (), s32[]{:S(2)}) async-start(), calls=%async_computation.20 | async-start | bytes 8257536
  (272 other events, 18083.9 us)
Sparse Core Ops, SparseCore 0:
  10.7 52.2 all-gather.17
  64.6 28.1 all-gather.13
  94.4 27.8 all-gather.21
  124.3 105.5 all-gather.15
  231.3 98.1 all-gather.27
  330.9 96.2 all-gather.25
  429.3 96.3 all-gather.23
  527.3 474.3 all-gather.19
  1266.6 19.3 reduce-scatter.13
  1422.0 23.2 reduce-scatter.9
  1449.2 34.4 reduce-scatter.17
  1486.9 33.5 reduce-scatter.11
  1522.7 42.2 all-gather.35
  1566.4 42.3 all-gather.29
  1610.3 42.3 all-gather.31
  1654.1 42.3 all-gather.33
  1698.9 1237.4 all-reduce.21
  3684.9 68.1 reduce-scatter.15
Sparse Core Ops, SparseCore 1:
  29.7 317.1 all-reduce.25
  1263.5 131.6 all-reduce.23
where the time goes:
time: 3910 us; the launch traced here: 3870 us
  waiting for transfers between devices  2010 us (51%)
  local copies, waits for them, and re-layouts  996 us (25%)
  matrix products  406 us (10%)
  blocking collectives  190 us (5%)
  other arithmetic  189 us (5%)
  starting transfers between devices  59.6 us (2%)
    unnamed x23, waiting for transfers between devices  1150 us
    unnamed x623, local copies, waits for them, and re-layouts  903 us
    all_gather x1, waiting for transfers between devices, fetch_each(): lax.all_gather(row_full[1], 'wa', axis=3, tiled=True)  415 us
    psum x1, waiting for transfers between devices, local(): lax.psum((partial_pool, first_part, second_part), ('ha', 'wa'))  185 us
    dot_general x12, matrix products, local(): jnp.einsum('trcd,rce->tde', stacked_taps[dilation_index], branch_gradient...  177 us
    psum x1, waiting for transfers between devices, local(): lax.psum((jnp.sum(dhid_branch, axis=(1, 2)), jnp.sum(dhid_branch * norm_b...  129 us
    all_gather x4, waiting for transfers between devices, local(): wide_rows = lax.all_gather(rim_rows, 'wa', axis=1, tiled=True)  124 us
    dot_general x12, matrix products, local(): jnp.einsum('trcd,tde->rce', stack_fwd, whole_dilated_conv[dilation_index]...  95.8 us
  transfers between devices with their start and end apart: 36, of which 13 were waited for; matrix products, arithmetic and copies ran while one was open for 15% of the time, Pallas kernels for 0%

commit v1 on v0

v1 whole, which is shorter than its diff:
```python
from functools import partial

import jax
import jax.numpy as jnp
from jax import lax
from jax.experimental import pallas as pl
from jax.experimental.pallas import tpu as pltpu
from jax.sharding import PartitionSpec as P

PADC = 7
IMG_DEV = 2
RATES = (6, 12, 18)
EPS = 1e-05
HIGHEST = lax.Precision.HIGHEST
F32 = jnp.float32
BF16 = jnp.bfloat16


def silu(u):
    return u * jax.nn.sigmoid(u)


def silu_slope(u):
    s = jax.nn.sigmoid(u)
    return s * (1.0 + u * (1.0 - s))


def swap(array, axis, bits, sources=None):
    count = lax.axis_size(axis)
    pairs = [(i, i ^ bits) for i in range(count) if sources is None or sources(i)]
    return lax.ppermute(array, axis, pairs)


def tree_sum(parts):
    while len(parts) > 1:
        parts = [parts[i] + parts[i + 1] for i in range(0, len(parts), 2)]
    return parts[0]


def plane_sum(array, groups):
    total = tree_sum([array] + [swap(array, "ha", k) for k in range(1, lax.axis_size("ha"))])
    bits = 1
    while bits < groups:
        total = total + swap(total, "wa", bits)
        bits *= 2
    return total


def take(array, index):
    return lax.dynamic_index_in_dim(array, index, 0, keepdims=False)


def by_distance(array):
    h = lax.axis_index("ha")
    return jnp.stack([take(array, h ^ k) for k in range(array.shape[0])])


def reduce_chunks(even, odd, groups):
    other = swap(odd, "ha", 1)
    both = [even[q].astype(F32) + other[q].astype(F32) for q in range(even.shape[0])]
    got = [swap(both[q].astype(BF16), "ha", 2 * q) for q in range(1, even.shape[0])]
    total = tree_sum([both[0]] + [part.astype(F32) for part in got])
    bits = 1
    while bits < groups:
        total = total + swap(total.astype(BF16), "wa", bits).astype(F32)
        bits *= 2
    return total


def gather_chunks(chunk):
    count = lax.axis_size("ha")
    near = jnp.stack([chunk] + [swap(chunk, "ha", 2 * q) for q in range(1, count // 2)])
    return near, swap(near, "ha", 1)


def in_order(near, far):
    every = jnp.stack([near, far], axis=1)
    return by_distance(every.reshape((2 * near.shape[0],) + near.shape[1:]))


def columns_of(gathered, first, count):
    planes, _, few, rows = gathered.shape
    picked = gathered[:, first : first + count]
    return picked.swapaxes(0, 1).reshape(count, planes * few, rows)


def line_scatter(parts):
    return lax.psum_scatter(parts, "wa", scatter_dimension=0, tiled=False).astype(F32)


def live_taps(rate, valid):
    return [(a, b) for a in (-1, 0, 1) for b in (-1, 0, 1) if b == 0 or valid > rate]


def span(b, rate, valid):
    return max(0, -b * rate), min(valid, valid - b * rate)


def moves(taps):
    return sorted({a for a, b in taps})


def forward_plain(x, shift, weights, rate, taps):
    valid = x.shape[0]
    moved = {
        a: x if a == 0 else jnp.einsum("pq,wqk->wpk", shift[(a + 1) // 2], x) for a in moves(taps)
    }
    out = jnp.zeros(x.shape[:2] + (weights.shape[1],), F32)
    for t, (a, b) in enumerate(taps):
        low, high = span(b, rate, valid)
        part = jnp.einsum(
            "wpk,ek->wpe", moved[a][low + b * rate : high + b * rate], weights[t], preferred_element_type=F32
        )
        out = out.at[low:high].add(part)
    return out


def backward_plain(x, shift, weights, rate, taps, grad, total):
    valid = x.shape[0]
    moved = {
        a: grad if a == 0 else jnp.einsum("pq,wqe->wpe", shift[(1 - a) // 2], grad)
        for a in moves(taps)
    }
    weight_grads = []
    for t, (a, b) in enumerate(taps):
        low, high = span(b, rate, valid)
        d = moved[a][low:high]
        source = slice(low + b * rate, high + b * rate)
        weight_grads.append(jnp.einsum("wpe,wpk->ek", d, x[source], preferred_element_type=F32))
        total = total.at[source].add(
            jnp.einsum("wpe,ek->wpk", d, weights[t], preferred_element_type=F32)
        )
    return jnp.stack(weight_grads), total


def dot(left, right, dims):
    return lax.dot_general(left, right, ((dims[0], dims[1]), ((), ())), preferred_element_type=F32)


NN = ((1,), (0,))
NT = ((1,), (1,))
TN = ((0,), (0,))
WHOLE = pl.BlockSpec(memory_space=pltpu.VMEM)
SCALAR = pl.BlockSpec(memory_space=pltpu.SMEM)
PARAMS = pltpu.CompilerParams(vmem_limit_bytes=32 * 1024 * 1024)


def ceil_to(n, step):
    return -(-n // step) * step


def spots_of(wanted, held):
    return ((wanted[:, None] == held[None, :]) & (wanted >= 0)[:, None]).astype(BF16)


def mixed_rows(size, micro):
    tall = ceil_to(size, 16)
    mixed = jnp.arange(ceil_to(size * micro, 128), dtype=jnp.int32)
    mixed = jnp.where(mixed < size * micro, mixed, -2)
    apart = jnp.arange(ceil_to(micro * tall, 128), dtype=jnp.int32)
    real = (apart < micro * tall) & (apart % tall < size)
    apart = jnp.where(real, apart % tall * micro + apart // tall, -1)
    return mixed, apart


def extract(features, cotangent, z):
    rows, cols, micro, channels = features.shape
    out = cotangent.shape[-1]
    size = rows * cols
    tall, full = ceil_to(size, 16), ceil_to(size * micro, 16)
    steps = channels // out
    mixed, apart = mixed_rows(size, micro)
    high = mixed.shape[0]
    spots = spots_of(apart[: micro * tall], mixed).reshape(micro, tall, high)
    flat = [jnp.pad(a.reshape(size * micro, -1), ((0, full - size * micro), (0, 0))) for a in (features, cotangent)]

    def kernel(z_ref, f_ref, c_ref, spots_ref, *refs):
        outs, held_ref = refs[:-1], refs[-1]
        held_ref[full:] = jnp.zeros((high - full, out), BF16)

        @pl.when(pl.program_id(0) < steps)
        def _():
            held_ref[:full] = f_ref[...]

        @pl.when(pl.program_id(0) == steps)
        def _():
            held_ref[:full] = c_ref[...]

        for k in range(micro):
            outs[k][...] = dot(spots_ref[z_ref[0] ^ k], held_ref[...], NN).astype(BF16)

    return pl.pallas_call(
        kernel,
        grid=(steps + 1,),
        out_shape=[jax.ShapeDtypeStruct((tall, channels + out), BF16)] * micro,
        in_specs=[
            SCALAR,
            pl.BlockSpec((full, out), lambda i: (0, jnp.minimum(i, steps - 1))),
            pl.BlockSpec((full, out), lambda i: (0, 0)),
            WHOLE,
        ],
        out_specs=[pl.BlockSpec((tall, out), lambda i: (0, i))] * micro,
        scratch_shapes=[pltpu.VMEM((high, out), BF16)],
        compiler_params=PARAMS,
        name="extract",
    )(z.reshape(1), *flat, spots)


def choose(slots, z, blocks, spots, cot_spots, ha):
    tall, wide = slots[0].shape
    out = wide // (ha + 1)
    high = spots.shape[1]

    def kernel(z_ref, *refs):
        spots_ref, cot_ref, send_ref, own_ref, held_ref = refs[len(slots) :]
        for v in range(len(slots)):

            @pl.when(z_ref[0] == v)
            def _():
                for j in range(blocks):
                    held_ref[j * tall : (j + 1) * tall] = refs[v ^ j][...]

        held_ref[blocks * tall :] = jnp.zeros((high - blocks * tall, wide), BF16)
        for d in range(ha):
            lanes = slice(d * out, (d + 1) * out)
            send_ref[d] = dot(spots_ref[...], held_ref[:, lanes], NN).astype(BF16)
        own_ref[...] = dot(cot_ref[...], held_ref[:, ha * out :], NN).astype(BF16)

    return pl.pallas_call(
        kernel,
        out_shape=[
            jax.ShapeDtypeStruct((ha, spots.shape[0], out), BF16),
            jax.ShapeDtypeStruct((cot_spots.shape[0], out), BF16),
        ],
        in_specs=[SCALAR] + [WHOLE] * (len(slots) + 2),
        out_specs=[WHOLE, WHOLE],
        scratch_shapes=[pltpu.VMEM((high, wide), BF16)],
        compiler_params=PARAMS,
        name="choose",
    )(z.reshape(1), *slots, spots, cot_spots)


def unchoose(pieces, z, blocks, spots):
    ha, fit, out = pieces.shape
    planes, tall, thick = spots.shape

    def kernel(z_ref, pieces_ref, spots_ref, *refs):
        outs, held_ref = refs[:-1], refs[-1]
        held_ref[fit:] = jnp.zeros((thick - fit, ha * out), BF16)
        for d in range(ha):
            held_ref[:fit, d * out : (d + 1) * out] = pieces_ref[d]
        for v in range(planes):

            @pl.when(z_ref[0] == v)
            def _():
                for j in range(planes):
                    if j < blocks:
                        outs[v ^ j][...] = dot(spots_ref[j], held_ref[...], NN).astype(BF16)
                    else:
                        outs[v ^ j][...] = jnp.zeros((tall, ha * out), BF16)

    return pl.pallas_call(
        kernel,
        out_shape=[jax.ShapeDtypeStruct((tall, ha * out), BF16)] * planes,
        in_specs=[SCALAR, WHOLE, WHOLE],
        out_specs=[WHOLE] * planes,
        scratch_shapes=[pltpu.VMEM((thick, ha * out), BF16)],
        compiler_params=PARAMS,
        name="unchoose",
    )(z.reshape(1), pieces, spots)


def interleave(got, z, blocks, rows, cols):
    micro = len(got)
    tall, channels = got[0].shape
    size = rows * cols
    full = ceil_to(size * micro, 16)
    lanes = min(channels, 512)
    mixed, apart = mixed_rows(size, micro)
    high = apart.shape[0]
    spots = spots_of(mixed[:full], apart)

    def kernel(z_ref, *refs):
        spots_ref, o_ref, held_ref = refs[micro:]
        for k in range(micro):
            at = pl.multiple_of((z_ref[0] ^ k) * tall, 16)
            held_ref[pl.ds(at, tall)] = jnp.where(z_ref[0] < blocks, refs[k][...], jnp.zeros((), BF16))
        held_ref[micro * tall :] = jnp.zeros((high - micro * tall, lanes), BF16)
        o_ref[...] = dot(spots_ref[...], held_ref[...], NN).astype(BF16)

    out = pl.pallas_call(
        kernel,
        grid=(channels // lanes,),
        out_shape=jax.ShapeDtypeStruct((full, channels), BF16),
        in_specs=[SCALAR] + [pl.BlockSpec((tall, lanes), lambda i: (0, i))] * micro + [WHOLE],
        out_specs=pl.BlockSpec((full, lanes), lambda i: (0, i)),
        scratch_shapes=[pltpu.VMEM((high, lanes), BF16)],
        compiler_params=PARAMS,
        name="interleave",
    )(z.reshape(1), *got, spots)
    return out[: size * micro].reshape(rows, cols, micro, channels)


def arrange(raw, place, h, valid, prows):
    ha, tall, deep = raw.shape
    high = place.shape[1]

    def kernel(h_ref, raw_ref, place_ref, x_ref, held_ref):
        held_ref[tall:] = jnp.zeros((high - tall, deep), BF16)
        for k in range(ha):
            held_ref[:tall] = raw_ref[h_ref[0] ^ k]
            block = dot(place_ref[...], held_ref[...], NN).astype(BF16)
            x_ref[:, k * prows : (k + 1) * prows, :] = block.reshape(valid, prows, deep)

    return pl.pallas_call(
        kernel,
        out_shape=jax.ShapeDtypeStruct((valid, ha * prows, deep), BF16),
        in_specs=[SCALAR, WHOLE, WHOLE],
        out_specs=WHOLE,
        scratch_shapes=[pltpu.VMEM((high, deep), BF16)],
        compiler_params=PARAMS,
        name="arrange",
    )(h.reshape(1), raw, place)


def sides_of(taps):
    return sorted({b for a, b in taps}, key=abs)


def in_steps(low, high, step, body):
    whole = (high - low) // step
    if whole:

        def one(i, carry):
            body(low + i * step, step)
            return carry

        lax.fori_loop(0, whole, one, 0)
    if (high - low) % step:
        body(low + whole * step, (high - low) % step)


def forward_kernel(x, weights, group, prows):
    valid, pheight, deep = x.shape
    wa, few = weights.shape[0], weights.shape[2]
    out = wa * few
    half = pheight // prows // 2
    operands, flops = [x, weights], 0
    for shift, first, rate, taps in group:
        operands += [] if shift is None else [shift]
        spans = [span(b, rate, valid) for a, b in taps]
        flops += 2 * pheight * deep * out * sum(high - low for low, high in spans)
    most = max(len(moves(g[3])) for g in group)
    most_sides = max(len(sides_of(g[3])) for g in group)

    def kernel(x_ref, w_ref, *refs):
        ins = list(refs[: len(operands) - 2])
        even_ref, odd_ref, moved_ref, wide_ref, sum_ref = refs[len(operands) - 2 :]
        for g, (shift, first, rate, taps) in enumerate(group):
            steps, sides = moves(taps), sides_of(taps)
            for i, b in enumerate(sides):
                for n, a in enumerate(steps):
                    t = first + taps.index((a, b))
                    for j in range(wa):
                        wide_ref[i, j * few : (j + 1) * few, n * deep : (n + 1) * deep] = w_ref[j, t]
            source_ref = x_ref
            if shift is not None:
                s_ref = ins.pop(0)
                source_ref = moved_ref

                def move(w, carry):
                    moved_ref[w, :, :deep] = dot(s_ref[0], x_ref[w], NN).astype(BF16)
                    moved_ref[w, :, deep : 2 * deep] = x_ref[w]
                    moved_ref[w, :, 2 * deep :] = dot(s_ref[1], x_ref[w], NN).astype(BF16)
                    return carry

                lax.fori_loop(0, valid, move, 0)

            for i, b in enumerate(sides):

                def columns(w, count):
                    values = source_ref[pl.ds(w + b * rate, count)].reshape(count * pheight, -1)
                    part = dot(values, wide_ref[i, :, : len(steps) * deep], NT)
                    part = part.reshape(count, pheight, out)
                    if b == 0:
                        sum_ref[pl.ds(w, count)] = part
                    else:
                        sum_ref[pl.ds(w, count)] += part

                in_steps(*span(b, rate, valid), 4, columns)

            def store(w, carry):
                at = pl.multiple_of(w * prows, prows)
                for k in range(2 * half):
                    to = odd_ref if k % 2 else even_ref
                    to[k // 2, g, pl.ds(at, prows), :] = sum_ref[w, k * prows : (k + 1) * prows].astype(BF16)
                return carry

            lax.fori_loop(0, valid, store, 0)

    shape = jax.ShapeDtypeStruct((half, len(group), valid * prows, out), BF16)
    return pl.pallas_call(
        kernel,
        out_shape=[shape] * 2,
        in_specs=[WHOLE] * len(operands),
        out_specs=[WHOLE] * 2,
        scratch_shapes=[
            pltpu.VMEM((valid, pheight, most * deep), BF16),
            pltpu.VMEM((most_sides, out, most * deep), BF16),
            pltpu.VMEM((valid, pheight, out), F32),
        ],
        compiler_params=PARAMS,
        cost_estimate=pl.CostEstimate(flops=flops, bytes_accessed=4 * x.size, transcendentals=0),
        name="forward",
    )(*operands)


def backward_kernel(x, weights, group, grads, start, h, place, prows):
    valid, pheight, deep = x.shape
    wa, few = weights.shape[0], weights.shape[2]
    out = wa * few
    ha = pheight // prows
    operands, flops = [h.reshape(1), x, start, *grads, weights], 0
    for shift, first, rate, taps in group:
        operands += [] if shift is None else [shift]
        spans = [span(b, rate, valid) for a, b in taps]
        flops += 4 * pheight * deep * out * sum(high - low for low, high in spans)
    if place is not None:
        operands += [place]
    most = max(len(moves(g[3])) for g in group)
    most_sides = max(len(sides_of(g[3])) for g in group)
    count = sum(len(g[3]) for g in group)

    def kernel(h_ref, x_ref, start_ref, near_ref, far_ref, w_ref, *refs):
        ins = list(refs[: len(operands) - 6])
        grad_ref, last_ref, moved_ref, wide_ref = refs[len(operands) - 6 :][:4]
        total_ref = last_ref if place is None else refs[-1]
        done = 0
        for g, (shift, first, rate, taps) in enumerate(group):
            steps, sides = moves(taps), sides_of(taps)
            for i, b in enumerate(sides):
                for n, a in enumerate(steps):
                    t = first + taps.index((a, b))
                    for j in range(wa):
                        at = n * out + j * few
                        wide_ref[i, at : at + few] = w_ref[j, t]
            s_ref = None if shift is None else ins.pop(0)
            middle = 0 if shift is None else out

            def move(w, carry):
                at = pl.multiple_of(w * prows, prows)
                for k in range(ha):
                    rows = slice(k * prows, (k + 1) * prows)
                    of = far_ref if k % 2 else near_ref
                    moved_ref[w, rows, middle : middle + out] = of[k // 2, g, pl.ds(at, prows), :]
                if s_ref is not None:
                    held = moved_ref[w, :, out : 2 * out]
                    moved_ref[w, :, :out] = dot(s_ref[1], held, NN).astype(BF16)
                    moved_ref[w, :, 2 * out :] = dot(s_ref[0], held, NN).astype(BF16)
                return carry

            lax.fori_loop(0, valid, move, 0)
            wide = len(steps) * out

            for i, b in enumerate(sides):
                low, high = span(b, rate, valid)
                left = moved_ref[low:high, :, :wide].reshape((high - low) * pheight, wide)
                right = x_ref[low + b * rate : high + b * rate].reshape((high - low) * pheight, deep)
                part = dot(left, right, TN).astype(BF16)
                for n, a in enumerate(steps):
                    t = done + taps.index((a, b))
                    for j in range(wa):
                        at = n * out + j * few
                        grad_ref[j, t] = part[at : at + few]
            done += len(taps)

            for i, b in enumerate(sides):

                def columns(w, count):
                    values = moved_ref[pl.ds(w - b * rate, count), :, :wide].reshape(count * pheight, wide)
                    part = dot(values, wide_ref[i, :wide], NN).reshape(count, pheight, deep)
                    if g or b != 0:
                        total_ref[pl.ds(w, count)] += part
                    elif start.ndim == 2:
                        total_ref[pl.ds(w, count)] = part + start_ref[...][None]
                    else:
                        total_ref[pl.ds(w, count)] = part + start_ref[pl.ds(w, count)]

                in_steps(*span(-b, rate, valid), 4, columns)
        if place is not None:
            for k in range(ha):
                block = total_ref[:, k * prows : (k + 1) * prows, :].astype(BF16)
                block = block.reshape(valid * prows, deep)
                piece = dot(ins[-1][...], block, TN).astype(BF16)
                last_ref[h_ref[0] ^ k] = piece[: last_ref.shape[1]]

    shapes = [jax.ShapeDtypeStruct((wa, count, few, deep), BF16)]
    scratch = [
        pltpu.VMEM((valid, pheight, most * out), BF16),
        pltpu.VMEM((most_sides, most * out, deep), BF16),
    ]
    specs = [SCALAR] + [WHOLE] * (len(operands) - 1)
    if place is None:
        shapes.append(jax.ShapeDtypeStruct(x.shape, F32))
    else:
        shapes.append(jax.ShapeDtypeStruct((ha, place.shape[1], deep), BF16))
        scratch.append(pltpu.VMEM(x.shape, F32))
    return pl.pallas_call(
        kernel,
        out_shape=shapes,
        in_specs=specs,
        out_specs=[WHOLE] * 2,
        scratch_shapes=scratch,
        compiler_params=PARAMS,
        cost_estimate=pl.CostEstimate(flops=flops, bytes_accessed=8 * x.size, transcendentals=0),
        name="backward",
    )(*operands)


def local(
    features,
    row_image,
    cotangent,
    w_one,
    dilated_weight,
    w_pool,
    w_proj,
    scales,
    shifts,
    out_scale,
    out_shift,
):
    micro, rows, cols, channels = features.shape
    ha, wa = lax.axis_size("ha"), lax.axis_size("wa")
    h, z = lax.axis_index("ha"), lax.axis_index("wa")
    planes = wa // micro
    batch, part = z // planes, z % planes
    deep = w_one.shape[0] // planes
    out = w_one.shape[1] * wa
    valid = cols * wa - PADC
    blocks = -(-valid // cols)
    prows = -(-rows // 16) * 16
    height, pheight = rows * ha, prows * ha
    images = IMG_DEV * ha
    pixels = float(height * valid)
    size = cols * rows

    fast = planes == 1 and 6 * valid * pheight * out < (16 << 20) and channels % out == 0 and deep == out

    taps = [live_taps(r, valid) for r in RATES]
    kept = [
        dilated_weight[j].swapaxes(1, 2)
        if len(taps[j]) == 9
        else jnp.stack([dilated_weight[j, 3 * (a + 1) + b + 1].T for a, b in taps[j]])
        for j in range(3)
    ]
    few = w_proj.shape[0]
    side = jnp.pad(w_proj.T, ((0, 0), (0, w_one.shape[0] - few)))
    near_weights = jnp.concatenate([w_one.T[None], kept[2], kept[1], w_pool.T[None], side[None]])
    near_weights = lax.all_gather(near_weights, "wa", axis=0, tiled=False)
    far_weights = lax.all_gather(kept[0], "wa", axis=0, tiled=False)
    side = columns_of(near_weights, near_weights.shape[1] - 1, 1)[0]
    proj = in_order(*gather_chunks(side))[..., :few].swapaxes(1, 2).reshape(ha * few, out)
    if planes > 1:
        near_weights = lax.dynamic_slice_in_dim(near_weights, part * deep, deep, 3)
        far_weights = lax.dynamic_slice_in_dim(far_weights, part * deep, deep, 3)
    wide_pool = columns_of(near_weights, near_weights.shape[1] - 2, 1)[0]

    if fast:
        slots = extract(features.transpose(1, 2, 0, 3), cotangent.transpose(1, 2, 0, 3), z)
        tall, fit = slots[0].shape[0], ceil_to(valid * rows, 16)
        slots = [slots[0]] + [swap(slots[k], "wa", k, lambda i: i < blocks) for k in range(1, wa)]
        high, thick = ceil_to(blocks * tall, 128), ceil_to(fit, 128)
        held = jnp.arange(high, dtype=jnp.int32)
        block_row = held % tall
        column = held // tall * cols + block_row % cols
        real = (block_row < size) & (column < valid)
        in_piece = jnp.where(real, column * rows + block_row // cols, -1)
        in_chunk = jnp.where(real, column * prows + block_row // cols, -1)
        spots = (jnp.arange(fit, dtype=jnp.int32)[:, None] == in_piece[None, :]).astype(BF16)
        cot_spots = (jnp.arange(valid * prows, dtype=jnp.int32)[:, None] == in_chunk[None, :]).astype(BF16)
        send, cot = choose(slots, z, blocks, spots, cot_spots, ha)
        raw = lax.all_to_all(send, "ha", 0, 0, tiled=True)
    else:
        f = features.transpose(0, 2, 1, 3).reshape(micro, size, ha, planes, deep)
        f = f.transpose(0, 3, 1, 2, 4).reshape(wa, size, ha * deep)
        c = cotangent.transpose(0, 2, 1, 3).reshape(micro, size, out)
        load = jnp.concatenate([f, jnp.repeat(c, planes, axis=0)], axis=-1)
        slots = [take(load, z)]
        for k in range(1, wa):
            slots.append(swap(take(load, z ^ k), "wa", k, lambda i: i < blocks))
        slots = jnp.stack(slots)
        block = jnp.concatenate([take(slots, z ^ j) for j in range(blocks)])[: valid * rows]
        raw = block[:, : ha * deep].reshape(valid * rows, ha, deep).swapaxes(0, 1)
        raw = lax.all_to_all(raw, "ha", 0, 0, tiled=True)
        cot = block[:, ha * deep :].reshape(valid, rows, out)
        cot = jnp.pad(cot, ((0, 0), (0, prows - rows), (0, 0))).reshape(valid * prows, out)
    cot = cot.astype(F32)

    order = h ^ jnp.arange(ha, dtype=jnp.int32)
    labels = by_distance(take(row_image, batch).reshape(ha, rows))
    number = order[:, None] * rows + jnp.arange(rows, dtype=jnp.int32)[None, :]
    pad = ((0, 0), (0, prows - rows))
    labels = jnp.pad(labels, pad, constant_values=-1).reshape(pheight)
    number = jnp.pad(number, pad, constant_values=-(1 << 20)).reshape(pheight)
    same = (labels[:, None] == labels[None, :]) & (labels >= 0)[:, None]
    apart = number[None, :] - number[:, None]
    shift = [
        jnp.stack([(same & (apart == a * r)).astype(BF16) for a in (-1, 1)]) for r in RATES
    ]
    ids = jnp.arange(images, dtype=jnp.int32)
    member = (labels[:, None] == ids[None, :]).astype(F32)
    counts = jnp.sum(member, axis=0) * valid
    own = member[:prows]
    mask = jnp.tile(jnp.sum(own, axis=1), valid)[:, None]

    groups = [
        (near_weights, [(None, 0, 0, [(0, 0)]), (shift[2], 1, RATES[2], taps[2])]),
        (near_weights, [(shift[1], 1 + len(taps[2]), RATES[1], taps[1])]),
        (far_weights, [(shift[0], 0, RATES[0], taps[0])]),
    ]
    chosen = [[0, 3], [2], [1]]
    if fast:
        spot = jnp.arange(valid * prows, dtype=jnp.int32)
        spot = jnp.where(spot % prows < rows, spot // prows * rows + spot % prows, -1)
        place = (spot[:, None] == jnp.arange(thick, dtype=jnp.int32)[None, :]).astype(BF16)
        x = arrange(raw, place, h, valid, prows)
    else:
        x = by_distance(raw).reshape(ha, valid, rows, deep)
        x = jnp.pad(x, ((0, 0), (0, 0), (0, prows - rows), (0, 0)))
        x = x.swapaxes(0, 1).reshape(valid, pheight, deep)
    branch = []
    for weights, group in groups:
        if fast:
            even, odd = forward_kernel(x, weights, group, prows)
        else:
            sums = jnp.stack(
                [forward_plain(x, s, columns_of(weights, n, len(t)), r, t) for s, n, r, t in group]
            )
            sums = sums.astype(BF16).reshape(len(group), valid, ha // 2, 2, prows, out)
            sums = sums.transpose(3, 2, 0, 1, 4, 5).reshape(2, ha // 2, len(group), valid * prows, out)
            even, odd = sums[0], sums[1]
        branch.append(reduce_chunks(even, odd, planes))
    branch = jnp.stack([branch[0][0], branch[2][0], branch[1][0], branch[0][1]])
    row_sums = jnp.sum(x.astype(F32), axis=0)
    pooled = (jnp.dot(member.T, row_sums, precision=HIGHEST) / counts[:, None]).astype(BF16)
    pool_part = dot(pooled, wide_pool, NT)

    once = (part == 0).astype(F32)
    first = plane_sum(
        jnp.concatenate(
            [once * jnp.sum(branch, axis=1), once * jnp.sum(branch * branch, axis=1), pool_part]
        ),
        planes,
    )
    mean = first[0:4] / pixels
    rstd = lax.rsqrt(first[4:8] / pixels - mean * mean + EPS)
    pool_out = first[8:]
    norm = (branch - mean[:, None]) * rstd[:, None]
    hid = norm * scales[:4, None] + shifts[:4, None]
    act = silu(hid)
    weighted = counts[:, None]
    pool_mean = jnp.sum(weighted * pool_out, axis=0) / pixels
    pool_second = jnp.sum(weighted * pool_out * pool_out, axis=0) / pixels
    pool_rstd = lax.rsqrt(pool_second - pool_mean * pool_mean + EPS)
    pool_norm = (pool_out - pool_mean) * pool_rstd
    pool_hid = pool_norm * scales[4] + shifts[4]
    spread = jnp.dot(own, silu(pool_hid), precision=HIGHEST)
    spread = jnp.broadcast_to(spread[None], (valid, prows, out)).reshape(valid * prows, out)
    joined = jnp.concatenate([act[0], act[1], act[2], act[3], spread], axis=-1).astype(BF16)
    projected = jnp.dot(joined, proj, preferred_element_type=F32)

    held = projected * mask
    second = plane_sum(
        jnp.stack([jnp.sum(held, axis=0), jnp.sum(held * held, axis=0)]) * once, planes
    )
    proj_mean = second[0] / pixels
    proj_rstd = lax.rsqrt(second[1] / pixels - proj_mean * proj_mean + EPS)
    proj_norm = (projected - proj_mean) * proj_rstd
    proj_hid = proj_norm * out_scale + out_shift
    activation = silu(proj_hid).astype(BF16)
    dproj_hid = cot * mask * silu_slope(proj_hid)
    third = plane_sum(
        jnp.stack([jnp.sum(dproj_hid, axis=0), jnp.sum(dproj_hid * proj_norm, axis=0)]) * once, planes
    )
    dproj = (
        out_scale * proj_rstd * (dproj_hid - (third[0] + proj_norm * third[1]) / pixels) * mask
    ).astype(BF16)
    djoined = lax.dot_general(dproj, proj, (((1,), (1,)), ((), ())), preferred_element_type=F32)
    grad_proj = lax.dot_general(joined, dproj, (((0,), (0,)), ((), ())), preferred_element_type=F32)
    dact = jnp.stack([djoined[:, j * out : (j + 1) * out] for j in range(4)])
    dspread = jnp.sum(djoined[:, 4 * out :].reshape(valid, prows, out), axis=0)
    image_part = jnp.dot(own.T, dspread, precision=HIGHEST)
    dhid = dact * silu_slope(hid) * mask
    fourth = plane_sum(
        jnp.concatenate([jnp.sum(dhid, axis=1), jnp.sum(dhid * norm, axis=1), image_part]) * once,
        planes,
    )
    branch_shift, branch_scale, image_total = fourth[0:4], fourth[4:8], fourth[8:]
    dbranch = (
        (scales[:4] * rstd)[:, None]
        * (dhid - (branch_shift[:, None] + norm * branch_scale[:, None]) / pixels)
        * mask
    ).astype(BF16)
    dpool_hid = silu_slope(pool_hid) * image_total
    pool_shift = jnp.sum(dpool_hid, axis=0)
    pool_scale = jnp.sum(dpool_hid * pool_norm, axis=0)
    dpool = (
        scales[4] * pool_rstd * (dpool_hid - weighted * (pool_shift + pool_norm * pool_scale) / pixels)
    ).astype(BF16)
    grad_pool = dot(dpool, pooled, TN)
    dpooled = dot(dpool, wide_pool, NN)

    total = jnp.dot(member, dpooled / counts[:, None], precision=HIGHEST)
    sent = [gather_chunks(jnp.stack([dbranch[j] for j in chosen[g]])) for g in (2, 1, 0)][::-1]
    tap_grads = [None] * 3
    if fast:
        for g in (2, 1, 0):
            weights, group = groups[g]
            ends = place if g == 0 else None
            grads, total = backward_kernel(x, weights, group, sent[g], total, h, ends, prows)
            tap_grads[g] = grads
        back = total[:, :fit]
    else:
        total = jnp.broadcast_to(total[None], (valid,) + total.shape)
        for g in (2, 1, 0):
            weights, group = groups[g]
            every = jnp.stack(sent[g], axis=1).reshape(ha, len(group), valid, prows, out)
            every = every.transpose(1, 2, 0, 3, 4).reshape(len(group), valid, pheight, out)
            found = []
            for (s, n, r, t), d in zip(group, every):
                grads, total = backward_plain(x, s, columns_of(weights, n, len(t)), r, t, d, total)
                found.append(grads.reshape(len(t), wa, out // wa, deep).swapaxes(0, 1).astype(BF16))
            tap_grads[g] = jnp.concatenate(found, axis=1)
        back = total.astype(BF16).reshape(valid, ha, prows, deep)[:, :, :rows]
        back = back.swapaxes(0, 1).reshape(ha, valid * rows, deep)
        back = by_distance(back)

    def in_place(grads):
        if planes == 1:
            return grads
        full = jnp.zeros(grads.shape[:-1] + (deep * planes,), grads.dtype)
        return lax.dynamic_update_slice_in_dim(full, grads, part * deep, grads.ndim - 1)

    grad_proj = by_distance((grad_proj * once).astype(BF16).reshape(ha, few, out))
    proj_chunk = reduce_chunks(grad_proj[0::2], grad_proj[1::2], 1)
    proj_chunk = jnp.pad(proj_chunk.T, ((0, 0), (0, w_one.shape[0] - few))).astype(BF16)
    grad_pool = in_place(grad_pool.astype(BF16)).reshape(wa, 1, out // wa, -1)
    proj_chunk = proj_chunk.reshape(wa, 1, out // wa, -1)
    first_sum = [in_place(tap_grads[0]), grad_pool, proj_chunk]
    tap_out = [line_scatter(in_place(tap_grads[2])), line_scatter(in_place(tap_grads[1])), None]
    first_sum = line_scatter(jnp.concatenate(first_sum, axis=1))
    tap_out[2] = first_sum[1:-2]
    one_out, pool_grad_out = first_sum[0].T, first_sum[-2].T
    proj_out = first_sum[-1][:, :few].T
    blank = jnp.zeros((out // wa, w_one.shape[0]), F32)
    atrous = []
    for j in range(3):
        if len(taps[j]) == 9:
            atrous.append(tap_out[j])
        else:
            found = {3 * (a + 1) + b + 1: tap_out[j][t] for t, (a, b) in enumerate(taps[j])}
            atrous.append(jnp.stack([found.get(t, blank) for t in range(9)]))
    atrous_out = jnp.stack(atrous).swapaxes(2, 3)
    sums = jnp.concatenate([branch_scale, pool_scale[None], branch_shift, pool_shift[None], third])
    sums = sums * once
    bits = 1
    while bits < wa:
        sums = sums + swap(sums, "wa", bits)
        bits *= 2

    back = lax.all_to_all(back, "ha", 0, 0, tiled=True)

    def home(i, k):
        return i ^ k < blocks

    if fast:
        number = jnp.arange(wa * tall, dtype=jnp.int32)
        block_row = number % tall
        column = number // tall * cols + block_row % cols
        real = (block_row < size) & (column < valid)
        in_piece = jnp.where(real, column * rows + block_row // cols, -1)
        in_chunk = jnp.where(real, column * prows + block_row // cols, -1)
        piece_spots = (in_piece[:, None] == jnp.arange(thick, dtype=jnp.int32)[None, :]).astype(BF16)
        chunk_spots = (in_chunk[:, None] == jnp.arange(valid * prows, dtype=jnp.int32)[None, :]).astype(BF16)
        got = unchoose(back, z, blocks, piece_spots.reshape(wa, tall, thick))
        got = [got[0]] + [swap(got[k], "wa", k, partial(home, k=k)) for k in range(1, wa)]
        df = interleave(got, z, blocks, rows, cols).transpose(2, 0, 1, 3)
        acts = jnp.dot(chunk_spots, activation, preferred_element_type=F32).astype(BF16)
        acts = acts.reshape(wa, tall, out)
        acts = [take(acts, z ^ k) for k in range(wa)]
        acts = [acts[0]] + [swap(acts[k], "wa", k, partial(home, k=k)) for k in range(1, wa)]
        acts = interleave(acts, z, blocks, rows, cols).transpose(2, 0, 1, 3)
    else:

        def send_home(array):
            array = jnp.pad(array, ((0, wa * size - valid * rows), (0, 0))).reshape(wa, size, -1)
            got = [take(array, z)]
            got += [swap(take(array, z ^ k), "wa", k, partial(home, k=k)) for k in range(1, wa)]
            got = jnp.stack(got)
            got = jnp.where(z < blocks, got, jnp.zeros((), got.dtype))
            return jnp.stack([take(got, z ^ t) for t in range(wa)])

        back = back.swapaxes(0, 1).reshape(valid * rows, ha * deep)
        df = send_home(back).reshape(micro, planes, cols, rows, ha, deep)
        df = df.transpose(0, 3, 2, 4, 1, 5).reshape(features.shape)
        activation = activation.reshape(valid, prows, out)[:, :rows].reshape(valid * rows, out)
        acts = send_home(activation).reshape(micro, planes, cols, rows, out)[:, 0].swapaxes(1, 2)
    return (
        acts,
        df,
        one_out,
        atrous_out,
        pool_grad_out,
        proj_out,
        sums[0:5],
        sums[5:10],
        sums[11],
        sums[10],
    )


def solution(mesh):
    specs = (
        P(None, "ha", "wa", None),
        P(),
        P(None, "ha", "wa", None),
        P("ha", "wa"),
        P(None, None, "ha", "wa"),
        P("ha", "wa"),
        P("ha", "wa"),
        P(),
        P(),
        P(),
        P(),
    )
    out_specs = (
        P(None, "ha", "wa", None),
        P(None, "ha", "wa", None),
        P("ha", "wa"),
        P(None, None, "ha", "wa"),
        P("ha", "wa"),
        P("ha", "wa"),
        P(),
        P(),
        P(),
        P(),
    )
    return jax.shard_map(local, mesh=mesh, in_specs=specs, out_specs=out_specs, check_vma=False)
```

time: 3910 us -> 499 us (0.13)
  waiting for transfers between devices: 2010 us -> 224 us
  local copies, waits for them, and re-layouts: 996 us -> 63.2 us
  matrix products: 406 us -> 4.57 us
  blocking collectives: 190 us -> 0 us
  other arithmetic: 189 us -> 30.4 us
  Pallas kernels: 0 us -> 62.1 us
    unnamed x23 -> x5, waiting for transfers between devices: 1150 us -> 0.08 us
    unnamed x623 -> x190, local copies, waits for them, and re-layouts: 903 us -> 37.1 us
    all_gather x12 -> x2, waiting for transfers between devices: 539 us -> 0.02 us  [the longest x1 0.02 us: local(): far_weights = lax.all_gather(kept[0], 'wa', axis=0, tiled=False)]
    dot_general x88 -> x11, matrix products: 406 us -> 4.57 us  [the longest x1 1.8 us: local(): lax.dot_general(joined, dproj, (((0,), (0,)), ((), ())), preferred_elemen...]
    psum x2 -> x0, waiting for transfers between devices: 314 us -> none  [the longest x1 185 us: local(): lax.psum((partial_pool, first_part, second_part), ('ha', 'wa'))]
    ppermute x16 -> x71, waiting for transfers between devices: 9.84 us -> 207 us  [swap(): return lax.ppermute(array, axis, pairs)]
    psum x3 -> x0, blocking collectives: 123 us -> none  [the longest x1 43.1 us: local(): lax.psum((partial_pool, first_part, second_part), ('ha', 'wa'))]
    unnamed x121 -> x0, other arithmetic: 86.4 us -> none
  transfers between devices with their start and end apart: 36 -> 78, of which waited for: 13 -> 33; matrix products, arithmetic and copies ran while one was open for 15% -> 13% of each run, Pallas kernels for 0% -> 10%
where the time goes in v1:
time: 499 us; the launch traced here: 494 us
  waiting for transfers between devices  224 us (45%)
  starting transfers between devices  94 us (19%)
  local copies, waits for them, and re-layouts  63.2 us (13%)
  Pallas kernels  62.1 us (12%)
  other arithmetic  30.4 us (6%)
  between operations  15.6 us (3%)
    ppermute x71, waiting for transfers between devices, swap(): return lax.ppermute(array, axis, pairs)  207 us
    ppermute x71, starting transfers between devices, swap(): return lax.ppermute(array, axis, pairs)  85.9 us
    unnamed x190, local copies, waits for them, and re-layouts  37.1 us
    pallas_call x3, Pallas kernels, backward_kernel(): pl.pallas_call(kernel, out_shape=shapes, in_specs=specs, out_specs=[WHOLE...  27.9 us
    pallas_call x3, Pallas kernels, forward_kernel(): pl.pallas_call(kernel, out_shape=[shape] * 2, in_specs=[WHOLE] * len(oper...  19.3 us
    all_to_all x1, waiting for transfers between devices, local(): raw = lax.all_to_all(send, 'ha', 0, 0, tiled=True)  16.6 us
  transfers between devices with their start and end apart: 78, of which 33 were waited for; matrix products, arithmetic and copies ran while one was open for 13% of the time, Pallas kernels for 10%

profile of v1, /device:TPU:8, one launch (start us, length us, event | category | flops | bytes accessed | tf_op | source)
XLA Modules:
  0.0 494.0 jit_solution(7648642688107200600)
XLA Ops:
  9.6 3.6 reshape.1446
  13.8 5.7 %extract.1 = (bf16[144,2304]{1,0:T(8,128)(2,1)S(1)}, bf16[144,2304]{1,0:T(8,128)(2,1)}, bf16[144,2304]{1,0:T(8,128)(2,1)}, bf16[144,2304]{1,0:T(8,128)(2,1)S(1)}) custom-call(s32[1]{0:T(128)} %bitcast.z_ref, bf16[528,2048]{1,0:T(8,128)(2,1)S(1)} %pad.24.f_ref, bf16[528,256]{1,0:T(8,128)(2,1)S(1)} %pad.25.c_ref, ...), custom_call_target="tpu_custom_call" | custom-call | tf_op jit(solution)/shard_map/extract/pallas_call | solution.py:192
  21.4 3.9 collective-permute-start.1
  25.3 3.4 collective-permute-start.2
  37.5 29.1 %collective-permute-done.refs_1_ = bf16[144,2304]{1,0:T(8,128)(2,1)S(1)} collective-permute-done((bf16[144,2304]{1,0:T(8,128)(2,1)}, bf16[144,2304]{1,0:T(8,128)(2,1)S(1)}, u32[]{:S(2)}, u32[]{:S(2)}) %collective-permute-start) | collective-permute-done | bytes 663584 | tf_op jit(solution)/shard_map/ppermute | solution.py:31
  66.6 58.3 %collective-permute-done.2.refs_3_ = bf16[144,2304]{1,0:T(8,128)(2,1)S(1)} collective-permute-done((bf16[144,2304]{1,0:T(8,128)(2,1)S(1)}, bf16[144,2304]{1,0:T(8,128)(2,1)S(1)}, u32[]{:S(2)}, u32[]{:S(2)}) %collective-permute-start.2) | collective-permute-done | bytes 663584 | tf_op jit(solution)/shard_map/ppermute | solution.py:31
  127.8 4.0 all-to-all-start
  134.7 16.6 %all-to-all-done.raw_ref = bf16[8,352,256]{2,1,0:T(8,128)(2,1)S(1)} async-done(((bf16[8,352,256]{2,1,0:T(8,128)(2,1)}), bf16[8,352,256]{2,1,0:T(8,128)(2,1)S(1)}, u32[]{:S(2)}, u32[]{:S(2)}) %all-to-all-start) | async-done | bytes 1441824 | tf_op jit(solution)/shard_map/all_to_all | solution.py:583
  154.7 6.9 %forward.4 = (bf16[4,1,416,256]{3,2,1,0:T(8,128)(2,1)S(1)}, bf16[4,1,416,256]{3,2,1,0:T(8,128)(2,1)S(1)}) custom-call(bf16[13,256,256]{2,1,0:T(8,128)(2,1)S(1)} %arrange.1.x_ref, bf16[4,9,64,256]{3,2,1,0:T(8,128)(2,1)S(1)} %bitcast.224, bf16[2,256,256]{2,1,0:T(8,128)(2,1)S(1)} %copy-done.8), custom_call_target="tpu_custom_call" | custom-call | flops 2717908992 | bytes 3407872 | tf_op jit(solution)/shard_map/forward/pallas_call | solution.py:402
  173.9 6.8 %forward.3 = (bf16[4,2,416,256]{3,2,1,0:T(8,128)(2,1)S(1)}, bf16[4,2,416,256]{3,2,1,0:T(8,128)(2,1)S(1)}) custom-call(bf16[13,256,256]{2,1,0:T(8,128)(2,1)S(1)} %arrange.1.x_ref, bf16[4,15,64,256]{3,2,1,0:T(8,128)(2,1)S(1)} %bitcast.220, bf16[2,256,256]{2,1,0:T(8,128)(2,1)S(1)} %get-tuple-element.154.refs_0_), custom_call_target="tpu_custom_call" | custom-call | flops 1744830464 | bytes 3407872 | tf_op jit(solution)/shard_map/forward/pallas_call | solution.py:402
  184.5 5.7 %forward.5 = (bf16[4,1,416,256]{3,2,1,0:T(8,128)(2,1)S(1)}, bf16[4,1,416,256]{3,2,1,0:T(8,128)(2,1)S(1)}) custom-call(bf16[13,256,256]{2,1,0:T(8,128)(2,1)S(1)} %arrange.1.x_ref, bf16[4,15,64,256]{3,2,1,0:T(8,128)(2,1)S(1)} %bitcast.221, bf16[2,256,256]{2,1,0:T(8,128)(2,1)S(1)} %get-tuple-element.155.refs_0_), custom_call_target="tpu_custom_call" | custom-call | flops 1509949440 | bytes 3407872 | tf_op jit(solution)/shard_map/forward/pallas_call | solution.py:402
  203.7 3.5 collective-permute-done.13
  207.3 9.0 %collective-permute-done.6 = bf16[2,416,256]{2,1,0:T(8,128)(2,1)S(1)} collective-permute-done((bf16[2,416,256]{2,1,0:T(8,128)(2,1)S(1)}, bf16[2,416,256]{2,1,0:T(8,128)(2,1)S(1)}, u32[]{:S(2)}, u32[]{:S(2)}) %collective-permute-start.6) | collective-permute-done | bytes 426016 | tf_op jit(solution)/shard_map/ppermute | solution.py:31
  216.3 8.1 %collective-permute-done.5 = bf16[2,416,256]{2,1,0:T(8,128)(2,1)S(1)} collective-permute-done((bf16[2,416,256]{2,1,0:T(8,128)(2,1)S(1)}, bf16[2,416,256]{2,1,0:T(8,128)(2,1)S(1)}, u32[]{:S(2)}, u32[]{:S(2)}) %collective-permute-start.5) | collective-permute-done | bytes 426016 | tf_op jit(solution)/shard_map/ppermute | solution.py:31
  278.1 5.6 %collective-permute-done.52 = bf16[1,416,256]{2,1,0:T(8,128)(2,1)S(1)} collective-permute-done((bf16[1,416,256]{2,1,0:T(8,128)(2,1)S(1)}, bf16[1,416,256]{2,1,0:T(8,128)(2,1)S(1)}, u32[]{:S(2)}, u32[]{:S(2)}) %collective-permute-start.52) | collective-permute-done | bytes 213024 | tf_op jit(solution)/shard_map/ppermute | solution.py:31
  283.7 3.1 collective-permute-done.51
  290.8 5.4 %collective-permute-done.56 = bf16[1,416,256]{2,1,0:T(8,128)(2,1)S(1)} collective-permute-done((bf16[1,416,256]{2,1,0:T(8,128)(2,1)S(1)}, bf16[1,416,256]{2,1,0:T(8,128)(2,1)S(1)}, u32[]{:S(2)}, u32[]{:S(2)}) %collective-permute-start.56) | collective-permute-done | bytes 213024 | tf_op jit(solution)/shard_map/ppermute | solution.py:31
  296.2 4.1 collective-permute-done.55
  301.1 9.5 %backward.3 = (bf16[4,9,64,256]{3,2,1,0:T(8,128)(2,1)}, f32[13,256,256]{2,1,0:T(8,128)S(1)}) custom-call(s32[1]{0:T(128)} %bitcast.1.h_ref, bf16[13,256,256]{2,1,0:T(8,128)(2,1)S(1)} %arrange.1.x_ref, f32[256,256]{1,0:T(8,128)S(1)} %fusion.37.start_ref, bf16[4,1,416,256]{3,2,1,0:T(8,128)(2,1)S(1)} %pad_maximum_fusion.3.near_ref, ...), custom_call_target="tpu_custom_call" | custom-call | flops 5435817984 | bytes 6815744 | tf_op jit(solution)/shard_map/backward/pallas_call | solution.py:508
  310.6 7.4 %backward.4 = (bf16[4,9,64,256]{3,2,1,0:T(8,128)(2,1)}, f32[13,256,256]{2,1,0:T(8,128)S(1)}) custom-call(s32[1]{0:T(128)} %bitcast.1.h_ref, bf16[13,256,256]{2,1,0:T(8,128)(2,1)S(1)} %arrange.1.x_ref, f32[13,256,256]{2,1,0:T(8,128)S(1)} %get-tuple-element.44.start_ref, bf16[4,1,416,256]{3,2,1,0:T(8,128)(2,1)S(1)} %pad_maximum_fusion.4.near_ref, ...), custom_call_target="tpu_custom_call" | custom-call | flops 3019898880 | bytes 6815744 | tf_op jit(solution)/shard_map/backward/pallas_call | solution.py:508
  330.7 7.3 %collective-permute-done.60 = bf16[2,416,256]{2,1,0:T(8,128)(2,1)S(1)} collective-permute-done((bf16[2,416,256]{2,1,0:T(8,128)(2,1)S(1)}, bf16[2,416,256]{2,1,0:T(8,128)(2,1)S(1)}, u32[]{:S(2)}, u32[]{:S(2)}) %collective-permute-start.60) | collective-permute-done | bytes 426016 | tf_op jit(solution)/shard_map/ppermute | solution.py:31
  338.1 8.6 %collective-permute-done.59 = bf16[2,416,256]{2,1,0:T(8,128)(2,1)S(1)} collective-permute-done((bf16[2,416,256]{2,1,0:T(8,128)(2,1)S(1)}, bf16[2,416,256]{2,1,0:T(8,128)(2,1)S(1)}, u32[]{:S(2)}, u32[]{:S(2)}) %collective-permute-start.59) | collective-permute-done | bytes 426016 | tf_op jit(solution)/shard_map/ppermute | solution.py:31
  367.8 3.5 collective-permute-done.68
  378.2 11.0 %backward.5 = (bf16[4,4,64,256]{3,2,1,0:T(8,128)(2,1)S(1)}, bf16[8,384,256]{2,1,0:T(8,128)(2,1)S(1)}) custom-call(s32[1]{0:T(128)} %bitcast.1.h_ref, bf16[13,256,256]{2,1,0:T(8,128)(2,1)S(1)} %arrange.1.x_ref, f32[13,256,256]{2,1,0:T(8,128)S(1)} %copy-done.18, bf16[4,2,416,256]{3,2,1,0:T(8,128)(2,1)S(1)} %pad_maximum_fusion.1.near_ref, ...), custom_call_target="tpu_custom_call" | custom-call | flops 3489660928 | bytes 6815744 | tf_op jit(solution)/shard_map/backward/pallas_call | solution.py:508
  393.3 3.7 all-to-all-start.1
  398.1 3.6 collective-permute-done.69
  403.6 3.9 collective-permute-start.33
  408.8 4.1 collective-permute-start.35
  414.0 3.1 collective-permute-done.34.refs_2_
  427.6 5.6 %collective-permute-start.64 = (bf16[144,2048]{1,0:T(8,128)(2,1)}, bf16[144,2048]{1,0:T(8,128)(2,1)S(1)}, u32[]{:S(2)}, u32[]{:S(2)}) collective-permute-start(bf16[144,2048]{1,0:T(8,128)(2,1)} %get-tuple-element.50), channel_id=1, source_target_pairs={{1,2},{2,1},{3,0},{5,6},{6,5},{7,4},{9,10},{10,9},{11,8},{13,14},{... | collective-permute-start | bytes 1769480 | tf_op jit(solution)/shard_map/ppermute | solution.py:31
  447.4 6.6 %collective-permute-done.63.refs_2_ = bf16[144,2048]{1,0:T(8,128)(2,1)S(1)} collective-permute-done((bf16[144,2048]{1,0:T(8,128)(2,1)}, bf16[144,2048]{1,0:T(8,128)(2,1)S(1)}, u32[]{:S(2)}, u32[]{:S(2)}) %collective-permute-start.63) | collective-permute-done | bytes 589856 | tf_op jit(solution)/shard_map/ppermute | solution.py:31
  454.1 27.9 %collective-permute-done.64.refs_3_ = bf16[144,2048]{1,0:T(8,128)(2,1)S(1)} collective-permute-done((bf16[144,2048]{1,0:T(8,128)(2,1)}, bf16[144,2048]{1,0:T(8,128)(2,1)S(1)}, u32[]{:S(2)}, u32[]{:S(2)}) %collective-permute-start.64) | collective-permute-done | bytes 589856 | tf_op jit(solution)/shard_map/ppermute | solution.py:31
  (457 shorter events, 189.8 us)
Async XLA Ops:
  7.2 145.2 %all-gather.7.cloned.1.call-start = ((), (), s32[]{:S(2)}) async-start(), calls=%async_computation.9 | async-start | bytes 1474560 | tf_op jit(solution)/shard_map/all_gather | solution.py:561
  8.9 158.8 %all-gather.5.cloned.1.call-start = ((), (), s32[]{:S(2)}) async-start(), calls=%async_computation.8 | async-start | bytes 2457600 | tf_op jit(solution)/shard_map/all_gather | solution.py:560
  19.5 47.1 %collective-permute-start = (bf16[144,2304]{1,0:T(8,128)(2,1)}, bf16[144,2304]{1,0:T(8,128)(2,1)S(1)}, u32[]{:S(2)}, u32[]{:S(2)}) collective-permute-start(bf16[144,2304]{1,0:T(8,128)(2,1)} %get-tuple-element.33), channel_id=1, source_target_pairs={{0,1},{1,0},{2,3},{4,5},{5,4},{6,7},{8,9},{9,8},{10,11},{12,13},{1... | collective-permute-start | bytes 1990664 | tf_op jit(solution)/shard_map/ppermute | solution.py:31
  21.4 45.2 %collective-permute-start.1 = (bf16[144,2304]{1,0:T(8,128)(2,1)}, bf16[144,2304]{1,0:T(8,128)(2,1)S(1)}, u32[]{:S(2)}, u32[]{:S(2)}) collective-permute-start(bf16[144,2304]{1,0:T(8,128)(2,1)} %get-tuple-element.34), channel_id=1, source_target_pairs={{0,2},{1,3},{2,0},{4,6},{5,7},{6,4},{8,10},{9,11},{10,8},{12,14},{... | collective-permute-start | bytes 1990664 | tf_op jit(solution)/shard_map/ppermute | solution.py:31
  25.3 99.6 %collective-permute-start.2 = (bf16[144,2304]{1,0:T(8,128)(2,1)S(1)}, bf16[144,2304]{1,0:T(8,128)(2,1)S(1)}, u32[]{:S(2)}, u32[]{:S(2)}) collective-permute-start(bf16[144,2304]{1,0:T(8,128)(2,1)S(1)} %get-tuple-element.35), channel_id=1, source_target_pairs={{0,3},{1,2},{2,1},{4,7},{5,6},{6,5},{8,11},{9,10},{10,9},{12,15},{... | collective-permute-start | bytes 1990664 | tf_op jit(solution)/shard_map/ppermute | solution.py:31
  127.8 23.6 %all-to-all-start = ((bf16[8,352,256]{2,1,0:T(8,128)(2,1)}), bf16[8,352,256]{2,1,0:T(8,128)(2,1)S(1)}, u32[]{:S(2)}, u32[]{:S(2)}) async-start(bf16[8,352,256]{2,1,0:T(8,128)(2,1)} %get-tuple-element.36), calls=%async_computation | async-start | bytes 2883584 | tf_op jit(solution)/shard_map/all_to_all | solution.py:583
  131.7 301.5 %reduce-scatter.8.cloned.1.call-start = ((), (), s32[]{:S(2)}) async-start(), calls=%async_computation.7 | async-start | bytes 1474560 | tf_op jit(solution)/shard_map/reduce_scatter | solution.py:88
  165.8 24.5 %collective-permute-start.10 = (bf16[1,416,256]{2,1,0:T(8,128)(2,1)}, bf16[1,416,256]{2,1,0:T(8,128)(2,1)S(1)}, u32[]{:S(2)}, u32[]{:S(2)}) collective-permute-start(bf16[1,416,256]{2,1,0:T(8,128)(2,1)} %get-tuple-element.80), channel_id=1, source_target_pairs={{0,24},{4,28},{8,16},{12,20},{16,8},{20,12},{24,0},{28,4},{1,25},{... | collective-permute-start | bytes 638984 | tf_op jit(solution)/shard_map/ppermute | solution.py:31
  166.4 23.9 %collective-permute-start.9 = (bf16[1,416,256]{2,1,0:T(8,128)(2,1)}, bf16[1,416,256]{2,1,0:T(8,128)(2,1)S(1)}, u32[]{:S(2)}, u32[]{:S(2)}) collective-permute-start(bf16[1,416,256]{2,1,0:T(8,128)(2,1)} %get-tuple-element.81), channel_id=1, source_target_pairs={{0,16},{4,20},{8,24},{12,28},{16,0},{20,4},{24,8},{28,12},{1,17},{... | collective-permute-start | bytes 638984 | tf_op jit(solution)/shard_map/ppermute | solution.py:31
  168.8 11.9 %collective-permute-start.24 = (bf16[256,256]{1,0:T(8,128)(2,1)S(1)}, bf16[256,256]{1,0:T(8,128)(2,1)S(1)}, u32[]{:S(2)}, u32[]{:S(2)}) collective-permute-start(bf16[256,256]{1,0:T(8,128)(2,1)S(1)} %bitcast.244), channel_id=1, source_target_pairs={{0,24},{4,28},{8,16},{12,20},{16,8},{20,12},{24,0},{28,4},{1,25},{... | collective-permute-start | bytes 393224 | tf_op jit(solution)/shard_map/ppermute | solution.py:31
  170.3 13.5 %collective-permute-start.23 = (bf16[256,256]{1,0:T(8,128)(2,1)S(1)}, bf16[256,256]{1,0:T(8,128)(2,1)S(1)}, u32[]{:S(2)}, u32[]{:S(2)}) collective-permute-start(bf16[256,256]{1,0:T(8,128)(2,1)S(1)} %bitcast.245), channel_id=1, source_target_pairs={{0,16},{4,20},{8,24},{12,28},{16,0},{20,4},{24,8},{28,12},{1,17},{... | collective-permute-start | bytes 393224 | tf_op jit(solution)/shard_map/ppermute | solution.py:31
  171.8 12.0 %collective-permute-start.22 = (bf16[256,256]{1,0:T(8,128)(2,1)S(1)}, bf16[256,256]{1,0:T(8,128)(2,1)S(1)}, u32[]{:S(2)}, u32[]{:S(2)}) collective-permute-start(bf16[256,256]{1,0:T(8,128)(2,1)S(1)} %bitcast.246), channel_id=1, source_target_pairs={{0,8},{4,12},{8,0},{12,4},{16,24},{20,28},{24,16},{28,20},{1,9},{5... | collective-permute-start | bytes 393224 | tf_op jit(solution)/shard_map/ppermute | solution.py:31
  183.8 13.1 %collective-permute-start.3 = (bf16[4,2,416,256]{3,2,1,0:T(8,128)(2,1)S(1)}, bf16[4,2,416,256]{3,2,1,0:T(8,128)(2,1)S(1)}, u32[]{:S(2)}, u32[]{:S(2)}) collective-permute-start(bf16[4,2,416,256]{3,2,1,0:T(8,128)(2,1)S(1)} %get-tuple-element.38), channel_id=1, source_target_pairs={{0,4},{4,0},{8,12},{12,8},{16,20},{20,16},{24,28},{28,24},{1,5},{5... | collective-permute-start | bytes 5111816 | tf_op jit(solution)/shard_map/ppermute | solution.py:31
  194.6 12.5 %collective-permute-start.13 = (bf16[1,416,256]{2,1,0:T(8,128)(2,1)S(1)}, bf16[1,416,256]{2,1,0:T(8,128)(2,1)S(1)}, u32[]{:S(2)}, u32[]{:S(2)}) collective-permute-start(bf16[1,416,256]{2,1,0:T(8,128)(2,1)S(1)} %get-tuple-element.84), channel_id=1, source_target_pairs={{0,16},{4,20},{8,24},{12,28},{16,0},{20,4},{24,8},{28,12},{1,17},{... | collective-permute-start | bytes 638984 | tf_op jit(solution)/shard_map/ppermute | solution.py:31
  196.0 11.1 %collective-permute-start.12 = (bf16[1,416,256]{2,1,0:T(8,128)(2,1)S(1)}, bf16[1,416,256]{2,1,0:T(8,128)(2,1)S(1)}, u32[]{:S(2)}, u32[]{:S(2)}) collective-permute-start(bf16[1,416,256]{2,1,0:T(8,128)(2,1)S(1)} %get-tuple-element.82), channel_id=1, source_target_pairs={{0,8},{4,12},{8,0},{12,4},{16,24},{20,28},{24,16},{28,20},{1,9},{5... | collective-permute-start | bytes 638984 | tf_op jit(solution)/shard_map/ppermute | solution.py:31
  197.3 19.0 %collective-permute-start.6 = (bf16[2,416,256]{2,1,0:T(8,128)(2,1)S(1)}, bf16[2,416,256]{2,1,0:T(8,128)(2,1)S(1)}, u32[]{:S(2)}, u32[]{:S(2)}) collective-permute-start(bf16[2,416,256]{2,1,0:T(8,128)(2,1)S(1)} %get-tuple-element.70), channel_id=1, source_target_pairs={{0,24},{4,28},{8,16},{12,20},{16,8},{20,12},{24,0},{28,4},{1,25},{... | collective-permute-start | bytes 1277960 | tf_op jit(solution)/shard_map/ppermute | solution.py:31
  198.5 25.8 %collective-permute-start.5 = (bf16[2,416,256]{2,1,0:T(8,128)(2,1)S(1)}, bf16[2,416,256]{2,1,0:T(8,128)(2,1)S(1)}, u32[]{:S(2)}, u32[]{:S(2)}) collective-permute-start(bf16[2,416,256]{2,1,0:T(8,128)(2,1)S(1)} %get-tuple-element.71), channel_id=1, source_target_pairs={{0,16},{4,20},{8,24},{12,28},{16,0},{20,4},{24,8},{28,12},{1,17},{... | collective-permute-start | bytes 1277960 | tf_op jit(solution)/shard_map/ppermute | solution.py:31
  202.5 21.8 %collective-permute-start.4 = (bf16[2,416,256]{2,1,0:T(8,128)(2,1)S(1)}, bf16[2,416,256]{2,1,0:T(8,128)(2,1)S(1)}, u32[]{:S(2)}, u32[]{:S(2)}) collective-permute-start(bf16[2,416,256]{2,1,0:T(8,128)(2,1)S(1)} %get-tuple-element.69), channel_id=1, source_target_pairs={{0,8},{4,12},{8,0},{12,4},{16,24},{20,28},{24,16},{28,20},{1,9},{5... | collective-permute-start | bytes 1277960 | tf_op jit(solution)/shard_map/ppermute | solution.py:31
  287.0 14.1 %collective-permute-start.53 = (bf16[4,1,416,256]{3,2,1,0:T(8,128)(2,1)S(1)}, bf16[4,1,416,256]{3,2,1,0:T(8,128)(2,1)S(1)}, u32[]{:S(2)}, u32[]{:S(2)}) collective-permute-start(bf16[4,1,416,256]{3,2,1,0:T(8,128)(2,1)S(1)} %pad_maximum_fusion.3.near_ref), channel_id=1, source_target_pairs={{0,4},{4,0},{8,12},{12,8},{16,20},{20,16},{24,28},{28,24},{1,5},{5... | collective-permute-start | bytes 2555912 | tf_op jit(solution)/shard_map/ppermute | solution.py:31
  288.7 11.6 %collective-permute-start.55 = (bf16[1,416,256]{2,1,0:T(8,128)(2,1)S(1)}, bf16[1,416,256]{2,1,0:T(8,128)(2,1)S(1)}, u32[]{:S(2)}, u32[]{:S(2)}) collective-permute-start(bf16[1,416,256]{2,1,0:T(8,128)(2,1)S(1)} %get-tuple-element.94), channel_id=1, source_target_pairs={{0,16},{4,20},{8,24},{12,28},{16,0},{20,4},{24,8},{28,12},{1,17},{... | collective-permute-start | bytes 638984 | tf_op jit(solution)/shard_map/ppermute | solution.py:31
  319.9 115.2 %reduce-scatter.6.cloned.1.call-start = ((), (), s32[]{:S(2)}) async-start(), calls=%async_computation.6 | async-start | bytes 1474560 | tf_op jit(solution)/shard_map/reduce_scatter | solution.py:88
  324.5 13.6 %collective-permute-start.60 = (bf16[2,416,256]{2,1,0:T(8,128)(2,1)S(1)}, bf16[2,416,256]{2,1,0:T(8,128)(2,1)S(1)}, u32[]{:S(2)}, u32[]{:S(2)}) collective-permute-start(bf16[2,416,256]{2,1,0:T(8,128)(2,1)S(1)} %get-tuple-element.109), channel_id=1, source_target_pairs={{0,24},{4,28},{8,16},{12,20},{16,8},{20,12},{24,0},{28,4},{1,25},{... | collective-permute-start | bytes 1277960 | tf_op jit(solution)/shard_map/ppermute | solution.py:31
  326.0 20.7 %collective-permute-start.59 = (bf16[2,416,256]{2,1,0:T(8,128)(2,1)S(1)}, bf16[2,416,256]{2,1,0:T(8,128)(2,1)S(1)}, u32[]{:S(2)}, u32[]{:S(2)}) collective-permute-start(bf16[2,416,256]{2,1,0:T(8,128)(2,1)S(1)} %get-tuple-element.109), channel_id=1, source_target_pairs={{0,16},{4,20},{8,24},{12,28},{16,0},{20,4},{24,8},{28,12},{1,17},{... | collective-permute-start | bytes 1277960 | tf_op jit(solution)/shard_map/ppermute | solution.py:31
  327.4 19.4 %collective-permute-start.58 = (bf16[2,416,256]{2,1,0:T(8,128)(2,1)S(1)}, bf16[2,416,256]{2,1,0:T(8,128)(2,1)}, u32[]{:S(2)}, u32[]{:S(2)}) collective-permute-start(bf16[2,416,256]{2,1,0:T(8,128)(2,1)S(1)} %get-tuple-element.109), channel_id=1, source_target_pairs={{0,8},{4,12},{8,0},{12,4},{16,24},{20,28},{24,16},{28,20},{1,9},{5... | collective-permute-start | bytes 1277960 | tf_op jit(solution)/shard_map/ppermute | solution.py:31
  330.7 106.2 %reduce-scatter.4.cloned.1.call-start = ((), (), s32[]{:S(2)}) async-start(), calls=%async_computation.5 | async-start | bytes 983040 | tf_op jit(solution)/shard_map/reduce_scatter | solution.py:88
  349.1 25.5 %collective-permute-start.61 = (bf16[4,2,416,256]{3,2,1,0:T(8,128)(2,1)S(1)}, bf16[4,2,416,256]{3,2,1,0:T(8,128)(2,1)}, u32[]{:S(2)}, u32[]{:S(2)}) collective-permute-start(bf16[4,2,416,256]{3,2,1,0:T(8,128)(2,1)S(1)} %pad_maximum_fusion.1.near_ref), channel_id=1, source_target_pairs={{0,4},{4,0},{8,12},{12,8},{16,20},{20,16},{24,28},{28,24},{1,5},{5... | collective-permute-start | bytes 5111816 | tf_op jit(solution)/shard_map/ppermute | solution.py:31
  393.3 28.0 %all-to-all-start.1 = ((bf16[8,352,256]{2,1,0:T(8,128)(2,1)}), bf16[8,352,256]{2,1,0:T(8,128)(2,1)S(1)}, u32[]{:S(2)}, u32[]{:S(2)}) async-start(bf16[8,352,256]{2,1,0:T(8,128)(2,1)} %slice.357), calls=%async_computation.1 | async-start | bytes 2883584 | tf_op jit(solution)/shard_map/all_to_all | solution.py:772
  401.6 11.2 %collective-permute-start.70 = (f32[12,256]{1,0:T(8,128)S(1)}, f32[12,256]{1,0:T(8,128)S(1)}, u32[]{:S(2)}, u32[]{:S(2)}) collective-permute-start(f32[12,256]{1,0:T(8,128)S(1)} %add.786), channel_id=1, source_target_pairs={{0,2},{1,3},{2,0},{3,1},{4,6},{5,7},{6,4},{7,5},{8,10},{9,11},{10,... | collective-permute-start | bytes 36872 | tf_op jit(solution)/shard_map/ppermute | solution.py:31
  408.8 11.3 %collective-permute-start.35 = (bf16[144,256]{1,0:T(8,128)(2,1)S(1)}, bf16[144,256]{1,0:T(8,128)(2,1)S(1)}, u32[]{:S(2)}, u32[]{:S(2)}) collective-permute-start(bf16[144,256]{1,0:T(8,128)(2,1)S(1)} %get-tuple-element.113), channel_id=1, source_target_pairs={{1,2},{2,1},{3,0},{5,6},{6,5},{7,4},{9,10},{10,9},{11,8},{13,14},{... | collective-permute-start | bytes 221192 | tf_op jit(solution)/shard_map/ppermute | solution.py:31
  424.0 23.4 %collective-permute-start.62 = (bf16[144,2048]{1,0:T(8,128)(2,1)}, bf16[144,2048]{1,0:T(8,128)(2,1)S(1)}, u32[]{:S(2)}, u32[]{:S(2)}) collective-permute-start(bf16[144,2048]{1,0:T(8,128)(2,1)} %get-tuple-element.48), channel_id=1, source_target_pairs={{0,1},{1,0},{3,2},{4,5},{5,4},{7,6},{8,9},{9,8},{11,10},{12,13},{1... | collective-permute-start | bytes 1769480 | tf_op jit(solution)/shard_map/ppermute | solution.py:31
  426.3 27.7 %collective-permute-start.63 = (bf16[144,2048]{1,0:T(8,128)(2,1)}, bf16[144,2048]{1,0:T(8,128)(2,1)S(1)}, u32[]{:S(2)}, u32[]{:S(2)}) collective-permute-start(bf16[144,2048]{1,0:T(8,128)(2,1)} %get-tuple-element.49), channel_id=1, source_target_pairs={{0,2},{2,0},{3,1},{4,6},{6,4},{7,5},{8,10},{10,8},{11,9},{12,14},{... | collective-permute-start | bytes 1769480 | tf_op jit(solution)/shard_map/ppermute | solution.py:31
  427.6 54.4 %collective-permute-start.64 = (bf16[144,2048]{1,0:T(8,128)(2,1)}, bf16[144,2048]{1,0:T(8,128)(2,1)S(1)}, u32[]{:S(2)}, u32[]{:S(2)}) collective-permute-start(bf16[144,2048]{1,0:T(8,128)(2,1)} %get-tuple-element.50), channel_id=1, source_target_pairs={{1,2},{2,1},{3,0},{5,6},{6,5},{7,4},{9,10},{10,9},{11,8},{13,14},{... | collective-permute-start | bytes 1769480 | tf_op jit(solution)/shard_map/ppermute | solution.py:31
  (122 other events, 988.1 us)
Sparse Core Ops, SparseCore 0:
  9.6 53.2 all-gather.6
  64.5 61.8 all-gather.4
  320.0 27.4 reduce-scatter.7
  350.2 27.8 reduce-scatter.5
  391.5 26.8 reduce-scatter.3

commit v2 on v1

v2 whole, which is shorter than its diff:
```python
from functools import partial

import jax
import jax.numpy as jnp
import numpy as np
from jax import lax
from jax.experimental import pallas as pl
from jax.experimental.pallas import tpu as pltpu
from jax.sharding import PartitionSpec as P

PADC = 7
IMG_DEV = 2
RATES = (6, 12, 18)
EPS = 1e-05
HIGHEST = lax.Precision.HIGHEST
F32 = jnp.float32
BF16 = jnp.bfloat16


def silu(u):
    return u * jax.nn.sigmoid(u)


def silu_slope(u):
    s = jax.nn.sigmoid(u)
    return s * (1.0 + u * (1.0 - s))


def swap(array, axis, bits, sources=None):
    count = lax.axis_size(axis)
    pairs = [(i, i ^ bits) for i in range(count) if sources is None or sources(i)]
    return lax.ppermute(array, axis, pairs)


def after(value, *others):
    return lax.optimization_barrier((value, *others))[0]


def tree_sum(parts):
    while len(parts) > 1:
        parts = [parts[i] + parts[i + 1] for i in range(0, len(parts), 2)]
    return parts[0]


def plane_parts(array):
    return [array] + [swap(array, "ha", k) for k in range(1, lax.axis_size("ha"))]


def plane_sum(array, groups):
    total = tree_sum(plane_parts(array))
    bits = 1
    while bits < groups:
        total = total + swap(total, "wa", bits)
        bits *= 2
    return total


def take(array, index):
    return lax.dynamic_index_in_dim(array, index, 0, keepdims=False)


def by_distance(array):
    h = lax.axis_index("ha")
    return jnp.stack([take(array, h ^ k) for k in range(array.shape[0])])


def spread_chunks(even, odd):
    other = swap(odd, "ha", 1)
    both = [even[q].astype(F32) + other[q].astype(F32) for q in range(even.shape[0])]
    return both[:1] + [swap(both[q].astype(BF16), "ha", 2 * q) for q in range(1, len(both))]


def sum_chunks(parts, groups):
    total = tree_sum([part.astype(F32) for part in parts])
    bits = 1
    while bits < groups:
        total = total + swap(total.astype(BF16), "wa", bits).astype(F32)
        bits *= 2
    return total


def reduce_square(even, odd):
    other = swap(odd, "ha", 1)
    half = even.shape[1] // 2
    low = even[:, :half].astype(F32) + other[:, :half].astype(F32)
    high = even[:, half:].astype(F32) + other[:, half:].astype(F32)
    low_got = swap(low[1::2].astype(BF16), "ha", 2)
    high_got = swap(high[2:].astype(BF16), "ha", 4)
    low_last = swap((low[2] + low_got[1].astype(F32)).astype(BF16), "ha", 4)
    high_last = swap((high[1] + high_got[1].astype(F32)).astype(BF16), "ha", 2)
    return low[0], low_got, low_last, high[0], high_got, high_last


def gather_square(chunk):
    half = chunk.shape[0] // 2
    low, high = chunk[:half], chunk[half:]
    low_one = swap(low, "ha", 2)
    high_one = swap(high, "ha", 4)
    low_two = swap(jnp.stack([low, low_one]), "ha", 4)
    high_two = swap(jnp.stack([high, high_one]), "ha", 2)
    near = [chunk, low_one, high_one, low_two, high_two]
    return near + [swap(piece, "ha", 1) for piece in near]


def piece_of(k, branch, branches):
    q, half = k // 2, branches // 2
    first = 5 * (k % 2)
    low = branch < half
    inner = branch if low else branch - half
    if q == 0:
        return first, (branch,)
    if q == (1 if low else 2):
        return first + (1 if low else 2), (inner,)
    return first + (3 if low else 4), (int(q == 3), inner)


def gather_near(chunk):
    return [chunk] + [swap(chunk, "ha", 2 * q) for q in range(1, lax.axis_size("ha") // 2)]


def gather_chunks(chunk):
    near = jnp.stack(gather_near(chunk))
    return near, swap(near, "ha", 1)


def in_order(near, far):
    every = jnp.stack([near, far], axis=1)
    return by_distance(every.reshape((2 * near.shape[0],) + near.shape[1:]))


def gather_columns(own):
    gathered = lax.all_gather(own, "wa", axis=0, tiled=False)
    planes, count, few, rows = gathered.shape
    return gathered.swapaxes(0, 1).reshape(count, planes * few, rows)


def neighbour(array, pairs):
    return lax.ppermute(array, "wa", pairs)


def gather_early(own, others):
    right = neighbour(own, [(0, 1), (1, 2), (2, 3)])
    left = neighbour(own, [(1, 0), (2, 1), (3, 2)])
    right_two = neighbour(after(right, others), [(2, 3)])
    left_two = neighbour(after(left, others), [(1, 0), (2, 1)])
    return right, left, right_two, left_two


def gather_late(own, early, *others):
    z = lax.axis_index("wa")
    right, left, right_two, left_two = early
    left_three = neighbour(left_two, [(1, 0)])
    last_two = neighbour(after(right, *others), [(1, 2)])
    last_three = neighbour(last_two, [(2, 3)])
    found = [
        lax.select_n(z, own, right, last_two, last_three),
        lax.select_n(z, left, own, right, right_two),
        lax.select_n(z, left_two, left, own, right),
        lax.select_n(z, left_three, left_two, left, own),
    ]
    return jnp.concatenate(found, axis=1)


def exchange_sum(parts):
    z = lax.axis_index("wa")
    got = [swap(take(parts, z ^ k), "wa", k) for k in range(1, lax.axis_size("wa"))]
    return tree_sum([take(parts, z)] + got)


def line_scatter(parts):
    return lax.psum_scatter(parts, "wa", scatter_dimension=0, tiled=False).astype(F32)


def live_taps(rate, valid):
    return [(a, b) for a in (-1, 0, 1) for b in (-1, 0, 1) if b == 0 or valid > rate]


def span(b, rate, valid):
    return max(0, -b * rate), min(valid, valid - b * rate)


def moves(taps):
    return sorted({a for a, b in taps})


def forward_plain(x, shift, weights, rate, taps):
    valid = x.shape[0]
    moved = {
        a: x if a == 0 else jnp.einsum("pq,wqk->wpk", shift[(a + 1) // 2], x) for a in moves(taps)
    }
    out = jnp.zeros(x.shape[:2] + (weights.shape[1],), F32)
    for t, (a, b) in enumerate(taps):
        low, high = span(b, rate, valid)
        part = jnp.einsum(
            "wpk,ek->wpe", moved[a][low + b * rate : high + b * rate], weights[t], preferred_element_type=F32
        )
        out = out.at[low:high].add(part)
    return out


def backward_plain(x, shift, weights, rate, taps, grad, total):
    valid = x.shape[0]
    moved = {
        a: grad if a == 0 else jnp.einsum("pq,wqe->wpe", shift[(1 - a) // 2], grad)
        for a in moves(taps)
    }
    weight_grads = []
    for t, (a, b) in enumerate(taps):
        low, high = span(b, rate, valid)
        d = moved[a][low:high]
        source = slice(low + b * rate, high + b * rate)
        weight_grads.append(jnp.einsum("wpe,wpk->ek", d, x[source], preferred_element_type=F32))
        total = total.at[source].add(
            jnp.einsum("wpe,ek->wpk", d, weights[t], preferred_element_type=F32)
        )
    return jnp.stack(weight_grads), total


def dot(left, right, dims):
    return lax.dot_general(left, right, ((dims[0], dims[1]), ((), ())), preferred_element_type=F32)


NN = ((1,), (0,))
NT = ((1,), (1,))
TN = ((0,), (0,))
WHOLE = pl.BlockSpec(memory_space=pltpu.VMEM)
SCALAR = pl.BlockSpec(memory_space=pltpu.SMEM)
NO_COST = pl.CostEstimate(flops=0, bytes_accessed=0, transcendentals=0)
WIDE = pltpu.CompilerParams(vmem_limit_bytes=60 * 1024 * 1024)
PARAMS = pltpu.CompilerParams(vmem_limit_bytes=32 * 1024 * 1024)


def ceil_to(n, step):
    return -(-n // step) * step


def pack_weights(w_one, dilated, w_pool, w_proj, taps):
    rows, deep = w_one.shape
    order = [(j, 3 * (a + 1) + b + 1) for j in range(3) for a, b in taps[j]]

    def kernel(one_ref, dilated_ref, pool_ref, proj_ref, out_ref):
        out_ref[0] = one_ref[...]
        for at, (j, t) in enumerate(order):
            out_ref[at + 1] = dilated_ref[j, t]
        out_ref[len(order) + 1] = pool_ref[...]
        out_ref[len(order) + 2] = proj_ref[...]

    return pl.pallas_call(
        kernel,
        out_shape=jax.ShapeDtypeStruct((len(order) + 3, rows, deep), BF16),
        in_specs=[WHOLE] * 4,
        out_specs=WHOLE,
        compiler_params=PARAMS,
        name="pack_weights",
    )(w_one, dilated, w_pool, w_proj)


def spots_of(wanted, held):
    return ((wanted[:, None] == held[None, :]) & (wanted >= 0)[:, None]).astype(BF16)


def mixed_rows(size, micro):
    tall = ceil_to(size, 16)
    mixed = np.arange(ceil_to(size * micro, 128))
    mixed = np.where(mixed < size * micro, mixed, -2)
    apart = np.arange(ceil_to(micro * tall, 128))
    real = (apart < micro * tall) & (apart % tall < size)
    return mixed, np.where(real, apart % tall * micro + apart // tall, -1)


def block_rows(count, tall, rows, cols, valid, pitch):
    row = np.arange(count)
    column = row // tall * cols + row % tall % cols
    real = (row % tall < rows * cols) & (column < valid)
    return np.where(real, column * pitch + row % tall // cols, -1)


def padded_rows(count, valid, prows, rows):
    row = np.arange(count)
    real = (row < valid * prows) & (row % prows < rows)
    return np.where(real, row // prows * rows + row % prows, -1)


def extract(features, cotangent, z):
    rows, cols, micro, channels = features.shape
    out = cotangent.shape[-1]
    size = rows * cols
    tall, full = ceil_to(size, 16), ceil_to(size * micro, 16)
    steps = channels // out
    mixed, apart = mixed_rows(size, micro)
    high = mixed.shape[0]
    spots = spots_of(apart[: micro * tall], mixed).reshape(micro, tall, high)
    flat = [jnp.pad(a.reshape(size * micro, -1), ((0, full - size * micro), (0, 0))) for a in (features, cotangent)]

    def kernel(z_ref, f_ref, c_ref, spots_ref, *refs):
        outs, held_ref = refs[:-1], refs[-1]
        held_ref[full:] = jnp.zeros((high - full, out), BF16)

        @pl.when(pl.program_id(0) < steps)
        def _():
            held_ref[:full] = f_ref[...]

        @pl.when(pl.program_id(0) == steps)
        def _():
            held_ref[:full] = c_ref[...]

        for k in range(micro):
            outs[k][...] = dot(spots_ref[z_ref[0] ^ k], held_ref[...], NN).astype(BF16)

    return pl.pallas_call(
        kernel,
        grid=(steps + 1,),
        out_shape=[jax.ShapeDtypeStruct((tall, channels + out), BF16)] * micro,
        in_specs=[
            SCALAR,
            pl.BlockSpec((full, out), lambda i: (0, jnp.minimum(i, steps - 1))),
            pl.BlockSpec((full, out), lambda i: (0, 0)),
            WHOLE,
        ],
        out_specs=[pl.BlockSpec((tall, out), lambda i: (0, i))] * micro,
        scratch_shapes=[pltpu.VMEM((high, out), BF16)],
        compiler_params=PARAMS,
        name="extract",
    )(z.reshape(1), *flat, spots)


def choose(slots, z, blocks, spots, last_spots, lanes):
    tall, wide = slots[0].shape
    high = spots.shape[1]
    count = wide // lanes - 1

    def kernel(z_ref, *refs):
        spots_ref, last_ref, send_ref, own_ref, held_ref = refs[len(slots) :]
        for v in range(len(slots)):

            @pl.when(z_ref[0] == v)
            def _():
                for j in range(blocks):
                    held_ref[j * tall : (j + 1) * tall] = refs[v ^ j][...]

        held_ref[blocks * tall :] = jnp.zeros((high - blocks * tall, wide), BF16)
        for d in range(count):
            part = held_ref[:, d * lanes : (d + 1) * lanes]
            send_ref[d] = dot(spots_ref[...], part, NN).astype(BF16)
        own_ref[...] = dot(last_ref[...], held_ref[:, count * lanes :], NN).astype(BF16)

    return pl.pallas_call(
        kernel,
        out_shape=[
            jax.ShapeDtypeStruct((count, spots.shape[0], lanes), BF16),
            jax.ShapeDtypeStruct((last_spots.shape[0], lanes), BF16),
        ],
        in_specs=[SCALAR] + [WHOLE] * (len(slots) + 2),
        out_specs=[WHOLE] * 2,
        scratch_shapes=[pltpu.VMEM((high, wide), BF16)],
        compiler_params=PARAMS,
        name="choose",
    )(z.reshape(1), *slots, spots, last_spots)


def unchoose(pieces, last, z, blocks, spots, last_spots):
    ha, fit, out = pieces.shape
    planes, tall, thick = spots.shape
    wide = (ha + 1) * out

    def kernel(z_ref, pieces_ref, last_ref, spots_ref, last_spots_ref, *refs):
        outs, held_ref = refs[:-1], refs[-1]
        held_ref[fit:] = jnp.zeros((thick - fit, ha * out), BF16)
        for d in range(ha):
            held_ref[:fit, d * out : (d + 1) * out] = pieces_ref[d]
        for v in range(planes):

            @pl.when(z_ref[0] == v)
            def _():
                for j in range(planes):
                    if j < blocks:
                        outs[v ^ j][:, : ha * out] = dot(spots_ref[j], held_ref[...], NN).astype(BF16)
                        outs[v ^ j][:, ha * out :] = dot(last_spots_ref[j], last_ref[...], NN).astype(BF16)
                    else:
                        outs[v ^ j][...] = jnp.zeros((tall, wide), BF16)

    return pl.pallas_call(
        kernel,
        out_shape=[jax.ShapeDtypeStruct((tall, wide), BF16)] * planes,
        in_specs=[SCALAR] + [WHOLE] * 4,
        out_specs=[WHOLE] * planes,
        scratch_shapes=[pltpu.VMEM((thick, ha * out), BF16)],
        compiler_params=PARAMS,
        name="unchoose",
    )(z.reshape(1), pieces, last, spots, last_spots)


def order_chunks(near, far, h, few):
    half, out, _ = near.shape

    def kernel(h_ref, near_ref, far_ref, out_ref):
        for k in range(2 * half):
            chunk = (far_ref if k % 2 else near_ref)[k // 2]
            at = pl.multiple_of((h_ref[0] ^ k) * few, 16)
            out_ref[pl.ds(at, few), :] = chunk.T[:few]

    return pl.pallas_call(
        kernel,
        out_shape=jax.ShapeDtypeStruct((2 * half * few, out), BF16),
        in_specs=[SCALAR, WHOLE, WHOLE],
        out_specs=WHOLE,
        compiler_params=PARAMS,
        cost_estimate=NO_COST,
        name="order_chunks",
    )(h.reshape(1), near, far)


def interleave(got, z, blocks, rows, cols, out, others):
    micro = len(got)
    tall, channels = got[0].shape
    channels -= out
    size = rows * cols
    full = ceil_to(size * micro, 16)
    lanes = 2 * out
    mixed, apart = mixed_rows(size, micro)
    high = apart.shape[0]
    spots = spots_of(mixed[:full], apart)

    def kernel(z_ref, *refs):
        spots_ref, df_ref, act_ref, held_ref = refs[2 * micro], refs[-3], refs[-2], refs[-1]
        held_ref[micro * tall :] = jnp.zeros((high - micro * tall, lanes), BF16)

        def place(parts, wide):
            for k in range(micro):
                at = pl.multiple_of((z_ref[0] ^ k) * tall, 16)
                part = jnp.where(z_ref[0] < blocks, parts[k][...], jnp.zeros((), BF16))
                held_ref[pl.ds(at, tall), :wide] = part
            return dot(spots_ref[...], held_ref[:, :wide], NN).astype(BF16)

        @pl.when(pl.program_id(0) == 0)
        def _():
            act_ref[...] = place(refs[micro : 2 * micro], out)

        df_ref[...] = place(refs[:micro], lanes)

    df, act = pl.pallas_call(
        kernel,
        grid=(channels // lanes,),
        out_shape=[jax.ShapeDtypeStruct((full, channels), BF16), jax.ShapeDtypeStruct((full, out), BF16)],
        in_specs=[SCALAR]
        + [pl.BlockSpec((tall, lanes), lambda i: (0, i))] * micro
        + [pl.BlockSpec((tall, out), lambda i: (0, channels // out))] * micro
        + [WHOLE]
        + [pl.BlockSpec(memory_space=pl.ANY)] * len(others),
        out_specs=[pl.BlockSpec((full, lanes), lambda i: (0, i)), pl.BlockSpec((full, out), lambda i: (0, 0))],
        scratch_shapes=[pltpu.VMEM((high, lanes), BF16)],
        compiler_params=PARAMS,
        name="interleave",
    )(z.reshape(1), *got, *got, spots, *others)
    return [a[: size * micro].reshape(rows, cols, micro, -1).transpose(2, 0, 1, 3) for a in (df, act)]


def arrange(raw, place, h, valid, prows):
    ha, tall, deep = raw.shape
    high = place.shape[1]

    def kernel(h_ref, raw_ref, place_ref, x_ref, sum_ref, held_ref):
        held_ref[tall:] = jnp.zeros((high - tall, deep), BF16)
        for k in range(ha):
            held_ref[:tall] = raw_ref[h_ref[0] ^ k]
            block = dot(place_ref[...], held_ref[...], NN).reshape(valid, prows, deep)
            x_ref[:, k * prows : (k + 1) * prows, :] = block.astype(BF16)
            sum_ref[k * prows : (k + 1) * prows] = jnp.sum(block, axis=0)

    return pl.pallas_call(
        kernel,
        out_shape=[
            jax.ShapeDtypeStruct((valid, ha * prows, deep), BF16),
            jax.ShapeDtypeStruct((ha * prows, deep), F32),
        ],
        in_specs=[SCALAR, WHOLE, WHOLE],
        out_specs=[WHOLE, WHOLE],
        scratch_shapes=[pltpu.VMEM((high, deep), BF16)],
        compiler_params=PARAMS,
        name="arrange",
    )(h.reshape(1), raw, place)


def sides_of(taps):
    return sorted({b for a, b in taps}, key=abs)


def in_steps(low, high, step, body):
    whole = (high - low) // step
    if whole:

        def one(i, carry):
            body(low + i * step, step)
            return carry

        lax.fori_loop(0, whole, one, 0)
    if (high - low) % step:
        body(low + whole * step, (high - low) % step)


def forward_kernel(x, weights, group, prows):
    valid, pheight, deep = x.shape
    out = weights.shape[1]
    half = pheight // prows // 2
    operands, flops = [x, weights], 0
    for shift, first, rate, taps in group:
        operands += [] if shift is None else [shift]
        spans = [span(b, rate, valid) for a, b in taps]
        flops += 2 * pheight * deep * out * sum(high - low for low, high in spans)
    most = max(len(moves(g[3])) for g in group)
    most_sides = max(len(sides_of(g[3])) for g in group)

    def kernel(x_ref, w_ref, *refs):
        ins = list(refs[: len(operands) - 2])
        even_ref, odd_ref, moved_ref, wide_ref, sum_ref = refs[len(operands) - 2 :]
        for g, (shift, first, rate, taps) in enumerate(group):
            steps, sides = moves(taps), sides_of(taps)
            for i, b in enumerate(sides):
                for n, a in enumerate(steps):
                    wide_ref[i, :, n * deep : (n + 1) * deep] = w_ref[first + taps.index((a, b))]
            source_ref = x_ref
            if shift is not None:
                s_ref = ins.pop(0)
                source_ref = moved_ref

                def move(w, carry):
                    values = x_ref[w]
                    both = dot(s_ref[...].reshape(2 * pheight, pheight), values, NN).astype(BF16)
                    moved_ref[w, :, :deep] = both[:pheight]
                    moved_ref[w, :, deep : 2 * deep] = values
                    moved_ref[w, :, 2 * deep :] = both[pheight:]
                    return carry

                lax.fori_loop(0, valid, move, 0, unroll=True)

            for i, b in enumerate(sides):

                def columns(w, count):
                    values = source_ref[pl.ds(w + b * rate, count)].reshape(count * pheight, -1)
                    part = dot(values, wide_ref[i, :, : len(steps) * deep], NT)
                    part = part.reshape(count, pheight, out)
                    if b == 0:
                        sum_ref[pl.ds(w, count)] = part
                    else:
                        sum_ref[pl.ds(w, count)] += part

                in_steps(*span(b, rate, valid), 7, columns)

            def store(w, carry):
                at = pl.multiple_of(w * prows, prows)
                for k in range(2 * half):
                    to = odd_ref if k % 2 else even_ref
                    to[k // 2, g, pl.ds(at, prows), :] = sum_ref[w, k * prows : (k + 1) * prows].astype(BF16)
                return carry

            lax.fori_loop(0, valid, store, 0, unroll=True)

    shape = jax.ShapeDtypeStruct((half, len(group), valid * prows, out), BF16)
    return pl.pallas_call(
        kernel,
        out_shape=[shape] * 2,
        in_specs=[WHOLE] * len(operands),
        out_specs=[WHOLE] * 2,
        scratch_shapes=[
            pltpu.VMEM((valid, pheight, most * deep), BF16),
            pltpu.VMEM((most_sides, out, most * deep), BF16),
            pltpu.VMEM((valid, pheight, out), F32),
        ],
        compiler_params=PARAMS,
        cost_estimate=NO_COST,
        name="forward",
    )(*operands)


def loaded(operands):
    return [
        pl.BlockSpec(a.shape, lambda i, n=a.ndim: (0,) * n, pipeline_mode=pl.Buffered(1)) for a in operands
    ]


def build_moved(pieces, moved_ref, s_ref, g, branches, valid, ha, prows, out):
    middle = 0 if s_ref is None else out

    def move(w, carry):
        at = pl.multiple_of(w * prows, prows)
        for k in range(ha):
            piece, index = piece_of(k, g, branches)
            rows = slice(k * prows, (k + 1) * prows)
            moved_ref[w, rows, middle : middle + out] = pieces[piece][(*index, pl.ds(at, prows))]
        if s_ref is not None:
            held = moved_ref[w, :, out : 2 * out]
            both = dot(s_ref[...].reshape(2 * ha * prows, ha * prows), held, NN).astype(BF16)
            moved_ref[w, :, :out] = both[ha * prows :]
            moved_ref[w, :, 2 * out :] = both[: ha * prows]
        return carry

    lax.fori_loop(0, valid, move, 0, unroll=True)


def weights_backward(x, group, pieces, wa, prows):
    valid, pheight, deep = x.shape
    out = pieces[0].shape[-1]
    few, ha, branches = out // wa, pheight // prows, len(group)
    shifts = [g[0] for g in group if g[0] is not None]
    operands = [x, *shifts, *pieces]
    shape = wa, sum(len(g[3]) for g in group), few, deep
    most = max(len(moves(g[3])) for g in group)

    def kernel(x_ref, *refs):
        shift_refs = list(refs[: len(shifts)])
        piece_refs = refs[len(shifts) : len(operands) - 1]
        grad_ref, moved_ref = refs[len(operands) - 1 :]
        done = 0
        for g, (shift, first, rate, taps) in enumerate(group):
            steps = moves(taps)
            s_ref = None if shift is None else shift_refs.pop(0)
            build_moved(piece_refs, moved_ref, s_ref, g, branches, valid, ha, prows, out)
            wide = len(steps) * out
            for b in sides_of(taps):
                low, high = span(b, rate, valid)
                left = moved_ref[low:high, :, :wide].reshape((high - low) * pheight, wide)
                right = x_ref[low + b * rate : high + b * rate].reshape((high - low) * pheight, deep)
                part = dot(left, right, TN).astype(BF16)
                for n, a in enumerate(steps):
                    t = done + taps.index((a, b))
                    for j in range(wa):
                        at = n * out + j * few
                        grad_ref[j, t] = part[at : at + few]
            done += len(taps)

    return pl.pallas_call(
        kernel,
        out_shape=jax.ShapeDtypeStruct(shape, BF16),
        grid=(1,),
        in_specs=loaded(operands),
        out_specs=pl.BlockSpec(shape, lambda i: (0, 0, 0, 0)),
        scratch_shapes=[pltpu.VMEM((valid, pheight, most * out), BF16)],
        compiler_params=WIDE,
        cost_estimate=NO_COST,
        name="weights_backward",
    )(*operands)


def features_backward(x, weights, group, pieces, start, h, place, fit, prows):
    valid, pheight, deep = x.shape
    out = weights.shape[1]
    ha, branches = pheight // prows, len(group)
    shifts = [g[0] for g in group if g[0] is not None]
    operands = [h.reshape(1), start, weights, place, *shifts, *pieces]
    high = place.shape[1]
    most = max(len(moves(g[3])) for g in group)
    most_sides = max(len(sides_of(g[3])) for g in group)

    def kernel(h_ref, start_ref, w_ref, place_ref, *refs):
        shift_refs = list(refs[: len(shifts)])
        piece_refs = refs[len(shifts) : len(operands) - 4]
        last_ref, moved_ref, wide_ref, total_ref, held_ref = refs[len(operands) - 4 :]
        for g, (shift, first, rate, taps) in enumerate(group):
            steps, sides = moves(taps), sides_of(taps)
            s_ref = None if shift is None else shift_refs.pop(0)
            build_moved(piece_refs, moved_ref, s_ref, g, branches, valid, ha, prows, out)
            for i, b in enumerate(sides):
                for n, a in enumerate(steps):
                    wide_ref[i, n * out : (n + 1) * out] = w_ref[first + taps.index((a, b))]
            wide = len(steps) * out
            for i, b in enumerate(sides):

                def columns(w, count):
                    values = moved_ref[pl.ds(w - b * rate, count), :, :wide].reshape(count * pheight, wide)
                    part = dot(values, wide_ref[i, :wide], NN).reshape(count, pheight, deep)
                    if g or b != 0:
                        total_ref[pl.ds(w, count)] += part
                    else:
                        total_ref[pl.ds(w, count)] = part + start_ref[...][None]

                in_steps(*span(-b, rate, valid), 4, columns)
        held_ref[valid * prows :] = jnp.zeros((high - valid * prows, deep), BF16)
        for k in range(ha):
            block = total_ref[:, k * prows : (k + 1) * prows, :].astype(BF16)
            held_ref[: valid * prows] = block.reshape(valid * prows, deep)
            last_ref[h_ref[0] ^ k] = dot(place_ref[...], held_ref[...], NN).astype(BF16)

    return pl.pallas_call(
        kernel,
        out_shape=jax.ShapeDtypeStruct((ha, fit, deep), BF16),
        grid=(1,),
        in_specs=[SCALAR] + loaded(operands[1:]),
        out_specs=pl.BlockSpec((ha, fit, deep), lambda i: (0, 0, 0)),
        scratch_shapes=[
            pltpu.VMEM((valid, pheight, most * out), BF16),
            pltpu.VMEM((most_sides, most * out, deep), BF16),
            pltpu.VMEM(x.shape, F32),
            pltpu.VMEM((high, deep), BF16),
        ],
        compiler_params=WIDE,
        cost_estimate=NO_COST,
        name="features_backward",
    )(*operands)


def real_rows(pixels, prows, rows):
    return (lax.broadcasted_iota(jnp.int32, (pixels, 1), 0) % prows < rows).astype(F32)


def total_of(refs):
    return tree_sum([r[...] for r in refs])


def column_sum(values):
    return jnp.sum(values, axis=0, keepdims=True)


def small_kernel(kernel, name, operands, shapes):
    return pl.pallas_call(
        kernel,
        out_shape=[jax.ShapeDtypeStruct(s, t) for s, t in shapes],
        in_specs=[WHOLE] * len(operands),
        out_specs=[WHOLE] * len(shapes),
        compiler_params=PARAMS,
        cost_estimate=NO_COST,
        name=name,
    )(*operands)


def branch_sums(parts, pool_part):
    _, pixels, out = parts[0].shape
    images = pool_part.shape[0]

    def kernel(low, low_got, low_last, high, high_got, high_last, pool_ref, branch_ref, sum_ref):
        for j in range(4):
            own, got, last = (low, low_got, low_last) if j < 2 else (high, high_got, high_last)
            value = own[j % 2] + got[0, j % 2].astype(F32) + last[j % 2].astype(F32)
            branch_ref[j] = value
            sum_ref[j : j + 1] = column_sum(value)
            sum_ref[4 + j : 5 + j] = column_sum(value * value)
        sum_ref[8:] = pool_ref[...]

    shapes = [((4, pixels, out), F32), ((8 + images, out), F32)]
    return small_kernel(kernel, "branch_sums", [*parts, pool_part], shapes)


def project(sums, branch, scales, shifts, counts, own, proj, rows, pixel_total):
    _, pixels, out = branch.shape
    images = counts.shape[0]
    prows = own.shape[0]
    many = len(sums)

    def kernel(*refs):
        branch_ref, scale_ref, shift_ref, count_ref, own_ref, proj_ref = refs[many : many + 6]
        joined_ref, projected_ref, second_ref, stat_ref, pool_ref = refs[many + 6 :]
        total = total_of(refs[:many])
        mean = total[0:4] / pixel_total
        rstd = lax.rsqrt(total[4:8] / pixel_total - mean * mean + EPS)
        stat_ref[0:4] = mean
        stat_ref[4:8] = rstd
        scale, shift = scale_ref[...], shift_ref[...]
        for j in range(4):
            norm = (branch_ref[j] - mean[j : j + 1]) * rstd[j : j + 1]
            hid = norm * scale[j : j + 1] + shift[j : j + 1]
            joined_ref[:, j * out : (j + 1) * out] = silu(hid).astype(BF16)
        pool_out = total[8:]
        weighted = count_ref[...]
        pool_mean = column_sum(weighted * pool_out) / pixel_total
        pool_second = column_sum(weighted * pool_out * pool_out) / pixel_total
        pool_rstd = lax.rsqrt(pool_second - pool_mean * pool_mean + EPS)
        pool_norm = (pool_out - pool_mean) * pool_rstd
        pool_hid = pool_norm * scale[4:5] + shift[4:5]
        pool_ref[0] = pool_norm
        pool_ref[1] = pool_hid
        pool_ref[2] = jnp.broadcast_to(pool_rstd, pool_out.shape)
        pool_act = silu(pool_hid)
        spread = jnp.zeros((prows, out), F32)
        for i in range(images):
            spread = spread + own_ref[:, i : i + 1] * pool_act[i : i + 1]
        spread = spread.astype(BF16)
        for w in range(pixels // prows):
            joined_ref[w * prows : (w + 1) * prows, 4 * out :] = spread
        projected = dot(joined_ref[...], proj_ref[...], NN)
        projected_ref[...] = projected
        held = projected * real_rows(pixels, prows, rows)
        second_ref[...] = jnp.zeros(second_ref.shape, F32)
        second_ref[0:1] = column_sum(held)
        second_ref[1:2] = column_sum(held * held)

    shapes = [((pixels, 5 * out), BF16), ((pixels, out), F32), ((8, out), F32), ((8, out), F32), ((3, images, out), F32)]
    return small_kernel(kernel, "project", [*sums, branch, scales, shifts, counts, own, proj], shapes)


def activate(sums, projected, cot, out_scale, out_shift, prows, rows, pixel_total):
    pixels, out = projected.shape
    many = len(sums)

    def kernel(*refs):
        projected_ref, cot_ref, scale_ref, shift_ref = refs[many : many + 4]
        act_ref, norm_ref, dhid_ref, third_ref, rstd_ref = refs[many + 4 :]
        total = total_of(refs[:many])
        mean = total[0:1] / pixel_total
        rstd = lax.rsqrt(total[1:2] / pixel_total - mean * mean + EPS)
        rstd_ref[...] = jnp.broadcast_to(rstd, rstd_ref.shape)
        norm = (projected_ref[...] - mean) * rstd
        norm_ref[...] = norm
        hid = norm * scale_ref[...] + shift_ref[...]
        act_ref[...] = silu(hid).astype(BF16)
        dhid = cot_ref[...].astype(F32) * real_rows(pixels, prows, rows) * silu_slope(hid)
        dhid_ref[...] = dhid
        third_ref[...] = jnp.zeros(third_ref.shape, F32)
        third_ref[0:1] = column_sum(dhid)
        third_ref[1:2] = column_sum(dhid * norm)

    shapes = [((pixels, out), BF16), ((pixels, out), F32), ((pixels, out), F32), ((8, out), F32), ((8, out), F32)]
    operands = [*sums, projected, cot, out_scale[None], out_shift[None]]
    return small_kernel(kernel, "activate", operands, shapes)


def unproject(sums, norm, dhid, rstd, out_scale, proj, joined, branch, stats, scales, shifts, own, ha, rows, pixel_total):
    _, pixels, out = branch.shape
    prows, images = own.shape
    many = len(sums)

    def kernel(*refs):
        norm_ref, dhid_ref, rstd_ref, oscale_ref, proj_ref, joined_ref = refs[many : many + 6]
        branch_ref, stat_ref, scale_ref, shift_ref, own_ref = refs[many + 6 : many + 11]
        third_ref, grad_ref, back_ref, fourth_ref = refs[many + 11 :]
        total = total_of(refs[:many])
        third_ref[...] = total
        mask = real_rows(pixels, prows, rows)
        dproj = dhid_ref[...] - (total[0:1] + norm_ref[...] * total[1:2]) / pixel_total
        dproj = (oscale_ref[...] * rstd_ref[0:1] * dproj * mask).astype(BF16)
        grad = dot(joined_ref[...], dproj, TN)
        grad_ref[...] = jnp.zeros(grad_ref.shape, BF16)
        few = 5 * out // ha
        for d in range(ha):
            grad_ref[d, :, :few] = grad[d * few : (d + 1) * few].T.astype(BF16)
        for j in range(5):
            dact = dot(dproj, proj_ref[j * out : (j + 1) * out], NT)
            if j < 4:
                branch_norm = (branch_ref[j] - stat_ref[j : j + 1]) * stat_ref[4 + j : 5 + j]
                hid = branch_norm * scale_ref[j : j + 1] + shift_ref[j : j + 1]
                back = dact * silu_slope(hid) * mask
                back_ref[j] = back
                fourth_ref[j : j + 1] = column_sum(back)
                fourth_ref[4 + j : 5 + j] = column_sum(back * branch_norm)
            else:
                across = jnp.sum(dact.reshape(pixels // prows, prows, out), axis=0)
                for i in range(images):
                    fourth_ref[8 + i : 9 + i] = column_sum(own_ref[:, i : i + 1] * across)

    shapes = [((8, out), F32), ((ha, out, out), BF16), ((4, pixels, out), F32), ((8 + images, out), F32)]
    operands = [*sums, norm, dhid, rstd, out_scale[None], proj, joined, branch, stats, scales, shifts, own]
    return small_kernel(kernel, "unproject", operands, shapes)


def branch_gradients(sums, back, branch, stats, scales, counts, pool, prows, rows, pixel_total):
    _, pixels, out = branch.shape
    images = counts.shape[0]
    many = len(sums)

    def kernel(*refs):
        back_ref, branch_ref, stat_ref, scale_ref, count_ref, pool_ref = refs[many : many + 6]
        grad_ref, dpool_ref, sum_ref = refs[many + 6 :]
        total = total_of(refs[:many])
        mask = real_rows(pixels, prows, rows)
        for j in range(4):
            rstd = stat_ref[4 + j : 5 + j]
            norm = (branch_ref[j] - stat_ref[j : j + 1]) * rstd
            value = back_ref[j] - (total[j : j + 1] + norm * total[4 + j : 5 + j]) / pixel_total
            grad_ref[j] = (scale_ref[j : j + 1] * rstd * value * mask).astype(BF16)
        dhid = silu_slope(pool_ref[1]) * total[8:]
        pool_shift = column_sum(dhid)
        pool_scale = column_sum(dhid * pool_ref[0])
        value = dhid - count_ref[...] * (pool_shift + pool_ref[0] * pool_scale) / pixel_total
        dpool_ref[...] = (scale_ref[4:5] * pool_ref[2] * value).astype(BF16)
        sum_ref[...] = jnp.zeros(sum_ref.shape, F32)
        sum_ref[0:4] = total[4:8]
        sum_ref[4:5] = pool_scale
        sum_ref[5:9] = total[0:4]
        sum_ref[9:10] = pool_shift

    shapes = [((4, pixels, out), BF16), ((images, out), BF16), ((16, out), F32)]
    operands = [*sums, back, branch, stats, scales, counts, pool]
    return small_kernel(kernel, "branch_gradients", operands, shapes)


def local(
    features,
    row_image,
    cotangent,
    w_one,
    dilated_weight,
    w_pool,
    w_proj,
    scales,
    shifts,
    out_scale,
    out_shift,
):
    micro, rows, cols, channels = features.shape
    ha, wa = lax.axis_size("ha"), lax.axis_size("wa")
    h, z = lax.axis_index("ha"), lax.axis_index("wa")
    planes = wa // micro
    batch, part = z // planes, z % planes
    deep = w_one.shape[0] // planes
    out = w_one.shape[1] * wa
    valid = cols * wa - PADC
    blocks = -(-valid // cols)
    prows = -(-rows // 16) * 16
    height, pheight = rows * ha, prows * ha
    images = IMG_DEV * ha
    pixels = float(height * valid)
    size = cols * rows

    fast = planes == 1 and wa == 4 and 6 * valid * pheight * out < (16 << 20) and channels % out == 0 and deep == out

    taps = [live_taps(r, valid) for r in RATES]
    few = w_proj.shape[0]
    side = jnp.pad(w_proj.T, ((0, 0), (0, w_one.shape[0] - few)))
    turned = dilated_weight.swapaxes(2, 3)
    if fast:
        weights = pack_weights(w_one.T, turned, w_pool.T, side, taps)
    else:
        picked = [turned[j, 3 * (a + 1) + b + 1] for j in range(3) for a, b in taps[j]]
        weights = gather_columns(jnp.stack([w_one.T, *picked, w_pool.T, side]))

    if fast:
        slots = extract(features.transpose(1, 2, 0, 3), cotangent.transpose(1, 2, 0, 3), z)
        tall, fit = slots[0].shape[0], ceil_to(valid * rows, 16)
        early = gather_early(weights, slots[0])
        slots = [slots[0]] + [swap(slots[k], "wa", k, lambda i: i < blocks) for k in range(1, wa)]
        slots = after(slots, early)
        high, thick = ceil_to(blocks * tall, 128), ceil_to(fit, 128)
        in_piece = block_rows(high, tall, rows, cols, valid, rows)
        in_chunk = block_rows(high, tall, rows, cols, valid, prows)
        spots = spots_of(np.arange(fit), in_piece)
        cot_spots = spots_of(np.arange(valid * prows), in_chunk)
        send, cot = choose(slots, z, blocks, spots, cot_spots, deep)
        raw = lax.all_to_all(send, "ha", 0, 0, tiled=True)
    else:
        f = features.transpose(0, 2, 1, 3).reshape(micro, size, ha, planes, deep)
        f = f.transpose(0, 3, 1, 2, 4).reshape(wa, size, ha * deep)
        c = cotangent.transpose(0, 2, 1, 3).reshape(micro, size, out)
        load = jnp.concatenate([f, jnp.repeat(c, planes, axis=0)], axis=-1)
        slots = [take(load, z)]
        for k in range(1, wa):
            slots.append(swap(take(load, z ^ k), "wa", k, lambda i: i < blocks))
        slots = jnp.stack(slots)
        block = jnp.concatenate([take(slots, z ^ j) for j in range(blocks)])[: valid * rows]
        raw = block[:, : ha * deep].reshape(valid * rows, ha, deep).swapaxes(0, 1)
        raw = lax.all_to_all(raw, "ha", 0, 0, tiled=True)
        cot = block[:, ha * deep :].reshape(valid, rows, out)
        cot = jnp.pad(cot, ((0, 0), (0, prows - rows), (0, 0))).reshape(valid * prows, out)
    if fast:
        weights = gather_late(weights, early, send)
    if fast:
        proj = order_chunks(*gather_chunks(weights[-1]), h, few)
    else:
        proj = in_order(*gather_chunks(weights[-1]))[..., :few].swapaxes(1, 2).reshape(ha * few, out)
    if planes > 1:
        weights = lax.dynamic_slice_in_dim(weights, part * deep, deep, 2)
    wide_pool = weights[-2]

    order = h ^ jnp.arange(ha, dtype=jnp.int32)
    labels = by_distance(take(row_image, batch).reshape(ha, rows))
    number = order[:, None] * rows + jnp.arange(rows, dtype=jnp.int32)[None, :]
    pad = ((0, 0), (0, prows - rows))
    labels = jnp.pad(labels, pad, constant_values=-1).reshape(pheight)
    number = jnp.pad(number, pad, constant_values=-(1 << 20)).reshape(pheight)
    same = (labels[:, None] == labels[None, :]) & (labels >= 0)[:, None]
    apart = number[None, :] - number[:, None]
    shift = [
        jnp.stack([(same & (apart == a * r)).astype(BF16) for a in (-1, 1)]) for r in RATES
    ]
    ids = jnp.arange(images, dtype=jnp.int32)
    member = (labels[:, None] == ids[None, :]).astype(F32)
    counts = jnp.sum(member, axis=0) * valid
    own = member[:prows]
    mask = jnp.tile(jnp.sum(own, axis=1), valid)[:, None]

    ahead = [1, 1 + len(taps[0]), 1 + len(taps[0]) + len(taps[1])]
    group = [(None, 0, 0, [(0, 0)])] + [(shift[j], ahead[j], RATES[j], taps[j]) for j in range(3)]
    if fast:
        place = spots_of(padded_rows(valid * prows, valid, prows, rows), np.arange(thick))
        x, row_sums = arrange(raw, place, h, valid, prows)
        unplace = spots_of(np.arange(fit), padded_rows(ceil_to(valid * prows, 128), valid, prows, rows))
    else:
        x = by_distance(raw).reshape(ha, valid, rows, deep)
        x = jnp.pad(x, ((0, 0), (0, 0), (0, prows - rows), (0, 0)))
        x = x.swapaxes(0, 1).reshape(valid, pheight, deep)
        row_sums = jnp.sum(x.astype(F32), axis=0)
    if fast:
        branch_parts = reduce_square(*forward_kernel(x, weights, group, prows))
    else:
        sums = jnp.stack([forward_plain(x, s, weights[n : n + len(t)], r, t) for s, n, r, t in group])
        sums = sums.astype(BF16).reshape(len(group), valid, ha // 2, 2, prows, out)
        sums = sums.transpose(3, 2, 0, 1, 4, 5).reshape(2, ha // 2, len(group), valid * prows, out)
        branch = sum_chunks(spread_chunks(sums[0], sums[1]), planes)
    pooled = (jnp.dot(member.T, row_sums, precision=HIGHEST) / counts[:, None]).astype(BF16)
    pool_part = dot(pooled, wide_pool, NT)

    weighted = counts[:, None]
    once = (part == 0).astype(F32)
    if fast:
        branch, first = branch_sums(branch_parts, pool_part)
        joined, projected, second, stats, pool = project(
            plane_parts(first), branch, scales, shifts, weighted, own, proj, rows, pixels
        )
        activation, proj_norm, dproj_hid, third, proj_rstd = activate(
            plane_parts(second), projected, cot, out_scale, out_shift, prows, rows, pixels
        )
        third, grad_proj, dhid, fourth = unproject(
            plane_parts(third),
            proj_norm,
            dproj_hid,
            proj_rstd,
            out_scale,
            proj,
            joined,
            branch,
            stats,
            scales,
            shifts,
            own,
            ha,
            rows,
            pixels,
        )
        dbranch, dpool, sums = branch_gradients(
            plane_parts(fourth), dhid, branch, stats, scales, weighted, pool, prows, rows, pixels
        )
        sums = jnp.concatenate([sums[:10], third[:2]])
    else:
        first = plane_sum(
            jnp.concatenate(
                [once * jnp.sum(branch, axis=1), once * jnp.sum(branch * branch, axis=1), pool_part]
            ),
            planes,
        )
        mean = first[0:4] / pixels
        rstd = lax.rsqrt(first[4:8] / pixels - mean * mean + EPS)
        pool_out = first[8:]
        norm = (branch - mean[:, None]) * rstd[:, None]
        hid = norm * scales[:4, None] + shifts[:4, None]
        act = silu(hid)
        weighted = counts[:, None]
        pool_mean = jnp.sum(weighted * pool_out, axis=0) / pixels
        pool_second = jnp.sum(weighted * pool_out * pool_out, axis=0) / pixels
        pool_rstd = lax.rsqrt(pool_second - pool_mean * pool_mean + EPS)
        pool_norm = (pool_out - pool_mean) * pool_rstd
        pool_hid = pool_norm * scales[4] + shifts[4]
        spread = jnp.dot(own, silu(pool_hid), precision=HIGHEST)
        spread = jnp.broadcast_to(spread[None], (valid, prows, out)).reshape(valid * prows, out)
        joined = jnp.concatenate([act[0], act[1], act[2], act[3], spread], axis=-1).astype(BF16)
        projected = jnp.dot(joined, proj, preferred_element_type=F32)

        held = projected * mask
        second = plane_sum(
            jnp.stack([jnp.sum(held, axis=0), jnp.sum(held * held, axis=0)]) * once, planes
        )
        proj_mean = second[0] / pixels
        proj_rstd = lax.rsqrt(second[1] / pixels - proj_mean * proj_mean + EPS)
        proj_norm = (projected - proj_mean) * proj_rstd
        proj_hid = proj_norm * out_scale + out_shift
        activation = silu(proj_hid).astype(BF16)
        dproj_hid = cot.astype(F32) * mask * silu_slope(proj_hid)
        third = plane_sum(
            jnp.stack([jnp.sum(dproj_hid, axis=0), jnp.sum(dproj_hid * proj_norm, axis=0)]) * once, planes
        )
        dproj = (
            out_scale * proj_rstd * (dproj_hid - (third[0] + proj_norm * third[1]) / pixels) * mask
        ).astype(BF16)
        djoined = lax.dot_general(dproj, proj, (((1,), (1,)), ((), ())), preferred_element_type=F32)
        grad_proj = dot(dproj, joined, TN)
        dact = jnp.stack([djoined[:, j * out : (j + 1) * out] for j in range(4)])
        dspread = jnp.sum(djoined[:, 4 * out :].reshape(valid, prows, out), axis=0)
        image_part = jnp.dot(own.T, dspread, precision=HIGHEST)
        dhid = dact * silu_slope(hid) * mask
        fourth = plane_sum(
            jnp.concatenate([jnp.sum(dhid, axis=1), jnp.sum(dhid * norm, axis=1), image_part]) * once,
            planes,
        )
        branch_shift, branch_scale, image_total = fourth[0:4], fourth[4:8], fourth[8:]
        dbranch = (
            (scales[:4] * rstd)[:, None]
            * (dhid - (branch_shift[:, None] + norm * branch_scale[:, None]) / pixels)
            * mask
        ).astype(BF16)
        dpool_hid = silu_slope(pool_hid) * image_total
        pool_shift = jnp.sum(dpool_hid, axis=0)
        pool_scale = jnp.sum(dpool_hid * pool_norm, axis=0)
        dpool = (
            scales[4] * pool_rstd * (dpool_hid - weighted * (pool_shift + pool_norm * pool_scale) / pixels)
        ).astype(BF16)
        sums = jnp.concatenate([branch_scale, pool_scale[None], branch_shift, pool_shift[None], third])
    grad_pool = dot(dpool, pooled, TN)
    dpooled = dot(dpool, wide_pool, NN)

    total = jnp.dot(member, dpooled / counts[:, None], precision=HIGHEST)
    if fast:
        pieces = gather_square(dbranch)
        tap_grads = weights_backward(x, group, pieces, wa, prows)
        back = features_backward(x, weights, group, pieces, total, h, unplace, fit, prows)
    else:
        total = jnp.broadcast_to(total[None], (valid,) + total.shape)
        near, far = gather_chunks(dbranch)
        every = jnp.stack([near, far], axis=1).reshape(ha, len(group), valid, prows, out)
        every = every.transpose(1, 2, 0, 3, 4).reshape(len(group), valid, pheight, out)
        found = []
        for (s, n, r, t), d in zip(group, every):
            grads, total = backward_plain(x, s, weights[n : n + len(t)], r, t, d, total)
            found.append(grads.reshape(len(t), wa, out // wa, deep).swapaxes(0, 1).astype(BF16))
        tap_grads = jnp.concatenate(found, axis=1)
        back = total.astype(BF16).reshape(valid, ha, prows, deep)[:, :, :rows]
        back = back.swapaxes(0, 1).reshape(ha, valid * rows, deep)
        back = by_distance(back)

    def in_place(grads):
        if planes == 1:
            return grads
        full = jnp.zeros(grads.shape[:-1] + (deep * planes,), grads.dtype)
        return lax.dynamic_update_slice_in_dim(full, grads, part * deep, grads.ndim - 1)

    if not fast:
        grad_proj = (grad_proj * once).reshape(out, ha, few).swapaxes(0, 1)
        grad_proj = jnp.pad(grad_proj, ((0, 0), (0, 0), (0, w_one.shape[0] - few))).astype(BF16)
    proj_chunk = lax.psum_scatter(grad_proj, "ha", scatter_dimension=0, tiled=False)
    grad_pool = in_place(grad_pool.astype(BF16)).reshape(wa, 1, out // wa, -1)
    proj_chunk = proj_chunk.reshape(wa, 1, out // wa, -1)
    tap_grads = line_scatter(in_place(tap_grads))
    rest = jnp.concatenate([grad_pool, proj_chunk], axis=1)
    if not fast:
        rest = line_scatter(rest)
    tap_out = [tap_grads[n : n + len(t)] for n, t in zip(ahead, taps)]
    blank = jnp.zeros((out // wa, w_one.shape[0]), F32)
    atrous = []
    for j in range(3):
        if len(taps[j]) == 9:
            atrous.append(tap_out[j])
        else:
            found = {3 * (a + 1) + b + 1: tap_out[j][t] for t, (a, b) in enumerate(taps[j])}
            atrous.append(jnp.stack([found.get(t, blank) for t in range(9)]))
    atrous = jnp.stack(atrous)
    atrous_out = atrous.swapaxes(2, 3)
    back = lax.all_to_all(back, "ha", 0, 0, tiled=True)

    def home(i, k):
        return i ^ k < blocks

    if fast:
        piece_spots = spots_of(block_rows(wa * tall, tall, rows, cols, valid, rows), np.arange(thick))
        chunk_spots = spots_of(block_rows(wa * tall, tall, rows, cols, valid, prows), np.arange(valid * prows))
        got = unchoose(
            back, activation, z, blocks, piece_spots.reshape(wa, tall, thick), chunk_spots.reshape(wa, tall, -1)
        )
        got = [got[0]] + [swap(got[k], "wa", k, partial(home, k=k)) for k in range(1, wa)]
        df, acts = interleave(got, z, blocks, rows, cols, out, [atrous])
        wide = jnp.broadcast_to(jnp.pad(sums, ((0, 4), (0, 0)))[None], (wa, 16, out))
        rest = jnp.concatenate([rest.astype(F32).reshape(wa, -1, out), wide], axis=1)
        rest = exchange_sum(after(rest, got[0]))
        sums = rest[-16:-4]
        rest = rest[:-16].reshape(2, -1, out)
    else:

        def send_home(array):
            array = jnp.pad(array, ((0, wa * size - valid * rows), (0, 0))).reshape(wa, size, -1)
            got = [take(array, z)]
            got += [swap(take(array, z ^ k), "wa", k, partial(home, k=k)) for k in range(1, wa)]
            got = jnp.stack(got)
            got = jnp.where(z < blocks, got, jnp.zeros((), got.dtype))
            return jnp.stack([take(got, z ^ t) for t in range(wa)])

        back = back.swapaxes(0, 1).reshape(valid * rows, ha * deep)
        df = send_home(back).reshape(micro, planes, cols, rows, ha, deep)
        df = df.transpose(0, 3, 2, 4, 1, 5).reshape(features.shape)
        activation = activation.reshape(valid, prows, out)[:, :rows].reshape(valid * rows, out)
        acts = send_home(activation).reshape(micro, planes, cols, rows, out)[:, 0].swapaxes(1, 2)
    if not fast:
        sums = sums * once
        sums = tree_sum([sums] + [swap(sums, "wa", k) for k in range(1, wa)])
    one_out, pool_grad_out, proj_out = tap_grads[0].T, rest[0].T, rest[1][:, :few].T
    return (
        acts,
        df,
        one_out,
        atrous_out,
        pool_grad_out,
        proj_out,
        sums[0:5],
        sums[5:10],
        sums[11],
        sums[10],
    )


def solution(mesh):
    specs = (
        P(None, "ha", "wa", None),
        P(),
        P(None, "ha", "wa", None),
        P("ha", "wa"),
        P(None, None, "ha", "wa"),
        P("ha", "wa"),
        P("ha", "wa"),
        P(),
        P(),
        P(),
        P(),
    )
    out_specs = (
        P(None, "ha", "wa", None),
        P(None, "ha", "wa", None),
        P("ha", "wa"),
        P(None, None, "ha", "wa"),
        P("ha", "wa"),
        P("ha", "wa"),
        P(),
        P(),
        P(),
        P(),
    )
    return jax.shard_map(local, mesh=mesh, in_specs=specs, out_specs=out_specs, check_vma=False)
```

time: 499 us -> 448 us (0.90)
  local copies, waits for them, and re-layouts: 63.2 us -> 35.3 us
  other arithmetic: 30.4 us -> 14.6 us
    unnamed x190 -> x88, local copies, waits for them, and re-layouts: 37.1 us -> 16 us
    ppermute x71 -> x55, waiting for transfers between devices: 207 us -> 187 us  [swap(): return lax.ppermute(array, axis, pairs)]
    ppermute x0 -> x7, starting transfers between devices: none -> 19.9 us  [neighbour(): return lax.ppermute(array, 'wa', pairs)]
    ppermute x71 -> x55, starting transfers between devices: 85.9 us -> 68.1 us  [swap(): return lax.ppermute(array, axis, pairs)]
    all_to_all x1, waiting for transfers between devices: 0.01 us -> 17.4 us  [local(): back = lax.all_to_all(back, 'ha', 0, 0, tiled=True)]
    all_to_all x1, waiting for transfers between devices: 16.6 us -> 5.6 us  [local(): raw = lax.all_to_all(send, 'ha', 0, 0, tiled=True)]
    ppermute x0 -> x7, waiting for transfers between devices: none -> 10.3 us  [neighbour(): return lax.ppermute(array, 'wa', pairs)]
    pallas_call x3 -> x1, Pallas kernels: 19.3 us -> 9.08 us  [forward_kernel(): pl.pallas_call(kernel, out_shape=[shape] * 2, in_specs=[WHOLE] * len(oper...]
  transfers between devices with their start and end apart: 78 -> 66, of which waited for: 33 -> 29; matrix products, arithmetic and copies ran while one was open for 13% -> 6% of each run, Pallas kernels for 10% -> 9%
where the time goes in v2:
time: 448 us; the launch traced here: 442 us
  waiting for transfers between devices  220 us (49%)
  starting transfers between devices  95.5 us (21%)
  Pallas kernels  59.7 us (13%)
  local copies, waits for them, and re-layouts  35.3 us (8%)
  between operations  15.1 us (3%)
  other arithmetic  14.6 us (3%)
    ppermute x55, waiting for transfers between devices, swap(): return lax.ppermute(array, axis, pairs)  187 us
    ppermute x55, starting transfers between devices, swap(): return lax.ppermute(array, axis, pairs)  68.1 us
    ppermute x7, starting transfers between devices, neighbour(): return lax.ppermute(array, 'wa', pairs)  19.9 us
    pallas_call x1, Pallas kernels, features_backward(): pl.pallas_call(kernel, out_shape=jax.ShapeDtypeStruct((ha, fit, deep), BF...  18.3 us
    all_to_all x1, waiting for transfers between devices, local(): back = lax.all_to_all(back, 'ha', 0, 0, tiled=True)  17.4 us
    unnamed x88, local copies, waits for them, and re-layouts  16 us
    pallas_call x1, Pallas kernels, weights_backward(): pl.pallas_call(kernel, out_shape=jax.ShapeDtypeStruct(shape, BF16), grid=...  14.1 us
    ppermute x7, waiting for transfers between devices, neighbour(): return lax.ppermute(array, 'wa', pairs)  10.3 us
  transfers between devices with their start and end apart: 66, of which 29 were waited for; matrix products, arithmetic and copies ran while one was open for 6% of the time, Pallas kernels for 9%

profile of v2, /device:TPU:8, one launch (start us, length us, event | category | flops | bytes accessed | tf_op | source)
XLA Modules:
  0.0 442.0 jit_solution(6936118116389085932)
XLA Ops:
  10.7 3.5 collective-permute-start.3
  14.2 3.3 collective-permute-start.4
  17.5 4.4 reshape.905
  27.6 4.4 %extract.1 = (bf16[144,2304]{1,0:T(8,128)(2,1)S(1)}, bf16[144,2304]{1,0:T(8,128)(2,1)S(1)}, bf16[144,2304]{1,0:T(8,128)(2,1)S(1)}, bf16[144,2304]{1,0:T(8,128)(2,1)S(1)}) custom-call(s32[1]{0:T(128)} %bitcast.z_ref, bf16[528,2048]{1,0:T(8,128)(2,1)S(1)} %pad.24.f_ref, bf16[528,256]{1,0:T(8,128)(2,1)S(1)} %pad.25.c_ref, bf16[4,144,640]{2,1,0:T(8,128)(2,1)S(1)} %copy-done.17), custom_call_target="tpu_custom_call" | custom-call | tf_op jit(solution)/shard_map/extract/pallas_call | solution.py:310
  35.2 3.2 collective-permute-start.6
  41.7 6.0 %collective-permute-start.2 = (bf16[144,2304]{1,0:T(8,128)(2,1)S(1)}, bf16[144,2304]{1,0:T(8,128)(2,1)S(1)}, u32[]{:S(2)}, u32[]{:S(2)}) collective-permute-start(bf16[144,2304]{1,0:T(8,128)(2,1)S(1)} %get-tuple-element.56), channel_id=1, source_target_pairs={{0,3},{1,2},{2,1},{4,7},{5,6},{6,5},{8,11},{9,10},{10,9},{12,15},{... | collective-permute-start | bytes 1990664 | tf_op jit(solution)/shard_map/ppermute | solution.py:32
  47.7 35.0 %collective-permute-done.refs_1_ = bf16[144,2304]{1,0:T(8,128)(2,1)S(1)} collective-permute-done((bf16[144,2304]{1,0:T(8,128)(2,1)S(1)}, bf16[144,2304]{1,0:T(8,128)(2,1)S(1)}, u32[]{:S(2)}, u32[]{:S(2)}) %collective-permute-start) | collective-permute-done | bytes 663584 | tf_op jit(solution)/shard_map/ppermute | solution.py:32
  85.5 11.9 %collective-permute-done.2.refs_3_ = bf16[144,2304]{1,0:T(8,128)(2,1)S(1)} collective-permute-done((bf16[144,2304]{1,0:T(8,128)(2,1)S(1)}, bf16[144,2304]{1,0:T(8,128)(2,1)S(1)}, u32[]{:S(2)}, u32[]{:S(2)}) %collective-permute-start.2) | collective-permute-done | bytes 663584 | tf_op jit(solution)/shard_map/ppermute | solution.py:32
  100.4 5.4 %collective-permute-start.7 = (bf16[24,64,256]{2,1,0:T(8,128)(2,1)}, bf16[24,64,256]{2,1,0:T(8,128)(2,1)}, u32[]{:S(2)}, u32[]{:S(2)}) collective-permute-start(bf16[24,64,256]{2,1,0:T(8,128)(2,1)} %collective-permute-done.3), channel_id=1, source_target_pairs={{1,2},{5,6},{9,10},{13,14},{17,18},{21,22},{25,26},{29,30}} | collective-permute-start | bytes 2359304 | tf_op jit(solution)/shard_map/ppermute | solution.py:138
  105.8 3.7 all-to-all-start
  112.1 7.8 %collective-permute-done.7 = bf16[24,64,256]{2,1,0:T(8,128)(2,1)} collective-permute-done((bf16[24,64,256]{2,1,0:T(8,128)(2,1)}, bf16[24,64,256]{2,1,0:T(8,128)(2,1)}, u32[]{:S(2)}, u32[]{:S(2)}) %collective-permute-start.7) | collective-permute-done | bytes 786464 | tf_op jit(solution)/shard_map/ppermute | solution.py:138
  123.5 5.6 %all-to-all-done.raw_ref = bf16[8,352,256]{2,1,0:T(8,128)(2,1)S(1)} async-done(((bf16[8,352,256]{2,1,0:T(8,128)(2,1)}), bf16[8,352,256]{2,1,0:T(8,128)(2,1)S(1)}, u32[]{:S(2)}, u32[]{:S(2)}) %all-to-all-start) | async-done | bytes 1441824 | tf_op jit(solution)/shard_map/all_to_all | solution.py:936
  134.2 9.1 %forward.1 = (bf16[4,4,416,256]{3,2,1,0:T(8,128)(2,1)S(1)}, bf16[4,4,416,256]{3,2,1,0:T(8,128)(2,1)S(1)}) custom-call(bf16[13,256,256]{2,1,0:T(8,128)(2,1)S(1)} %get-tuple-element.64.x_ref, bf16[24,256,256]{2,1,0:T(8,128)(2,1)S(1)} %pad_maximum_fusion.w_ref, bf16[2,256,256]{2,1,0:T(8,128)(2,1)S(1)} %get-tuple-element.140.refs_0_, ...), custom_call_target="tpu_custom_call" | custom-call | tf_op jit(solution)/shard_map/forward/pallas_call | solution.py:559
  143.3 6.0 %collective-permute-done.10 = bf16[4,4,416,256]{3,2,1,0:T(8,128)(2,1)S(1)} collective-permute-done((bf16[4,4,416,256]{3,2,1,0:T(8,128)(2,1)S(1)}, bf16[4,4,416,256]{3,2,1,0:T(8,128)(2,1)S(1)}, u32[]{:S(2)}, u32[]{:S(2)}) %collective-permute-start.10) | collective-permute-done | bytes 3407904 | tf_op jit(solution)/shard_map/ppermute | solution.py:32
  155.7 19.4 %collective-permute-done.24 = bf16[256,256]{1,0:T(8,128)(2,1)S(1)} collective-permute-done((bf16[256,256]{1,0:T(8,128)(2,1)S(1)}, bf16[256,256]{1,0:T(8,128)(2,1)S(1)}, u32[]{:S(2)}, u32[]{:S(2)}) %collective-permute-start.24) | collective-permute-done | bytes 131104 | tf_op jit(solution)/shard_map/ppermute | solution.py:32
  180.7 9.4 %collective-permute-done.12.low_last = bf16[2,416,256]{2,1,0:T(8,128)(2,1)S(1)} collective-permute-done((bf16[2,416,256]{2,1,0:T(8,128)(2,1)S(1)}, bf16[2,416,256]{2,1,0:T(8,128)(2,1)S(1)}, u32[]{:S(2)}, u32[]{:S(2)}) %collective-permute-start.12) | collective-permute-done | bytes 426016 | tf_op jit(solution)/shard_map/ppermute | solution.py:32
  240.0 10.2 %collective-permute-done.47.refs_4_ = bf16[2,416,256]{2,1,0:T(8,128)(2,1)S(1)} collective-permute-done((bf16[2,416,256]{2,1,0:T(8,128)(2,1)S(1)}, bf16[2,416,256]{2,1,0:T(8,128)(2,1)S(1)}, u32[]{:S(2)}, u32[]{:S(2)}) %collective-permute-start.47) | collective-permute-done | bytes 426016 | tf_op jit(solution)/shard_map/ppermute | solution.py:32
  254.9 16.9 %collective-permute-done.49.refs_6_ = bf16[2,2,416,256]{3,2,1,0:T(8,128)(2,1)} collective-permute-done((bf16[2,2,416,256]{3,2,1,0:T(8,128)(2,1)}, bf16[2,2,416,256]{3,2,1,0:T(8,128)(2,1)}, u32[]{:S(2)}, u32[]{:S(2)}) %collective-permute-start.49) | collective-permute-done | bytes 852000 | tf_op jit(solution)/shard_map/ppermute | solution.py:32
  274.3 3.0 collective-permute-done.52.refs_9_
  278.1 14.1 %weights_backward.1 = bf16[4,22,64,256]{3,2,1,0:T(8,128)(2,1)} custom-call(bf16[13,256,256]{2,1,0:T(8,128)(2,1)} %copy-done.7, bf16[2,256,256]{2,1,0:T(8,128)(2,1)} %copy-done.8, bf16[2,256,256]{2,1,0:T(8,128)(2,1)} %get-tuple-element.141.refs_1_, bf16[2,256,256]{2,1,0:T(8,128)(2,1)} %add_convert_fusion.2.refs_2_, bf16[4,416,256]{2,1,0:T(8,128)(2,1)} %copy-done.6, ...), custom_call_target="tpu_custom_call" | custom-call | tf_op jit(solution)/shard_map/weights_backward/pallas_call | solution.py:631
  293.4 18.3 %features_backward.1 = bf16[8,352,256]{2,1,0:T(8,128)(2,1)} custom-call(s32[1]{0:T(128)} %bitcast.1.h_ref, f32[256,256]{1,0:T(8,128)} %fusion.12.start_ref, bf16[24,256,256]{2,1,0:T(8,128)(2,1)} %copy-done.2, bf16[352,512]{1,0:T(8,128)(2,1)} %constant.115.clone.place_ref, bf16[2,256,256]{2,1,0:T(8,128)(2,1)} %copy-done.8, ...), custom_call_target="tpu_custom_call" | custom-call | tf_op jit(solution)/shard_map/features_backward/pallas_call | solution.py:683
  311.7 3.7 all-to-all-start.1
  317.6 17.4 %all-to-all-done.1.pieces_ref = bf16[8,352,256]{2,1,0:T(8,128)(2,1)S(1)} async-done(((bf16[8,352,256]{2,1,0:T(8,128)(2,1)}), bf16[8,352,256]{2,1,0:T(8,128)(2,1)S(1)}, u32[]{:S(2)}, u32[]{:S(2)}) %all-to-all-start.1) | async-done | bytes 1441824 | tf_op jit(solution)/shard_map/all_to_all | solution.py:1142
  335.0 2.9 unchoose.1
  341.1 8.3 %collective-permute-start.60 = (f32[144,256]{1,0:T(8,128)S(1)}, f32[144,256]{1,0:T(8,128)S(1)}, u32[]{:S(2)}, u32[]{:S(2)}) collective-permute-start(f32[144,256]{1,0:T(8,128)S(1)} %get-tuple-element.118), channel_id=1, source_target_pairs={{0,2},{1,3},{2,0},{3,1},{4,6},{5,7},{6,4},{7,5},{8,10},{9,11},{10,... | collective-permute-start | bytes 442376 | tf_op jit(solution)/shard_map/ppermute | solution.py:32
  350.0 3.4 collective-permute-start.56
  354.6 6.7 %collective-permute-start.58 = (bf16[144,2304]{1,0:T(8,128)(2,1)}, bf16[144,2304]{1,0:T(8,128)(2,1)S(1)}, u32[]{:S(2)}, u32[]{:S(2)}) collective-permute-start(bf16[144,2304]{1,0:T(8,128)(2,1)} %get-tuple-element.89), channel_id=1, source_target_pairs={{1,2},{2,1},{3,0},{5,6},{6,5},{7,4},{9,10},{10,9},{11,8},{13,14},{... | collective-permute-start | bytes 1990664 | tf_op jit(solution)/shard_map/ppermute | solution.py:32
  363.7 5.5 %collective-permute-done.61 = f32[144,256]{1,0:T(8,128)S(1)} collective-permute-done((f32[144,256]{1,0:T(8,128)S(1)}, f32[144,256]{1,0:T(8,128)S(1)}, u32[]{:S(2)}, u32[]{:S(2)}) %collective-permute-start.61) | collective-permute-done | bytes 147488 | tf_op jit(solution)/shard_map/ppermute | solution.py:32
  376.3 13.6 %collective-permute-done.56.refs_1_.refs_5_ = bf16[144,2304]{1,0:T(8,128)(2,1)S(1)} collective-permute-done((bf16[144,2304]{1,0:T(8,128)(2,1)}, bf16[144,2304]{1,0:T(8,128)(2,1)S(1)}, u32[]{:S(2)}, u32[]{:S(2)}) %collective-permute-start.56) | collective-permute-done | bytes 663584 | tf_op jit(solution)/shard_map/ppermute | solution.py:32
  389.9 6.2 %collective-permute-done.57.refs_2_.refs_6_ = bf16[144,2304]{1,0:T(8,128)(2,1)S(1)} collective-permute-done((bf16[144,2304]{1,0:T(8,128)(2,1)}, bf16[144,2304]{1,0:T(8,128)(2,1)S(1)}, u32[]{:S(2)}, u32[]{:S(2)}) %collective-permute-start.57) | collective-permute-done | bytes 663584 | tf_op jit(solution)/shard_map/ppermute | solution.py:32
  396.2 28.9 %collective-permute-done.58.refs_3_.refs_7_ = bf16[144,2304]{1,0:T(8,128)(2,1)S(1)} collective-permute-done((bf16[144,2304]{1,0:T(8,128)(2,1)}, bf16[144,2304]{1,0:T(8,128)(2,1)S(1)}, u32[]{:S(2)}, u32[]{:S(2)}) %collective-permute-start.58) | collective-permute-done | bytes 663584 | tf_op jit(solution)/shard_map/ppermute | solution.py:32
  425.0 3.9 interleave.1
  (267 shorter events, 125.7 us)
Async XLA Ops:
  10.7 21.3 %collective-permute-start.3 = (bf16[24,64,256]{2,1,0:T(8,128)(2,1)S(1)}, bf16[24,64,256]{2,1,0:T(8,128)(2,1)}, u32[]{:S(2)}, u32[]{:S(2)}) collective-permute-start(bf16[24,64,256]{2,1,0:T(8,128)(2,1)S(1)} %pack_weights.1), channel_id=1, source_target_pairs={{0,1},{1,2},{2,3},{4,5},{5,6},{6,7},{8,9},{9,10},{10,11},{12,13},{... | collective-permute-start | bytes 2359304 | tf_op jit(solution)/shard_map/ppermute | solution.py:138
  14.2 21.0 %collective-permute-start.4 = (bf16[24,64,256]{2,1,0:T(8,128)(2,1)S(1)}, bf16[24,64,256]{2,1,0:T(8,128)(2,1)}, u32[]{:S(2)}, u32[]{:S(2)}) collective-permute-start(bf16[24,64,256]{2,1,0:T(8,128)(2,1)S(1)} %pack_weights.1), channel_id=1, source_target_pairs={{1,0},{2,1},{3,2},{5,4},{6,5},{7,6},{9,8},{10,9},{11,10},{13,12},{... | collective-permute-start | bytes 2359304 | tf_op jit(solution)/shard_map/ppermute | solution.py:138
  32.0 65.4 %collective-permute-start.5 = (bf16[24,64,256]{2,1,0:T(8,128)(2,1)}, bf16[24,64,256]{2,1,0:T(8,128)(2,1)S(1)}, u32[]{:S(2)}, u32[]{:S(2)}) collective-permute-start(bf16[24,64,256]{2,1,0:T(8,128)(2,1)} %collective-permute-done.3), channel_id=1, source_target_pairs={{2,3},{6,7},{10,11},{14,15},{18,19},{22,23},{26,27},{30,31}} | collective-permute-start | bytes 2359304 | tf_op jit(solution)/shard_map/ppermute | solution.py:138
  35.2 62.2 %collective-permute-start.6 = (bf16[24,64,256]{2,1,0:T(8,128)(2,1)}, bf16[24,64,256]{2,1,0:T(8,128)(2,1)}, u32[]{:S(2)}, u32[]{:S(2)}) collective-permute-start(bf16[24,64,256]{2,1,0:T(8,128)(2,1)} %collective-permute-done.4), channel_id=1, source_target_pairs={{1,0},{2,1},{5,4},{6,5},{9,8},{10,9},{13,12},{14,13},{17,16},{18,1... | collective-permute-start | bytes 2359304 | tf_op jit(solution)/shard_map/ppermute | solution.py:138
  38.5 44.2 %collective-permute-start = (bf16[144,2304]{1,0:T(8,128)(2,1)S(1)}, bf16[144,2304]{1,0:T(8,128)(2,1)S(1)}, u32[]{:S(2)}, u32[]{:S(2)}) collective-permute-start(bf16[144,2304]{1,0:T(8,128)(2,1)S(1)} %get-tuple-element.54), channel_id=1, source_target_pairs={{0,1},{1,0},{2,3},{4,5},{5,4},{6,7},{8,9},{9,8},{10,11},{12,13},{1... | collective-permute-start | bytes 1990664 | tf_op jit(solution)/shard_map/ppermute | solution.py:32
  40.4 45.1 %collective-permute-start.1 = (bf16[144,2304]{1,0:T(8,128)(2,1)S(1)}, bf16[144,2304]{1,0:T(8,128)(2,1)S(1)}, u32[]{:S(2)}, u32[]{:S(2)}) collective-permute-start(bf16[144,2304]{1,0:T(8,128)(2,1)S(1)} %get-tuple-element.55), channel_id=1, source_target_pairs={{0,2},{1,3},{2,0},{4,6},{5,7},{6,4},{8,10},{9,11},{10,8},{12,14},{... | collective-permute-start | bytes 1990664 | tf_op jit(solution)/shard_map/ppermute | solution.py:32
  41.7 55.7 %collective-permute-start.2 = (bf16[144,2304]{1,0:T(8,128)(2,1)S(1)}, bf16[144,2304]{1,0:T(8,128)(2,1)S(1)}, u32[]{:S(2)}, u32[]{:S(2)}) collective-permute-start(bf16[144,2304]{1,0:T(8,128)(2,1)S(1)} %get-tuple-element.56), channel_id=1, source_target_pairs={{0,3},{1,2},{2,1},{4,7},{5,6},{6,5},{8,11},{9,10},{10,9},{12,15},{... | collective-permute-start | bytes 1990664 | tf_op jit(solution)/shard_map/ppermute | solution.py:32
  100.4 19.6 %collective-permute-start.7 = (bf16[24,64,256]{2,1,0:T(8,128)(2,1)}, bf16[24,64,256]{2,1,0:T(8,128)(2,1)}, u32[]{:S(2)}, u32[]{:S(2)}) collective-permute-start(bf16[24,64,256]{2,1,0:T(8,128)(2,1)} %collective-permute-done.3), channel_id=1, source_target_pairs={{1,2},{5,6},{9,10},{13,14},{17,18},{21,22},{25,26},{29,30}} | collective-permute-start | bytes 2359304 | tf_op jit(solution)/shard_map/ppermute | solution.py:138
  105.8 23.3 %all-to-all-start = ((bf16[8,352,256]{2,1,0:T(8,128)(2,1)}), bf16[8,352,256]{2,1,0:T(8,128)(2,1)S(1)}, u32[]{:S(2)}, u32[]{:S(2)}) async-start(bf16[8,352,256]{2,1,0:T(8,128)(2,1)} %copy-done.14), calls=%async_computation | async-start | bytes 2883584 | tf_op jit(solution)/shard_map/all_to_all | solution.py:936
  109.5 206.2 %reduce-scatter.5.cloned.1.call-start = ((), (), s32[]{:S(2)}) async-start(), calls=%async_computation.5 | async-start | bytes 1179648 | tf_op jit(solution)/shard_map/reduce_scatter | solution.py:1124
  109.9 20.3 %collective-permute-start.9 = (bf16[24,64,256]{2,1,0:T(8,128)(2,1)}, bf16[24,64,256]{2,1,0:T(8,128)(2,1)}, u32[]{:S(2)}, u32[]{:S(2)}) collective-permute-start(bf16[24,64,256]{2,1,0:T(8,128)(2,1)} %collective-permute-done.6), channel_id=1, source_target_pairs={{1,0},{5,4},{9,8},{13,12},{17,16},{21,20},{25,24},{29,28}} | collective-permute-start | bytes 2359304 | tf_op jit(solution)/shard_map/ppermute | solution.py:138
  150.3 27.3 %collective-permute-start.11 = (bf16[2,2,416,256]{3,2,1,0:T(8,128)(2,1)S(1)}, bf16[2,2,416,256]{3,2,1,0:T(8,128)(2,1)S(1)}, u32[]{:S(2)}, u32[]{:S(2)}) collective-permute-start(bf16[2,2,416,256]{3,2,1,0:T(8,128)(2,1)S(1)} %slice.132), channel_id=1, source_target_pairs={{0,8},{4,12},{8,0},{12,4},{16,24},{20,28},{24,16},{28,20},{1,9},{5... | collective-permute-start | bytes 2555912 | tf_op jit(solution)/shard_map/ppermute | solution.py:32
  151.1 27.7 %collective-permute-start.13 = (bf16[2,2,416,256]{3,2,1,0:T(8,128)(2,1)S(1)}, bf16[2,2,416,256]{3,2,1,0:T(8,128)(2,1)S(1)}, u32[]{:S(2)}, u32[]{:S(2)}) collective-permute-start(bf16[2,2,416,256]{3,2,1,0:T(8,128)(2,1)S(1)} %slice.230), channel_id=1, source_target_pairs={{0,16},{4,20},{8,24},{12,28},{16,0},{20,4},{24,8},{28,12},{1,17},{... | collective-permute-start | bytes 2555912 | tf_op jit(solution)/shard_map/ppermute | solution.py:32
  152.1 22.9 %collective-permute-start.24 = (bf16[256,256]{1,0:T(8,128)(2,1)S(1)}, bf16[256,256]{1,0:T(8,128)(2,1)S(1)}, u32[]{:S(2)}, u32[]{:S(2)}) collective-permute-start(bf16[256,256]{1,0:T(8,128)(2,1)S(1)} %get-tuple-element.104), channel_id=1, source_target_pairs={{0,24},{4,28},{8,16},{12,20},{16,8},{20,12},{24,0},{28,4},{1,25},{... | collective-permute-start | bytes 393224 | tf_op jit(solution)/shard_map/ppermute | solution.py:32
  154.3 23.3 %collective-permute-start.23 = (bf16[256,256]{1,0:T(8,128)(2,1)S(1)}, bf16[256,256]{1,0:T(8,128)(2,1)S(1)}, u32[]{:S(2)}, u32[]{:S(2)}) collective-permute-start(bf16[256,256]{1,0:T(8,128)(2,1)S(1)} %get-tuple-element.104), channel_id=1, source_target_pairs={{0,16},{4,20},{8,24},{12,28},{16,0},{20,4},{24,8},{28,12},{1,17},{... | collective-permute-start | bytes 393224 | tf_op jit(solution)/shard_map/ppermute | solution.py:32
  154.8 22.7 %collective-permute-start.22 = (bf16[256,256]{1,0:T(8,128)(2,1)S(1)}, bf16[256,256]{1,0:T(8,128)(2,1)S(1)}, u32[]{:S(2)}, u32[]{:S(2)}) collective-permute-start(bf16[256,256]{1,0:T(8,128)(2,1)S(1)} %get-tuple-element.104), channel_id=1, source_target_pairs={{0,8},{4,12},{8,0},{12,4},{16,24},{20,28},{24,16},{28,20},{1,9},{5... | collective-permute-start | bytes 393224 | tf_op jit(solution)/shard_map/ppermute | solution.py:32
  177.6 18.0 %collective-permute-start.25 = (bf16[4,256,256]{2,1,0:T(8,128)(2,1)S(1)}, bf16[4,256,256]{2,1,0:T(8,128)(2,1)S(1)}, u32[]{:S(2)}, u32[]{:S(2)}) collective-permute-start(bf16[4,256,256]{2,1,0:T(8,128)(2,1)S(1)} %pad_maximum_fusion.5.near_ref), channel_id=1, source_target_pairs={{0,4},{4,0},{8,12},{12,8},{16,20},{20,16},{24,28},{28,24},{1,5},{5... | collective-permute-start | bytes 1572872 | tf_op jit(solution)/shard_map/ppermute | solution.py:32
  177.9 12.3 %collective-permute-start.12 = (bf16[2,416,256]{2,1,0:T(8,128)(2,1)S(1)}, bf16[2,416,256]{2,1,0:T(8,128)(2,1)S(1)}, u32[]{:S(2)}, u32[]{:S(2)}) collective-permute-start(bf16[2,416,256]{2,1,0:T(8,128)(2,1)S(1)} %get-tuple-element.101), channel_id=1, source_target_pairs={{0,16},{4,20},{8,24},{12,28},{16,0},{20,4},{24,8},{28,12},{1,17},{... | collective-permute-start | bytes 1277960 | tf_op jit(solution)/shard_map/ppermute | solution.py:32
  179.0 12.0 %collective-permute-start.14 = (bf16[2,416,256]{2,1,0:T(8,128)(2,1)S(1)}, bf16[2,416,256]{2,1,0:T(8,128)(2,1)S(1)}, u32[]{:S(2)}, u32[]{:S(2)}) collective-permute-start(bf16[2,416,256]{2,1,0:T(8,128)(2,1)S(1)} %get-tuple-element.99), channel_id=1, source_target_pairs={{0,8},{4,12},{8,0},{12,4},{16,24},{20,28},{24,16},{28,20},{1,9},{5... | collective-permute-start | bytes 1277960 | tf_op jit(solution)/shard_map/ppermute | solution.py:32
  238.4 11.9 %collective-permute-start.47 = (bf16[2,416,256]{2,1,0:T(8,128)(2,1)S(1)}, bf16[2,416,256]{2,1,0:T(8,128)(2,1)S(1)}, u32[]{:S(2)}, u32[]{:S(2)}) collective-permute-start(bf16[2,416,256]{2,1,0:T(8,128)(2,1)S(1)} %get-tuple-element.114), channel_id=1, source_target_pairs={{0,8},{4,12},{8,0},{12,4},{16,24},{20,28},{24,16},{28,20},{1,9},{5... | collective-permute-start | bytes 1277960 | tf_op jit(solution)/shard_map/ppermute | solution.py:32
  238.9 12.9 %collective-permute-start.48 = (bf16[2,416,256]{2,1,0:T(8,128)(2,1)S(1)}, bf16[2,416,256]{2,1,0:T(8,128)(2,1)S(1)}, u32[]{:S(2)}, u32[]{:S(2)}) collective-permute-start(bf16[2,416,256]{2,1,0:T(8,128)(2,1)S(1)} %get-tuple-element.113), channel_id=1, source_target_pairs={{0,16},{4,20},{8,24},{12,28},{16,0},{20,4},{24,8},{28,12},{1,17},{... | collective-permute-start | bytes 1277960 | tf_op jit(solution)/shard_map/ppermute | solution.py:32
  251.3 20.4 %collective-permute-start.49 = (bf16[2,2,416,256]{3,2,1,0:T(8,128)(2,1)}, bf16[2,2,416,256]{3,2,1,0:T(8,128)(2,1)}, u32[]{:S(2)}, u32[]{:S(2)}) collective-permute-start(bf16[2,2,416,256]{3,2,1,0:T(8,128)(2,1)} %pad_maximum_fusion.2), channel_id=1, source_target_pairs={{0,16},{4,20},{8,24},{12,28},{16,0},{20,4},{24,8},{28,12},{1,17},{... | collective-permute-start | bytes 2555912 | tf_op jit(solution)/shard_map/ppermute | solution.py:32
  253.7 20.2 %collective-permute-start.50 = (bf16[2,2,416,256]{3,2,1,0:T(8,128)(2,1)}, bf16[2,2,416,256]{3,2,1,0:T(8,128)(2,1)}, u32[]{:S(2)}, u32[]{:S(2)}) collective-permute-start(bf16[2,2,416,256]{3,2,1,0:T(8,128)(2,1)} %pad_maximum_fusion.3), channel_id=1, source_target_pairs={{0,8},{4,12},{8,0},{12,4},{16,24},{20,28},{24,16},{28,20},{1,9},{5... | collective-permute-start | bytes 2555912 | tf_op jit(solution)/shard_map/ppermute | solution.py:32
  254.7 117.9 %reduce-scatter.3.cloned.1.call-start = ((), (), s32[]{:S(2)}) async-start(), calls=%async_computation.4 | async-start | bytes 3604480 | tf_op jit(solution)/shard_map/reduce_scatter | solution.py:171
  254.8 19.6 %collective-permute-start.51 = (bf16[4,416,256]{2,1,0:T(8,128)(2,1)}, bf16[4,416,256]{2,1,0:T(8,128)(2,1)}, u32[]{:S(2)}, u32[]{:S(2)}) collective-permute-start(bf16[4,416,256]{2,1,0:T(8,128)(2,1)} %copy-done.6), channel_id=1, source_target_pairs={{0,4},{4,0},{8,12},{12,8},{16,20},{20,16},{24,28},{28,24},{1,5},{5... | collective-permute-start | bytes 2555912 | tf_op jit(solution)/shard_map/ppermute | solution.py:32
  311.7 23.3 %all-to-all-start.1 = ((bf16[8,352,256]{2,1,0:T(8,128)(2,1)}), bf16[8,352,256]{2,1,0:T(8,128)(2,1)S(1)}, u32[]{:S(2)}, u32[]{:S(2)}) async-start(bf16[8,352,256]{2,1,0:T(8,128)(2,1)} %features_backward.1), calls=%async_computation.1 | async-start | bytes 2883584 | tf_op jit(solution)/shard_map/all_to_all | solution.py:1142
  339.0 15.7 %collective-permute-start.59 = (f32[144,256]{1,0:T(8,128)S(1)}, f32[144,256]{1,0:T(8,128)S(1)}, u32[]{:S(2)}, u32[]{:S(2)}) collective-permute-start(f32[144,256]{1,0:T(8,128)S(1)} %get-tuple-element.119), channel_id=1, source_target_pairs={{0,1},{1,0},{2,3},{3,2},{4,5},{5,4},{6,7},{7,6},{8,9},{9,8},{10,11... | collective-permute-start | bytes 442376 | tf_op jit(solution)/shard_map/ppermute | solution.py:32
  341.1 22.6 %collective-permute-start.60 = (f32[144,256]{1,0:T(8,128)S(1)}, f32[144,256]{1,0:T(8,128)S(1)}, u32[]{:S(2)}, u32[]{:S(2)}) collective-permute-start(f32[144,256]{1,0:T(8,128)S(1)} %get-tuple-element.118), channel_id=1, source_target_pairs={{0,2},{1,3},{2,0},{3,1},{4,6},{5,7},{6,4},{7,5},{8,10},{9,11},{10,... | collective-permute-start | bytes 442376 | tf_op jit(solution)/shard_map/ppermute | solution.py:32
  349.5 19.8 %collective-permute-start.61 = (f32[144,256]{1,0:T(8,128)S(1)}, f32[144,256]{1,0:T(8,128)S(1)}, u32[]{:S(2)}, u32[]{:S(2)}) collective-permute-start(f32[144,256]{1,0:T(8,128)S(1)} %get-tuple-element.117), channel_id=1, source_target_pairs={{0,3},{1,2},{2,1},{3,0},{4,7},{5,6},{6,5},{7,4},{8,11},{9,10},{10,... | collective-permute-start | bytes 442376 | tf_op jit(solution)/shard_map/ppermute | solution.py:32
  350.0 40.0 %collective-permute-start.56 = (bf16[144,2304]{1,0:T(8,128)(2,1)}, bf16[144,2304]{1,0:T(8,128)(2,1)S(1)}, u32[]{:S(2)}, u32[]{:S(2)}) collective-permute-start(bf16[144,2304]{1,0:T(8,128)(2,1)} %get-tuple-element.87), channel_id=1, source_target_pairs={{0,1},{1,0},{3,2},{4,5},{5,4},{7,6},{8,9},{9,8},{11,10},{12,13},{1... | collective-permute-start | bytes 1990664 | tf_op jit(solution)/shard_map/ppermute | solution.py:32
  353.3 42.8 %collective-permute-start.57 = (bf16[144,2304]{1,0:T(8,128)(2,1)}, bf16[144,2304]{1,0:T(8,128)(2,1)S(1)}, u32[]{:S(2)}, u32[]{:S(2)}) collective-permute-start(bf16[144,2304]{1,0:T(8,128)(2,1)} %get-tuple-element.88), channel_id=1, source_target_pairs={{0,2},{2,0},{3,1},{4,6},{6,4},{7,5},{8,10},{10,8},{11,9},{12,14},{... | collective-permute-start | bytes 1990664 | tf_op jit(solution)/shard_map/ppermute | solution.py:32
  354.6 70.4 %collective-permute-start.58 = (bf16[144,2304]{1,0:T(8,128)(2,1)}, bf16[144,2304]{1,0:T(8,128)(2,1)S(1)}, u32[]{:S(2)}, u32[]{:S(2)}) collective-permute-start(bf16[144,2304]{1,0:T(8,128)(2,1)} %get-tuple-element.89), channel_id=1, source_target_pairs={{1,2},{2,1},{3,0},{5,6},{6,5},{7,4},{9,10},{10,9},{11,8},{13,14},{... | collective-permute-start | bytes 1990664 | tf_op jit(solution)/shard_map/ppermute | solution.py:32
  (75 other events, 946.5 us)
Sparse Core Ops, SparseCore 0:
  254.8 43.9 reduce-scatter.4
  301.2 65.5 reduce-scatter.2

commit v3 on v2

--- a/solution.py
+++ b/solution.py
@@ -43,7 +43,8 @@
 
 
 def plane_parts(array):
-    return [array] + [swap(array, "ha", k) for k in range(1, lax.axis_size("ha"))]
+    pair = array + swap(array, "ha", 1)
+    return [pair] + [swap(pair, "ha", k) for k in range(2, lax.axis_size("ha"), 2)]
 
 
 def plane_sum(array, groups):
@@ -259,15 +260,6 @@
     return ((wanted[:, None] == held[None, :]) & (wanted >= 0)[:, None]).astype(BF16)
 
 
-def mixed_rows(size, micro):
-    tall = ceil_to(size, 16)
-    mixed = np.arange(ceil_to(size * micro, 128))
-    mixed = np.where(mixed < size * micro, mixed, -2)
-    apart = np.arange(ceil_to(micro * tall, 128))
-    real = (apart < micro * tall) & (apart % tall < size)
-    return mixed, np.where(real, apart % tall * micro + apart // tall, -1)
-
-
 def block_rows(count, tall, rows, cols, valid, pitch):
     row = np.arange(count)
     column = row // tall * cols + row % tall % cols
@@ -285,27 +277,27 @@
     rows, cols, micro, channels = features.shape
     out = cotangent.shape[-1]
     size = rows * cols
-    tall, full = ceil_to(size, 16), ceil_to(size * micro, 16)
+    tall = ceil_to(size, 16)
     steps = channels // out
-    mixed, apart = mixed_rows(size, micro)
-    high = mixed.shape[0]
-    spots = spots_of(apart[: micro * tall], mixed).reshape(micro, tall, high)
-    flat = [jnp.pad(a.reshape(size * micro, -1), ((0, full - size * micro), (0, 0))) for a in (features, cotangent)]
-
-    def kernel(z_ref, f_ref, c_ref, spots_ref, *refs):
+
+    def kernel(z_ref, f_ref, c_ref, *refs):
         outs, held_ref = refs[:-1], refs[-1]
-        held_ref[full:] = jnp.zeros((high - full, out), BF16)
+        held_ref[:, size // 8 * 8 :] = jnp.zeros((micro, tall - size // 8 * 8, out), F32)
+
+        def put(ref):
+            values = ref[...]
+            for m in range(micro):
+                held_ref[m, :size] = values[:, m, :].astype(F32)
+            for k in range(micro):
+                outs[k][...] = held_ref[z_ref[0] ^ k].astype(BF16)
 
         @pl.when(pl.program_id(0) < steps)
         def _():
-            held_ref[:full] = f_ref[...]
+            put(f_ref)
 
         @pl.when(pl.program_id(0) == steps)
         def _():
-            held_ref[:full] = c_ref[...]
-
-        for k in range(micro):
-            outs[k][...] = dot(spots_ref[z_ref[0] ^ k], held_ref[...], NN).astype(BF16)
+            put(c_ref)
 
     return pl.pallas_call(
         kernel,
@@ -313,15 +305,14 @@
         out_shape=[jax.ShapeDtypeStruct((tall, channels + out), BF16)] * micro,
         in_specs=[
             SCALAR,
-            pl.BlockSpec((full, out), lambda i: (0, jnp.minimum(i, steps - 1))),
-            pl.BlockSpec((full, out), lambda i: (0, 0)),
-            WHOLE,
+            pl.BlockSpec((size, micro, out), lambda i: (0, 0, jnp.minimum(i, steps - 1))),
+            pl.BlockSpec((size, micro, out), lambda i: (0, 0, 0)),
         ],
         out_specs=[pl.BlockSpec((tall, out), lambda i: (0, i))] * micro,
-        scratch_shapes=[pltpu.VMEM((high, out), BF16)],
+        scratch_shapes=[pltpu.VMEM((micro, tall, out), F32)],
         compiler_params=PARAMS,
         name="extract",
-    )(z.reshape(1), *flat, spots)
+    )(z.reshape(1), features.reshape(size, micro, channels), cotangent.reshape(size, micro, out))
 
 
 def choose(slots, z, blocks, spots, last_spots, lanes):
@@ -415,22 +406,16 @@
     tall, channels = got[0].shape
     channels -= out
     size = rows * cols
-    full = ceil_to(size * micro, 16)
     lanes = 2 * out
-    mixed, apart = mixed_rows(size, micro)
-    high = apart.shape[0]
-    spots = spots_of(mixed[:full], apart)
 
     def kernel(z_ref, *refs):
-        spots_ref, df_ref, act_ref, held_ref = refs[2 * micro], refs[-3], refs[-2], refs[-1]
-        held_ref[micro * tall :] = jnp.zeros((high - micro * tall, lanes), BF16)
+        df_ref, act_ref, held_ref = refs[-3:]
 
         def place(parts, wide):
             for k in range(micro):
-                at = pl.multiple_of((z_ref[0] ^ k) * tall, 16)
                 part = jnp.where(z_ref[0] < blocks, parts[k][...], jnp.zeros((), BF16))
-                held_ref[pl.ds(at, tall), :wide] = part
-            return dot(spots_ref[...], held_ref[:, :wide], NN).astype(BF16)
+                held_ref[z_ref[0] ^ k, :, :wide] = part
+            return jnp.stack([held_ref[m, :, :wide][:size] for m in range(micro)], axis=1)
 
         @pl.when(pl.program_id(0) == 0)
         def _():
@@ -441,18 +426,20 @@
     df, act = pl.pallas_call(
         kernel,
         grid=(channels // lanes,),
-        out_shape=[jax.ShapeDtypeStruct((full, channels), BF16), jax.ShapeDtypeStruct((full, out), BF16)],
+        out_shape=[jax.ShapeDtypeStruct((size, micro, n), BF16) for n in (channels, out)],
         in_specs=[SCALAR]
         + [pl.BlockSpec((tall, lanes), lambda i: (0, i))] * micro
         + [pl.BlockSpec((tall, out), lambda i: (0, channels // out))] * micro
-        + [WHOLE]
         + [pl.BlockSpec(memory_space=pl.ANY)] * len(others),
-        out_specs=[pl.BlockSpec((full, lanes), lambda i: (0, i)), pl.BlockSpec((full, out), lambda i: (0, 0))],
-        scratch_shapes=[pltpu.VMEM((high, lanes), BF16)],
+        out_specs=[
+            pl.BlockSpec((size, micro, lanes), lambda i: (0, 0, i)),
+            pl.BlockSpec((size, micro, out), lambda i: (0, 0, 0)),
+        ],
+        scratch_shapes=[pltpu.VMEM((micro, tall, lanes), BF16)],
         compiler_params=PARAMS,
         name="interleave",
-    )(z.reshape(1), *got, *got, spots, *others)
-    return [a[: size * micro].reshape(rows, cols, micro, -1).transpose(2, 0, 1, 3) for a in (df, act)]
+    )(z.reshape(1), *got, *got, *others)
+    return [a.reshape(rows, cols, micro, -1).transpose(2, 0, 1, 3) for a in (df, act)]
 
 
 def arrange(raw, place, h, valid, prows):
@@ -924,9 +911,8 @@
     if fast:
         slots = extract(features.transpose(1, 2, 0, 3), cotangent.transpose(1, 2, 0, 3), z)
         tall, fit = slots[0].shape[0], ceil_to(valid * rows, 16)
-        early = gather_early(weights, slots[0])
         slots = [slots[0]] + [swap(slots[k], "wa", k, lambda i: i < blocks) for k in range(1, wa)]
-        slots = after(slots, early)
+        early = gather_early(weights, slots[1])
         high, thick = ceil_to(blocks * tall, 128), ceil_to(fit, 128)
         in_piece = block_rows(high, tall, rows, cols, valid, rows)
         in_chunk = block_rows(high, tall, rows, cols, valid, prows)
@@ -949,7 +935,7 @@
         cot = block[:, ha * deep :].reshape(valid, rows, out)
         cot = jnp.pad(cot, ((0, 0), (0, prows - rows), (0, 0))).reshape(valid * prows, out)
     if fast:
-        weights = gather_late(weights, early, send)
+        weights = gather_late(weights, early, *slots)
     if fast:
         proj = order_chunks(*gather_chunks(weights[-1]), h, few)
     else:

time: 448 us -> 437 us (0.975)
  local copies, waits for them, and re-layouts: 35.3 us -> 18.7 us
  waiting for transfers between devices: 220 us -> 225 us
    reshape x4 -> x0, local copies, waits for them, and re-layouts: 9.05 us -> none  [the longest x2 6.19 us: extract(): a.reshape(size * micro, -1)]
    reduce_scatter x1, waiting for transfers between devices: 0.01 us -> 7.47 us  [line_scatter(): lax.psum_scatter(parts, 'wa', scatter_dimension=0, tiled=False).astype(F32)]
    ppermute x7, waiting for transfers between devices: 10.3 us -> 4.55 us  [neighbour(): return lax.ppermute(array, 'wa', pairs)]
    ppermute x55 -> x43, starting transfers between devices: 68.1 us -> 64.2 us  [swap(): return lax.ppermute(array, axis, pairs)]
    unnamed x88 -> x78, local copies, waits for them, and re-layouts: 16 us -> 13 us
    ppermute x55 -> x43, waiting for transfers between devices: 187 us -> 188 us  [swap(): return lax.ppermute(array, axis, pairs)]
  transfers between devices with their start and end apart: 66 -> 54, of which waited for: 29 -> 37; matrix products, arithmetic and copies ran while one was open for 6% -> 4% of each run, Pallas kernels for 9% -> 10%
where the time goes in v3:
time: 437 us; the launch traced here: 431 us
  waiting for transfers between devices  225 us (51%)
  starting transfers between devices  92.8 us (21%)
  Pallas kernels  62.3 us (14%)
  local copies, waits for them, and re-layouts  18.7 us (4%)
  between operations  15.4 us (4%)
  other arithmetic  15.1 us (3%)
    ppermute x43, waiting for transfers between devices, swap(): return lax.ppermute(array, axis, pairs)  188 us
    ppermute x43, starting transfers between devices, swap(): return lax.ppermute(array, axis, pairs)  64.2 us
    ppermute x7, starting transfers between devices, neighbour(): return lax.ppermute(array, 'wa', pairs)  20.9 us
    pallas_call x1, Pallas kernels, features_backward(): pl.pallas_call(kernel, out_shape=jax.ShapeDtypeStruct((ha, fit, deep), BF...  18.3 us
    all_to_all x1, waiting for transfers between devices, local(): back = lax.all_to_all(back, 'ha', 0, 0, tiled=True)  17.4 us
    pallas_call x1, Pallas kernels, weights_backward(): pl.pallas_call(kernel, out_shape=jax.ShapeDtypeStruct(shape, BF16), grid=...  14.3 us
    unnamed x78, local copies, waits for them, and re-layouts  13 us
    pallas_call x1, Pallas kernels, forward_kernel(): pl.pallas_call(kernel, out_shape=[shape] * 2, in_specs=[WHOLE] * len(oper...  9.08 us
  transfers between devices with their start and end apart: 54, of which 37 were waited for; matrix products, arithmetic and copies ran while one was open for 4% of the time, Pallas kernels for 10%

profile of v3, /device:TPU:8, one launch (start us, length us, event | category | flops | bytes accessed | tf_op | source)
XLA Modules:
  0.0 431.5 jit_solution(6352238887847152805)
XLA Ops:
  12.8 3.9 collective-permute-start.3
  19.3 3.2 extract.1
  26.6 5.1 %collective-permute-start.2 = (bf16[144,2304]{1,0:T(8,128)(2,1)S(1)}, bf16[144,2304]{1,0:T(8,128)(2,1)S(1)}, u32[]{:S(2)}, u32[]{:S(2)}) collective-permute-start(bf16[144,2304]{1,0:T(8,128)(2,1)S(1)} %get-tuple-element.52), channel_id=1, source_target_pairs={{0,3},{1,2},{2,1},{4,7},{5,6},{6,5},{8,11},{9,10},{10,9},{12,15},{... | collective-permute-start | bytes 1990664 | tf_op jit(solution)/shard_map/ppermute | solution.py:32
  31.7 26.6 %collective-permute-done.refs_1_ = bf16[144,2304]{1,0:T(8,128)(2,1)S(1)} collective-permute-done((bf16[144,2304]{1,0:T(8,128)(2,1)S(1)}, bf16[144,2304]{1,0:T(8,128)(2,1)S(1)}, u32[]{:S(2)}, u32[]{:S(2)}) %collective-permute-start) | collective-permute-done | bytes 663584 | tf_op jit(solution)/shard_map/ppermute | solution.py:32
  58.3 4.4 %collective-permute-start.8 = (bf16[24,64,256]{2,1,0:T(8,128)(2,1)S(1)}, bf16[24,64,256]{2,1,0:T(8,128)(2,1)}, u32[]{:S(2)}, u32[]{:S(2)}) collective-permute-start(bf16[24,64,256]{2,1,0:T(8,128)(2,1)S(1)} %collective-permute-done.6), channel_id=1, source_target_pairs={{1,0},{2,1},{5,4},{6,5},{9,8},{10,9},{13,12},{14,13},{17,16},{18,1... | collective-permute-start | bytes 2359304 | tf_op jit(solution)/shard_map/ppermute | solution.py:139
  62.7 14.7 %collective-permute-done.1.refs_2_ = bf16[144,2304]{1,0:T(8,128)(2,1)S(1)} collective-permute-done((bf16[144,2304]{1,0:T(8,128)(2,1)S(1)}, bf16[144,2304]{1,0:T(8,128)(2,1)S(1)}, u32[]{:S(2)}, u32[]{:S(2)}) %collective-permute-start.1) | collective-permute-done | bytes 663584 | tf_op jit(solution)/shard_map/ppermute | solution.py:32
  77.4 12.8 %collective-permute-done.2.refs_3_ = bf16[144,2304]{1,0:T(8,128)(2,1)S(1)} collective-permute-done((bf16[144,2304]{1,0:T(8,128)(2,1)S(1)}, bf16[144,2304]{1,0:T(8,128)(2,1)S(1)}, u32[]{:S(2)}, u32[]{:S(2)}) %collective-permute-start.2) | collective-permute-done | bytes 663584 | tf_op jit(solution)/shard_map/ppermute | solution.py:32
  90.1 5.3 %collective-permute-start.4 = (bf16[24,64,256]{2,1,0:T(8,128)(2,1)}, bf16[24,64,256]{2,1,0:T(8,128)(2,1)}, u32[]{:S(2)}, u32[]{:S(2)}) collective-permute-start(bf16[24,64,256]{2,1,0:T(8,128)(2,1)} %collective-permute-done.3), channel_id=1, source_target_pairs={{1,2},{5,6},{9,10},{13,14},{17,18},{21,22},{25,26},{29,30}} | collective-permute-start | bytes 2359304 | tf_op jit(solution)/shard_map/ppermute | solution.py:139
  98.4 3.9 all-to-all-start
  106.4 4.1 collective-permute-done.4
  114.0 7.8 %all-to-all-done.raw_ref = bf16[8,352,256]{2,1,0:T(8,128)(2,1)S(1)} async-done(((bf16[8,352,256]{2,1,0:T(8,128)(2,1)}), bf16[8,352,256]{2,1,0:T(8,128)(2,1)S(1)}, u32[]{:S(2)}, u32[]{:S(2)}) %all-to-all-start) | async-done | bytes 1441824 | tf_op jit(solution)/shard_map/all_to_all | solution.py:922
  126.8 9.1 %forward.1 = (bf16[4,4,416,256]{3,2,1,0:T(8,128)(2,1)S(1)}, bf16[4,4,416,256]{3,2,1,0:T(8,128)(2,1)S(1)}) custom-call(bf16[13,256,256]{2,1,0:T(8,128)(2,1)S(1)} %get-tuple-element.54.x_ref, bf16[24,256,256]{2,1,0:T(8,128)(2,1)S(1)} %pad_maximum_fusion.w_ref, bf16[2,256,256]{2,1,0:T(8,128)(2,1)S(1)} %get-tuple-element.132.refs_0_, ...), custom_call_target="tpu_custom_call" | custom-call | tf_op jit(solution)/shard_map/forward/pallas_call | solution.py:546
  136.0 6.0 %collective-permute-done.10 = bf16[4,4,416,256]{3,2,1,0:T(8,128)(2,1)S(1)} collective-permute-done((bf16[4,4,416,256]{3,2,1,0:T(8,128)(2,1)S(1)}, bf16[4,4,416,256]{3,2,1,0:T(8,128)(2,1)S(1)}, u32[]{:S(2)}, u32[]{:S(2)}) %collective-permute-start.10) | collective-permute-done | bytes 3407904 | tf_op jit(solution)/shard_map/ppermute | solution.py:32
  150.0 18.8 %collective-permute-done.21 = bf16[256,256]{1,0:T(8,128)(2,1)S(1)} collective-permute-done((bf16[256,256]{1,0:T(8,128)(2,1)S(1)}, bf16[256,256]{1,0:T(8,128)(2,1)S(1)}, u32[]{:S(2)}, u32[]{:S(2)}) %collective-permute-start.21) | collective-permute-done | bytes 131104 | tf_op jit(solution)/shard_map/ppermute | solution.py:32
  175.1 9.5 %collective-permute-done.12.low_last = bf16[2,416,256]{2,1,0:T(8,128)(2,1)S(1)} collective-permute-done((bf16[2,416,256]{2,1,0:T(8,128)(2,1)S(1)}, bf16[2,416,256]{2,1,0:T(8,128)(2,1)S(1)}, u32[]{:S(2)}, u32[]{:S(2)}) %collective-permute-start.12) | collective-permute-done | bytes 426016 | tf_op jit(solution)/shard_map/ppermute | solution.py:32
  227.8 9.2 %collective-permute-done.35.refs_4_ = bf16[2,416,256]{2,1,0:T(8,128)(2,1)S(1)} collective-permute-done((bf16[2,416,256]{2,1,0:T(8,128)(2,1)S(1)}, bf16[2,416,256]{2,1,0:T(8,128)(2,1)S(1)}, u32[]{:S(2)}, u32[]{:S(2)}) %collective-permute-start.35) | collective-permute-done | bytes 426016 | tf_op jit(solution)/shard_map/ppermute | solution.py:32
  241.0 15.7 %collective-permute-done.37.refs_6_ = bf16[2,2,416,256]{3,2,1,0:T(8,128)(2,1)} collective-permute-done((bf16[2,2,416,256]{3,2,1,0:T(8,128)(2,1)}, bf16[2,2,416,256]{3,2,1,0:T(8,128)(2,1)}, u32[]{:S(2)}, u32[]{:S(2)}) %collective-permute-start.37) | collective-permute-done | bytes 852000 | tf_op jit(solution)/shard_map/ppermute | solution.py:32
  259.5 2.9 collective-permute-done.40.refs_9_
  263.2 14.3 %weights_backward.1 = bf16[4,22,64,256]{3,2,1,0:T(8,128)(2,1)} custom-call(bf16[13,256,256]{2,1,0:T(8,128)(2,1)} %copy-done.7, bf16[2,256,256]{2,1,0:T(8,128)(2,1)} %copy-done.8, bf16[2,256,256]{2,1,0:T(8,128)(2,1)} %get-tuple-element.133.refs_1_, bf16[2,256,256]{2,1,0:T(8,128)(2,1)} %add_convert_fusion.2.refs_2_, bf16[4,416,256]{2,1,0:T(8,128)(2,1)} %copy-done.6, ...), custom_call_target="tpu_custom_call" | custom-call | tf_op jit(solution)/shard_map/weights_backward/pallas_call | solution.py:618
  278.8 18.3 %features_backward.1 = bf16[8,352,256]{2,1,0:T(8,128)(2,1)} custom-call(s32[1]{0:T(128)} %bitcast.1.h_ref, f32[256,256]{1,0:T(8,128)} %fusion.12.start_ref, bf16[24,256,256]{2,1,0:T(8,128)(2,1)} %copy-done.2, bf16[352,512]{1,0:T(8,128)(2,1)} %constant.110.clone.place_ref, bf16[2,256,256]{2,1,0:T(8,128)(2,1)} %copy-done.8, ...), custom_call_target="tpu_custom_call" | custom-call | tf_op jit(solution)/shard_map/features_backward/pallas_call | solution.py:670
  297.1 3.7 all-to-all-start.1
  303.0 17.4 %all-to-all-done.1.pieces_ref = bf16[8,352,256]{2,1,0:T(8,128)(2,1)S(1)} async-done(((bf16[8,352,256]{2,1,0:T(8,128)(2,1)}), bf16[8,352,256]{2,1,0:T(8,128)(2,1)S(1)}, u32[]{:S(2)}, u32[]{:S(2)}) %all-to-all-start.1) | async-done | bytes 1441824 | tf_op jit(solution)/shard_map/all_to_all | solution.py:1128
  320.4 2.9 unchoose.1
  327.2 13.0 %collective-permute-start.48 = (f32[144,256]{1,0:T(8,128)S(1)}, f32[144,256]{1,0:T(8,128)S(1)}, u32[]{:S(2)}, u32[]{:S(2)}) collective-permute-start(f32[144,256]{1,0:T(8,128)S(1)} %get-tuple-element.110), channel_id=1, source_target_pairs={{0,2},{1,3},{2,0},{3,1},{4,6},{5,7},{6,4},{7,5},{8,10},{9,11},{10,... | collective-permute-start | bytes 442376 | tf_op jit(solution)/shard_map/ppermute | solution.py:32
  340.7 3.4 collective-permute-start.44
  345.4 8.2 %collective-permute-start.46 = (bf16[144,2304]{1,0:T(8,128)(2,1)}, bf16[144,2304]{1,0:T(8,128)(2,1)S(1)}, u32[]{:S(2)}, u32[]{:S(2)}) collective-permute-start(bf16[144,2304]{1,0:T(8,128)(2,1)} %get-tuple-element.81), channel_id=1, source_target_pairs={{1,2},{2,1},{3,0},{5,6},{6,5},{7,4},{9,10},{10,9},{11,8},{13,14},{... | collective-permute-start | bytes 1990664 | tf_op jit(solution)/shard_map/ppermute | solution.py:32
  354.5 7.2 %collective-permute-done.49 = f32[144,256]{1,0:T(8,128)S(1)} collective-permute-done((f32[144,256]{1,0:T(8,128)S(1)}, f32[144,256]{1,0:T(8,128)S(1)}, u32[]{:S(2)}, u32[]{:S(2)}) %collective-permute-start.49) | collective-permute-done | bytes 147488 | tf_op jit(solution)/shard_map/ppermute | solution.py:32
  365.0 7.5 %reduce-scatter.3.cloned.1.call-done = bf16[1,22,64,256]{3,2,1,0:T(8,128)(2,1)} async-done(((bf16[4,22,64,256]{3,2,1,0:T(8,128)(2,1)}), bf16[1,22,64,256]{3,2,1,0:T(8,128)(2,1)}) %reduce-scatter.3.cloned.1.call-update) | async-done | bytes 720912 | tf_op jit(solution)/shard_map/reduce_scatter | solution.py:172
  376.4 6.2 %collective-permute-done.44.refs_1_.refs_5_ = bf16[144,2304]{1,0:T(8,128)(2,1)S(1)} collective-permute-done((bf16[144,2304]{1,0:T(8,128)(2,1)}, bf16[144,2304]{1,0:T(8,128)(2,1)S(1)}, u32[]{:S(2)}, u32[]{:S(2)}) %collective-permute-start.44) | collective-permute-done | bytes 663584 | tf_op jit(solution)/shard_map/ppermute | solution.py:32
  382.6 6.2 %collective-permute-done.45.refs_2_.refs_6_ = bf16[144,2304]{1,0:T(8,128)(2,1)S(1)} collective-permute-done((bf16[144,2304]{1,0:T(8,128)(2,1)}, bf16[144,2304]{1,0:T(8,128)(2,1)S(1)}, u32[]{:S(2)}, u32[]{:S(2)}) %collective-permute-start.45) | collective-permute-done | bytes 663584 | tf_op jit(solution)/shard_map/ppermute | solution.py:32
  388.8 28.9 %collective-permute-done.46.refs_3_.refs_7_ = bf16[144,2304]{1,0:T(8,128)(2,1)S(1)} collective-permute-done((bf16[144,2304]{1,0:T(8,128)(2,1)}, bf16[144,2304]{1,0:T(8,128)(2,1)S(1)}, u32[]{:S(2)}, u32[]{:S(2)}) %collective-permute-start.46) | collective-permute-done | bytes 663584 | tf_op jit(solution)/shard_map/ppermute | solution.py:32
  417.8 6.6 %interleave.1 = (bf16[130,4,2048]{2,1,0:T(4,128)(2,1)}, bf16[130,4,256]{2,1,0:T(4,128)(2,1)}) custom-call(s32[1]{0:T(128)} %bitcast.z_ref, bf16[144,2304]{1,0:T(8,128)(2,1)S(1)} %get-tuple-element.78.refs_0_.refs_4_, bf16[144,2304]{1,0:T(8,128)(2,1)S(1)} %collective-permute-done.44.refs_1_.refs_5_, ...), custom_call_target="tpu_custom_call" | custom-call | tf_op jit(solution)/shard_map/interleave/pallas_call | solution.py:426
  (229 shorter events, 109.5 us)
Async XLA Ops:
  10.7 47.6 %collective-permute-start.6 = (bf16[24,64,256]{2,1,0:T(8,128)(2,1)S(1)}, bf16[24,64,256]{2,1,0:T(8,128)(2,1)S(1)}, u32[]{:S(2)}, u32[]{:S(2)}) collective-permute-start(bf16[24,64,256]{2,1,0:T(8,128)(2,1)S(1)} %pack_weights.1), channel_id=1, source_target_pairs={{1,0},{2,1},{3,2},{5,4},{6,5},{7,6},{9,8},{10,9},{11,10},{13,12},{... | collective-permute-start | bytes 2359304 | tf_op jit(solution)/shard_map/ppermute | solution.py:139
  12.8 77.4 %collective-permute-start.3 = (bf16[24,64,256]{2,1,0:T(8,128)(2,1)S(1)}, bf16[24,64,256]{2,1,0:T(8,128)(2,1)}, u32[]{:S(2)}, u32[]{:S(2)}) collective-permute-start(bf16[24,64,256]{2,1,0:T(8,128)(2,1)S(1)} %pack_weights.1), channel_id=1, source_target_pairs={{0,1},{1,2},{2,3},{4,5},{5,6},{6,7},{8,9},{9,10},{10,11},{12,13},{... | collective-permute-start | bytes 2359304 | tf_op jit(solution)/shard_map/ppermute | solution.py:139
  22.5 35.8 %collective-permute-start = (bf16[144,2304]{1,0:T(8,128)(2,1)S(1)}, bf16[144,2304]{1,0:T(8,128)(2,1)S(1)}, u32[]{:S(2)}, u32[]{:S(2)}) collective-permute-start(bf16[144,2304]{1,0:T(8,128)(2,1)S(1)} %get-tuple-element.50), channel_id=1, source_target_pairs={{0,1},{1,0},{2,3},{4,5},{5,4},{6,7},{8,9},{9,8},{10,11},{12,13},{1... | collective-permute-start | bytes 1990664 | tf_op jit(solution)/shard_map/ppermute | solution.py:32
  25.2 52.1 %collective-permute-start.1 = (bf16[144,2304]{1,0:T(8,128)(2,1)S(1)}, bf16[144,2304]{1,0:T(8,128)(2,1)S(1)}, u32[]{:S(2)}, u32[]{:S(2)}) collective-permute-start(bf16[144,2304]{1,0:T(8,128)(2,1)S(1)} %get-tuple-element.51), channel_id=1, source_target_pairs={{0,2},{1,3},{2,0},{4,6},{5,7},{6,4},{8,10},{9,11},{10,8},{12,14},{... | collective-permute-start | bytes 1990664 | tf_op jit(solution)/shard_map/ppermute | solution.py:32
  26.6 63.5 %collective-permute-start.2 = (bf16[144,2304]{1,0:T(8,128)(2,1)S(1)}, bf16[144,2304]{1,0:T(8,128)(2,1)S(1)}, u32[]{:S(2)}, u32[]{:S(2)}) collective-permute-start(bf16[144,2304]{1,0:T(8,128)(2,1)S(1)} %get-tuple-element.52), channel_id=1, source_target_pairs={{0,3},{1,2},{2,1},{4,7},{5,6},{6,5},{8,11},{9,10},{10,9},{12,15},{... | collective-permute-start | bytes 1990664 | tf_op jit(solution)/shard_map/ppermute | solution.py:32
  58.3 45.9 %collective-permute-start.8 = (bf16[24,64,256]{2,1,0:T(8,128)(2,1)S(1)}, bf16[24,64,256]{2,1,0:T(8,128)(2,1)}, u32[]{:S(2)}, u32[]{:S(2)}) collective-permute-start(bf16[24,64,256]{2,1,0:T(8,128)(2,1)S(1)} %collective-permute-done.6), channel_id=1, source_target_pairs={{1,0},{2,1},{5,4},{6,5},{9,8},{10,9},{13,12},{14,13},{17,16},{18,1... | collective-permute-start | bytes 2359304 | tf_op jit(solution)/shard_map/ppermute | solution.py:139
  90.1 20.3 %collective-permute-start.4 = (bf16[24,64,256]{2,1,0:T(8,128)(2,1)}, bf16[24,64,256]{2,1,0:T(8,128)(2,1)}, u32[]{:S(2)}, u32[]{:S(2)}) collective-permute-start(bf16[24,64,256]{2,1,0:T(8,128)(2,1)} %collective-permute-done.3), channel_id=1, source_target_pairs={{1,2},{5,6},{9,10},{13,14},{17,18},{21,22},{25,26},{29,30}} | collective-permute-start | bytes 2359304 | tf_op jit(solution)/shard_map/ppermute | solution.py:139
  98.4 23.5 %all-to-all-start = ((bf16[8,352,256]{2,1,0:T(8,128)(2,1)}), bf16[8,352,256]{2,1,0:T(8,128)(2,1)S(1)}, u32[]{:S(2)}, u32[]{:S(2)}) async-start(bf16[8,352,256]{2,1,0:T(8,128)(2,1)} %copy-done.12), calls=%async_computation | async-start | bytes 2883584 | tf_op jit(solution)/shard_map/all_to_all | solution.py:922
  102.2 198.8 %reduce-scatter.5.cloned.1.call-start = ((), (), s32[]{:S(2)}) async-start(), calls=%async_computation.5 | async-start | bytes 1179648 | tf_op jit(solution)/shard_map/reduce_scatter | solution.py:1110
  102.6 20.3 %collective-permute-start.7 = (bf16[24,64,256]{2,1,0:T(8,128)(2,1)}, bf16[24,64,256]{2,1,0:T(8,128)(2,1)}, u32[]{:S(2)}, u32[]{:S(2)}) collective-permute-start(bf16[24,64,256]{2,1,0:T(8,128)(2,1)} %collective-permute-done.3), channel_id=1, source_target_pairs={{2,3},{6,7},{10,11},{14,15},{18,19},{22,23},{26,27},{30,31}} | collective-permute-start | bytes 2359304 | tf_op jit(solution)/shard_map/ppermute | solution.py:139
  104.2 19.2 %collective-permute-start.9 = (bf16[24,64,256]{2,1,0:T(8,128)(2,1)}, bf16[24,64,256]{2,1,0:T(8,128)(2,1)}, u32[]{:S(2)}, u32[]{:S(2)}) collective-permute-start(bf16[24,64,256]{2,1,0:T(8,128)(2,1)} %collective-permute-done.8), channel_id=1, source_target_pairs={{1,0},{5,4},{9,8},{13,12},{17,16},{21,20},{25,24},{29,28}} | collective-permute-start | bytes 2359304 | tf_op jit(solution)/shard_map/ppermute | solution.py:139
  110.4 13.0 %collective-permute-start.5 = (bf16[24,64,256]{2,1,0:T(8,128)(2,1)}, bf16[24,64,256]{2,1,0:T(8,128)(2,1)}, u32[]{:S(2)}, u32[]{:S(2)}) collective-permute-start(bf16[24,64,256]{2,1,0:T(8,128)(2,1)} %collective-permute-done.4), channel_id=1, source_target_pairs={{2,3},{6,7},{10,11},{14,15},{18,19},{22,23},{26,27},{30,31}} | collective-permute-start | bytes 2359304 | tf_op jit(solution)/shard_map/ppermute | solution.py:139
  143.0 29.1 %collective-permute-start.11 = (bf16[2,2,416,256]{3,2,1,0:T(8,128)(2,1)S(1)}, bf16[2,2,416,256]{3,2,1,0:T(8,128)(2,1)S(1)}, u32[]{:S(2)}, u32[]{:S(2)}) collective-permute-start(bf16[2,2,416,256]{3,2,1,0:T(8,128)(2,1)S(1)} %slice.126), channel_id=1, source_target_pairs={{0,8},{4,12},{8,0},{12,4},{16,24},{20,28},{24,16},{28,20},{1,9},{5... | collective-permute-start | bytes 2555912 | tf_op jit(solution)/shard_map/ppermute | solution.py:32
  144.9 29.0 %collective-permute-start.13 = (bf16[2,2,416,256]{3,2,1,0:T(8,128)(2,1)S(1)}, bf16[2,2,416,256]{3,2,1,0:T(8,128)(2,1)S(1)}, u32[]{:S(2)}, u32[]{:S(2)}) collective-permute-start(bf16[2,2,416,256]{3,2,1,0:T(8,128)(2,1)S(1)} %slice.222), channel_id=1, source_target_pairs={{0,16},{4,20},{8,24},{12,28},{16,0},{20,4},{24,8},{28,12},{1,17},{... | collective-permute-start | bytes 2555912 | tf_op jit(solution)/shard_map/ppermute | solution.py:32
  146.4 22.3 %collective-permute-start.21 = (bf16[256,256]{1,0:T(8,128)(2,1)S(1)}, bf16[256,256]{1,0:T(8,128)(2,1)S(1)}, u32[]{:S(2)}, u32[]{:S(2)}) collective-permute-start(bf16[256,256]{1,0:T(8,128)(2,1)S(1)} %get-tuple-element.96), channel_id=1, source_target_pairs={{0,24},{4,28},{8,16},{12,20},{16,8},{20,12},{24,0},{28,4},{1,25},{... | collective-permute-start | bytes 393224 | tf_op jit(solution)/shard_map/ppermute | solution.py:32
  146.9 24.3 %collective-permute-start.20 = (bf16[256,256]{1,0:T(8,128)(2,1)S(1)}, bf16[256,256]{1,0:T(8,128)(2,1)S(1)}, u32[]{:S(2)}, u32[]{:S(2)}) collective-permute-start(bf16[256,256]{1,0:T(8,128)(2,1)S(1)} %get-tuple-element.96), channel_id=1, source_target_pairs={{0,16},{4,20},{8,24},{12,28},{16,0},{20,4},{24,8},{28,12},{1,17},{... | collective-permute-start | bytes 393224 | tf_op jit(solution)/shard_map/ppermute | solution.py:32
  148.5 22.8 %collective-permute-start.19 = (bf16[256,256]{1,0:T(8,128)(2,1)S(1)}, bf16[256,256]{1,0:T(8,128)(2,1)S(1)}, u32[]{:S(2)}, u32[]{:S(2)}) collective-permute-start(bf16[256,256]{1,0:T(8,128)(2,1)S(1)} %get-tuple-element.96), channel_id=1, source_target_pairs={{0,8},{4,12},{8,0},{12,4},{16,24},{20,28},{24,16},{28,20},{1,9},{5... | collective-permute-start | bytes 393224 | tf_op jit(solution)/shard_map/ppermute | solution.py:32
  172.1 20.4 %collective-permute-start.22 = (bf16[4,256,256]{2,1,0:T(8,128)(2,1)}, bf16[4,256,256]{2,1,0:T(8,128)(2,1)}, u32[]{:S(2)}, u32[]{:S(2)}) collective-permute-start(bf16[4,256,256]{2,1,0:T(8,128)(2,1)} %pad_maximum_fusion.5.near_ref), channel_id=1, source_target_pairs={{0,4},{4,0},{8,12},{12,8},{16,20},{20,16},{24,28},{28,24},{1,5},{5... | collective-permute-start | bytes 1572872 | tf_op jit(solution)/shard_map/ppermute | solution.py:32
  172.3 12.3 %collective-permute-start.12 = (bf16[2,416,256]{2,1,0:T(8,128)(2,1)S(1)}, bf16[2,416,256]{2,1,0:T(8,128)(2,1)S(1)}, u32[]{:S(2)}, u32[]{:S(2)}) collective-permute-start(bf16[2,416,256]{2,1,0:T(8,128)(2,1)S(1)} %get-tuple-element.93), channel_id=1, source_target_pairs={{0,16},{4,20},{8,24},{12,28},{16,0},{20,4},{24,8},{28,12},{1,17},{... | collective-permute-start | bytes 1277960 | tf_op jit(solution)/shard_map/ppermute | solution.py:32
  174.0 12.0 %collective-permute-start.14 = (bf16[2,416,256]{2,1,0:T(8,128)(2,1)S(1)}, bf16[2,416,256]{2,1,0:T(8,128)(2,1)S(1)}, u32[]{:S(2)}, u32[]{:S(2)}) collective-permute-start(bf16[2,416,256]{2,1,0:T(8,128)(2,1)S(1)} %get-tuple-element.91), channel_id=1, source_target_pairs={{0,8},{4,12},{8,0},{12,4},{16,24},{20,28},{24,16},{28,20},{1,9},{5... | collective-permute-start | bytes 1277960 | tf_op jit(solution)/shard_map/ppermute | solution.py:32
  227.4 11.3 %collective-permute-start.36 = (bf16[2,416,256]{2,1,0:T(8,128)(2,1)S(1)}, bf16[2,416,256]{2,1,0:T(8,128)(2,1)S(1)}, u32[]{:S(2)}, u32[]{:S(2)}) collective-permute-start(bf16[2,416,256]{2,1,0:T(8,128)(2,1)S(1)} %get-tuple-element.105), channel_id=1, source_target_pairs={{0,16},{4,20},{8,24},{12,28},{16,0},{20,4},{24,8},{28,12},{1,17},{... | collective-permute-start | bytes 1277960 | tf_op jit(solution)/shard_map/ppermute | solution.py:32
  238.0 18.7 %collective-permute-start.37 = (bf16[2,2,416,256]{3,2,1,0:T(8,128)(2,1)}, bf16[2,2,416,256]{3,2,1,0:T(8,128)(2,1)}, u32[]{:S(2)}, u32[]{:S(2)}) collective-permute-start(bf16[2,2,416,256]{3,2,1,0:T(8,128)(2,1)} %pad_maximum_fusion.2), channel_id=1, source_target_pairs={{0,16},{4,20},{8,24},{12,28},{16,0},{20,4},{24,8},{28,12},{1,17},{... | collective-permute-start | bytes 2555912 | tf_op jit(solution)/shard_map/ppermute | solution.py:32
  240.5 18.5 %collective-permute-start.38 = (bf16[2,2,416,256]{3,2,1,0:T(8,128)(2,1)}, bf16[2,2,416,256]{3,2,1,0:T(8,128)(2,1)}, u32[]{:S(2)}, u32[]{:S(2)}) collective-permute-start(bf16[2,2,416,256]{3,2,1,0:T(8,128)(2,1)} %pad_maximum_fusion.3), channel_id=1, source_target_pairs={{0,8},{4,12},{8,0},{12,4},{16,24},{20,28},{24,16},{28,20},{1,9},{5... | collective-permute-start | bytes 2555912 | tf_op jit(solution)/shard_map/ppermute | solution.py:32
  240.9 131.6 %reduce-scatter.3.cloned.1.call-start = ((), (), s32[]{:S(2)}) async-start(), calls=%async_computation.4 | async-start | bytes 3604480 | tf_op jit(solution)/shard_map/reduce_scatter | solution.py:172
  240.9 18.6 %collective-permute-start.39 = (bf16[4,416,256]{2,1,0:T(8,128)(2,1)}, bf16[4,416,256]{2,1,0:T(8,128)(2,1)}, u32[]{:S(2)}, u32[]{:S(2)}) collective-permute-start(bf16[4,416,256]{2,1,0:T(8,128)(2,1)} %copy-done.6), channel_id=1, source_target_pairs={{0,4},{4,0},{8,12},{12,8},{16,20},{20,16},{24,28},{28,24},{1,5},{5... | collective-permute-start | bytes 2555912 | tf_op jit(solution)/shard_map/ppermute | solution.py:32
  297.1 23.3 %all-to-all-start.1 = ((bf16[8,352,256]{2,1,0:T(8,128)(2,1)}), bf16[8,352,256]{2,1,0:T(8,128)(2,1)S(1)}, u32[]{:S(2)}, u32[]{:S(2)}) async-start(bf16[8,352,256]{2,1,0:T(8,128)(2,1)} %features_backward.1), calls=%async_computation.1 | async-start | bytes 2883584 | tf_op jit(solution)/shard_map/all_to_all | solution.py:1128
  324.4 21.0 %collective-permute-start.47 = (f32[144,256]{1,0:T(8,128)S(1)}, f32[144,256]{1,0:T(8,128)S(1)}, u32[]{:S(2)}, u32[]{:S(2)}) collective-permute-start(f32[144,256]{1,0:T(8,128)S(1)} %get-tuple-element.111), channel_id=1, source_target_pairs={{0,1},{1,0},{2,3},{3,2},{4,5},{5,4},{6,7},{7,6},{8,9},{9,8},{10,11... | collective-permute-start | bytes 442376 | tf_op jit(solution)/shard_map/ppermute | solution.py:32
  327.2 27.3 %collective-permute-start.48 = (f32[144,256]{1,0:T(8,128)S(1)}, f32[144,256]{1,0:T(8,128)S(1)}, u32[]{:S(2)}, u32[]{:S(2)}) collective-permute-start(f32[144,256]{1,0:T(8,128)S(1)} %get-tuple-element.110), channel_id=1, source_target_pairs={{0,2},{1,3},{2,0},{3,1},{4,6},{5,7},{6,4},{7,5},{8,10},{9,11},{10,... | collective-permute-start | bytes 442376 | tf_op jit(solution)/shard_map/ppermute | solution.py:32
  340.2 21.4 %collective-permute-start.49 = (f32[144,256]{1,0:T(8,128)S(1)}, f32[144,256]{1,0:T(8,128)S(1)}, u32[]{:S(2)}, u32[]{:S(2)}) collective-permute-start(f32[144,256]{1,0:T(8,128)S(1)} %get-tuple-element.109), channel_id=1, source_target_pairs={{0,3},{1,2},{2,1},{3,0},{4,7},{5,6},{6,5},{7,4},{8,11},{9,10},{10,... | collective-permute-start | bytes 442376 | tf_op jit(solution)/shard_map/ppermute | solution.py:32
  340.7 41.9 %collective-permute-start.44 = (bf16[144,2304]{1,0:T(8,128)(2,1)}, bf16[144,2304]{1,0:T(8,128)(2,1)S(1)}, u32[]{:S(2)}, u32[]{:S(2)}) collective-permute-start(bf16[144,2304]{1,0:T(8,128)(2,1)} %get-tuple-element.79), channel_id=1, source_target_pairs={{0,1},{1,0},{3,2},{4,5},{5,4},{7,6},{8,9},{9,8},{11,10},{12,13},{1... | collective-permute-start | bytes 1990664 | tf_op jit(solution)/shard_map/ppermute | solution.py:32
  344.1 44.7 %collective-permute-start.45 = (bf16[144,2304]{1,0:T(8,128)(2,1)}, bf16[144,2304]{1,0:T(8,128)(2,1)S(1)}, u32[]{:S(2)}, u32[]{:S(2)}) collective-permute-start(bf16[144,2304]{1,0:T(8,128)(2,1)} %get-tuple-element.80), channel_id=1, source_target_pairs={{0,2},{2,0},{3,1},{4,6},{6,4},{7,5},{8,10},{10,8},{11,9},{12,14},{... | collective-permute-start | bytes 1990664 | tf_op jit(solution)/shard_map/ppermute | solution.py:32
  345.4 72.4 %collective-permute-start.46 = (bf16[144,2304]{1,0:T(8,128)(2,1)}, bf16[144,2304]{1,0:T(8,128)(2,1)S(1)}, u32[]{:S(2)}, u32[]{:S(2)}) collective-permute-start(bf16[144,2304]{1,0:T(8,128)(2,1)} %get-tuple-element.81), channel_id=1, source_target_pairs={{1,2},{2,1},{3,0},{5,6},{6,5},{7,4},{9,10},{10,9},{11,8},{13,14},{... | collective-permute-start | bytes 1990664 | tf_op jit(solution)/shard_map/ppermute | solution.py:32
  (58 other events, 837.7 us)
Sparse Core Ops, SparseCore 0:
  241.0 50.5 reduce-scatter.4
  293.9 78.5 reduce-scatter.2

commit v4 on v3

--- a/solution.py
+++ b/solution.py
@@ -277,17 +277,15 @@
     rows, cols, micro, channels = features.shape
     out = cotangent.shape[-1]
     size = rows * cols
-    tall = ceil_to(size, 16)
     steps = channels // out
 
     def kernel(z_ref, f_ref, c_ref, *refs):
         outs, held_ref = refs[:-1], refs[-1]
-        held_ref[:, size // 8 * 8 :] = jnp.zeros((micro, tall - size // 8 * 8, out), F32)
 
         def put(ref):
             values = ref[...]
             for m in range(micro):
-                held_ref[m, :size] = values[:, m, :].astype(F32)
+                held_ref[m] = values[:, m, :].astype(F32)
             for k in range(micro):
                 outs[k][...] = held_ref[z_ref[0] ^ k].astype(BF16)
 
@@ -302,34 +300,35 @@
     return pl.pallas_call(
         kernel,
         grid=(steps + 1,),
-        out_shape=[jax.ShapeDtypeStruct((tall, channels + out), BF16)] * micro,
+        out_shape=[jax.ShapeDtypeStruct((size, channels + out), BF16)] * micro,
         in_specs=[
             SCALAR,
             pl.BlockSpec((size, micro, out), lambda i: (0, 0, jnp.minimum(i, steps - 1))),
             pl.BlockSpec((size, micro, out), lambda i: (0, 0, 0)),
         ],
-        out_specs=[pl.BlockSpec((tall, out), lambda i: (0, i))] * micro,
-        scratch_shapes=[pltpu.VMEM((micro, tall, out), F32)],
+        out_specs=[pl.BlockSpec((size, out), lambda i: (0, i))] * micro,
+        scratch_shapes=[pltpu.VMEM((micro, size, out), F32)],
         compiler_params=PARAMS,
         name="extract",
     )(z.reshape(1), features.reshape(size, micro, channels), cotangent.reshape(size, micro, out))
 
 
 def choose(slots, z, blocks, spots, last_spots, lanes):
-    tall, wide = slots[0].shape
+    size, wide = slots[0].shape
+    tall = ceil_to(size, 16)
     high = spots.shape[1]
     count = wide // lanes - 1
 
     def kernel(z_ref, *refs):
         spots_ref, last_ref, send_ref, own_ref, held_ref = refs[len(slots) :]
+        held_ref[...] = jnp.zeros((high, wide), BF16)
         for v in range(len(slots)):
 
             @pl.when(z_ref[0] == v)
             def _():
                 for j in range(blocks):
-                    held_ref[j * tall : (j + 1) * tall] = refs[v ^ j][...]
-
-        held_ref[blocks * tall :] = jnp.zeros((high - blocks * tall, wide), BF16)
+                    held_ref[j * tall : j * tall + size] = refs[v ^ j][...]
+
         for d in range(count):
             part = held_ref[:, d * lanes : (d + 1) * lanes]
             send_ref[d] = dot(spots_ref[...], part, NN).astype(BF16)
@@ -349,7 +348,7 @@
     )(z.reshape(1), *slots, spots, last_spots)
 
 
-def unchoose(pieces, last, z, blocks, spots, last_spots):
+def unchoose(pieces, last, z, blocks, size, spots, last_spots):
     ha, fit, out = pieces.shape
     planes, tall, thick = spots.shape
     wide = (ha + 1) * out
@@ -365,14 +364,16 @@
             def _():
                 for j in range(planes):
                     if j < blocks:
-                        outs[v ^ j][:, : ha * out] = dot(spots_ref[j], held_ref[...], NN).astype(BF16)
-                        outs[v ^ j][:, ha * out :] = dot(last_spots_ref[j], last_ref[...], NN).astype(BF16)
+                        block = dot(spots_ref[j], held_ref[...], NN).astype(BF16)
+                        outs[v ^ j][:, : ha * out] = block[:size]
+                        block = dot(last_spots_ref[j], last_ref[...], NN).astype(BF16)
+                        outs[v ^ j][:, ha * out :] = block[:size]
                     else:
-                        outs[v ^ j][...] = jnp.zeros((tall, wide), BF16)
+                        outs[v ^ j][...] = jnp.zeros((size, wide), BF16)
 
     return pl.pallas_call(
         kernel,
-        out_shape=[jax.ShapeDtypeStruct((tall, wide), BF16)] * planes,
+        out_shape=[jax.ShapeDtypeStruct((size, wide), BF16)] * planes,
         in_specs=[SCALAR] + [WHOLE] * 4,
         out_specs=[WHOLE] * planes,
         scratch_shapes=[pltpu.VMEM((thick, ha * out), BF16)],
@@ -403,9 +404,8 @@
 
 def interleave(got, z, blocks, rows, cols, out, others):
     micro = len(got)
-    tall, channels = got[0].shape
+    size, channels = got[0].shape
     channels -= out
-    size = rows * cols
     lanes = 2 * out
 
     def kernel(z_ref, *refs):
@@ -415,7 +415,7 @@
             for k in range(micro):
                 part = jnp.where(z_ref[0] < blocks, parts[k][...], jnp.zeros((), BF16))
                 held_ref[z_ref[0] ^ k, :, :wide] = part
-            return jnp.stack([held_ref[m, :, :wide][:size] for m in range(micro)], axis=1)
+            return jnp.stack([held_ref[m, :, :wide] for m in range(micro)], axis=1)
 
         @pl.when(pl.program_id(0) == 0)
         def _():
@@ -428,14 +428,14 @@
         grid=(channels // lanes,),
         out_shape=[jax.ShapeDtypeStruct((size, micro, n), BF16) for n in (channels, out)],
         in_specs=[SCALAR]
-        + [pl.BlockSpec((tall, lanes), lambda i: (0, i))] * micro
-        + [pl.BlockSpec((tall, out), lambda i: (0, channels // out))] * micro
+        + [pl.BlockSpec((size, lanes), lambda i: (0, i))] * micro
+        + [pl.BlockSpec((size, out), lambda i: (0, channels // out))] * micro
         + [pl.BlockSpec(memory_space=pl.ANY)] * len(others),
         out_specs=[
             pl.BlockSpec((size, micro, lanes), lambda i: (0, 0, i)),
             pl.BlockSpec((size, micro, out), lambda i: (0, 0, 0)),
         ],
-        scratch_shapes=[pltpu.VMEM((micro, tall, lanes), BF16)],
+        scratch_shapes=[pltpu.VMEM((micro, size, lanes), BF16)],
         compiler_params=PARAMS,
         name="interleave",
     )(z.reshape(1), *got, *got, *others)
@@ -910,7 +910,7 @@
 
     if fast:
         slots = extract(features.transpose(1, 2, 0, 3), cotangent.transpose(1, 2, 0, 3), z)
-        tall, fit = slots[0].shape[0], ceil_to(valid * rows, 16)
+        tall, fit = ceil_to(size, 16), ceil_to(valid * rows, 16)
         slots = [slots[0]] + [swap(slots[k], "wa", k, lambda i: i < blocks) for k in range(1, wa)]
         early = gather_early(weights, slots[1])
         high, thick = ceil_to(blocks * tall, 128), ceil_to(fit, 128)
@@ -1134,7 +1134,7 @@
         piece_spots = spots_of(block_rows(wa * tall, tall, rows, cols, valid, rows), np.arange(thick))
         chunk_spots = spots_of(block_rows(wa * tall, tall, rows, cols, valid, prows), np.arange(valid * prows))
         got = unchoose(
-            back, activation, z, blocks, piece_spots.reshape(wa, tall, thick), chunk_spots.reshape(wa, tall, -1)
+            back, activation, z, blocks, size, piece_spots.reshape(wa, tall, thick), chunk_spots.reshape(wa, tall, -1)
         )
         got = [got[0]] + [swap(got[k], "wa", k, partial(home, k=k)) for k in range(1, wa)]
         df, acts = interleave(got, z, blocks, rows, cols, out, [atrous])

time: 437 us -> 431 us (0.986)
  waiting for transfers between devices: 225 us -> 219 us
    ppermute x43, waiting for transfers between devices: 188 us -> 182 us  [swap(): return lax.ppermute(array, axis, pairs)]
where the time goes in v4:
time: 431 us; the launch traced here: 425 us
  waiting for transfers between devices  219 us (51%)
  starting transfers between devices  92.8 us (22%)
  Pallas kernels  62.3 us (14%)
  local copies, waits for them, and re-layouts  18.7 us (4%)
  between operations  15.4 us (4%)
  other arithmetic  15.1 us (4%)
    ppermute x43, waiting for transfers between devices, swap(): return lax.ppermute(array, axis, pairs)  182 us
    ppermute x43, starting transfers between devices, swap(): return lax.ppermute(array, axis, pairs)  64.2 us
    ppermute x7, starting transfers between devices, neighbour(): return lax.ppermute(array, 'wa', pairs)  21.1 us
    pallas_call x1, Pallas kernels, features_backward(): pl.pallas_call(kernel, out_shape=jax.ShapeDtypeStruct((ha, fit, deep), BF...  18.3 us
    all_to_all x1, waiting for transfers between devices, local(): back = lax.all_to_all(back, 'ha', 0, 0, tiled=True)  17.4 us
    pallas_call x1, Pallas kernels, weights_backward(): pl.pallas_call(kernel, out_shape=jax.ShapeDtypeStruct(shape, BF16), grid=...  14.3 us
    unnamed x78, local copies, waits for them, and re-layouts  13 us
    pallas_call x1, Pallas kernels, forward_kernel(): pl.pallas_call(kernel, out_shape=[shape] * 2, in_specs=[WHOLE] * len(oper...  9.08 us
  transfers between devices with their start and end apart: 54, of which 37 were waited for; matrix products, arithmetic and copies ran while one was open for 4% of the time, Pallas kernels for 10%

profile of v4, /device:TPU:8, one launch (start us, length us, event | category | flops | bytes accessed | tf_op | source)
XLA Modules:
  0.0 425.3 jit_solution(10633210636183981439)
XLA Ops:
  12.8 3.9 collective-permute-start.3
  19.3 3.2 extract.1
  26.6 5.1 %collective-permute-start.2 = (bf16[130,2304]{1,0:T(8,128)(2,1)S(1)}, bf16[130,2304]{1,0:T(8,128)(2,1)S(1)}, u32[]{:S(2)}, u32[]{:S(2)}) collective-permute-start(bf16[130,2304]{1,0:T(8,128)(2,1)S(1)} %get-tuple-element.52), channel_id=1, source_target_pairs={{0,3},{1,2},{2,1},{4,7},{5,6},{6,5},{8,11},{9,10},{10,9},{12,15},{... | collective-permute-start | bytes 1797128 | tf_op jit(solution)/shard_map/ppermute | solution.py:32
  31.7 25.0 %collective-permute-done.refs_1_ = bf16[130,2304]{1,0:T(8,128)(2,1)S(1)} collective-permute-done((bf16[130,2304]{1,0:T(8,128)(2,1)S(1)}, bf16[130,2304]{1,0:T(8,128)(2,1)S(1)}, u32[]{:S(2)}, u32[]{:S(2)}) %collective-permute-start) | collective-permute-done | bytes 599072 | tf_op jit(solution)/shard_map/ppermute | solution.py:32
  56.7 4.4 %collective-permute-start.8 = (bf16[24,64,256]{2,1,0:T(8,128)(2,1)S(1)}, bf16[24,64,256]{2,1,0:T(8,128)(2,1)}, u32[]{:S(2)}, u32[]{:S(2)}) collective-permute-start(bf16[24,64,256]{2,1,0:T(8,128)(2,1)S(1)} %collective-permute-done.6), channel_id=1, source_target_pairs={{1,0},{2,1},{5,4},{6,5},{9,8},{10,9},{13,12},{14,13},{17,16},{18,1... | collective-permute-start | bytes 2359304 | tf_op jit(solution)/shard_map/ppermute | solution.py:139
  61.1 13.9 %collective-permute-done.1.refs_2_ = bf16[130,2304]{1,0:T(8,128)(2,1)S(1)} collective-permute-done((bf16[130,2304]{1,0:T(8,128)(2,1)S(1)}, bf16[130,2304]{1,0:T(8,128)(2,1)S(1)}, u32[]{:S(2)}, u32[]{:S(2)}) %collective-permute-start.1) | collective-permute-done | bytes 599072 | tf_op jit(solution)/shard_map/ppermute | solution.py:32
  75.0 12.0 %collective-permute-done.2.refs_3_ = bf16[130,2304]{1,0:T(8,128)(2,1)S(1)} collective-permute-done((bf16[130,2304]{1,0:T(8,128)(2,1)S(1)}, bf16[130,2304]{1,0:T(8,128)(2,1)S(1)}, u32[]{:S(2)}, u32[]{:S(2)}) %collective-permute-start.2) | collective-permute-done | bytes 599072 | tf_op jit(solution)/shard_map/ppermute | solution.py:32
  87.0 5.4 %collective-permute-start.4 = (bf16[24,64,256]{2,1,0:T(8,128)(2,1)}, bf16[24,64,256]{2,1,0:T(8,128)(2,1)}, u32[]{:S(2)}, u32[]{:S(2)}) collective-permute-start(bf16[24,64,256]{2,1,0:T(8,128)(2,1)} %collective-permute-done.3), channel_id=1, source_target_pairs={{1,2},{5,6},{9,10},{13,14},{17,18},{21,22},{25,26},{29,30}} | collective-permute-start | bytes 2359304 | tf_op jit(solution)/shard_map/ppermute | solution.py:139
  95.5 3.7 all-to-all-start
  103.3 4.0 collective-permute-done.4
  111.0 7.8 %all-to-all-done.raw_ref = bf16[8,352,256]{2,1,0:T(8,128)(2,1)S(1)} async-done(((bf16[8,352,256]{2,1,0:T(8,128)(2,1)}), bf16[8,352,256]{2,1,0:T(8,128)(2,1)S(1)}, u32[]{:S(2)}, u32[]{:S(2)}) %all-to-all-start) | async-done | bytes 1441824 | tf_op jit(solution)/shard_map/all_to_all | solution.py:922
  123.8 9.1 %forward.1 = (bf16[4,4,416,256]{3,2,1,0:T(8,128)(2,1)S(1)}, bf16[4,4,416,256]{3,2,1,0:T(8,128)(2,1)S(1)}) custom-call(bf16[13,256,256]{2,1,0:T(8,128)(2,1)S(1)} %get-tuple-element.54.x_ref, bf16[24,256,256]{2,1,0:T(8,128)(2,1)S(1)} %pad_maximum_fusion.w_ref, bf16[2,256,256]{2,1,0:T(8,128)(2,1)S(1)} %get-tuple-element.132.refs_0_, ...), custom_call_target="tpu_custom_call" | custom-call | tf_op jit(solution)/shard_map/forward/pallas_call | solution.py:546
  133.0 6.0 %collective-permute-done.10 = bf16[4,4,416,256]{3,2,1,0:T(8,128)(2,1)S(1)} collective-permute-done((bf16[4,4,416,256]{3,2,1,0:T(8,128)(2,1)S(1)}, bf16[4,4,416,256]{3,2,1,0:T(8,128)(2,1)S(1)}, u32[]{:S(2)}, u32[]{:S(2)}) %collective-permute-start.10) | collective-permute-done | bytes 3407904 | tf_op jit(solution)/shard_map/ppermute | solution.py:32
  147.0 18.8 %collective-permute-done.21 = bf16[256,256]{1,0:T(8,128)(2,1)S(1)} collective-permute-done((bf16[256,256]{1,0:T(8,128)(2,1)S(1)}, bf16[256,256]{1,0:T(8,128)(2,1)S(1)}, u32[]{:S(2)}, u32[]{:S(2)}) %collective-permute-start.21) | collective-permute-done | bytes 131104 | tf_op jit(solution)/shard_map/ppermute | solution.py:32
  172.1 9.5 %collective-permute-done.12.low_last = bf16[2,416,256]{2,1,0:T(8,128)(2,1)S(1)} collective-permute-done((bf16[2,416,256]{2,1,0:T(8,128)(2,1)S(1)}, bf16[2,416,256]{2,1,0:T(8,128)(2,1)S(1)}, u32[]{:S(2)}, u32[]{:S(2)}) %collective-permute-start.12) | collective-permute-done | bytes 426016 | tf_op jit(solution)/shard_map/ppermute | solution.py:32
  224.8 9.2 %collective-permute-done.35.refs_4_ = bf16[2,416,256]{2,1,0:T(8,128)(2,1)S(1)} collective-permute-done((bf16[2,416,256]{2,1,0:T(8,128)(2,1)S(1)}, bf16[2,416,256]{2,1,0:T(8,128)(2,1)S(1)}, u32[]{:S(2)}, u32[]{:S(2)}) %collective-permute-start.35) | collective-permute-done | bytes 426016 | tf_op jit(solution)/shard_map/ppermute | solution.py:32
  238.0 15.7 %collective-permute-done.37.refs_6_ = bf16[2,2,416,256]{3,2,1,0:T(8,128)(2,1)} collective-permute-done((bf16[2,2,416,256]{3,2,1,0:T(8,128)(2,1)}, bf16[2,2,416,256]{3,2,1,0:T(8,128)(2,1)}, u32[]{:S(2)}, u32[]{:S(2)}) %collective-permute-start.37) | collective-permute-done | bytes 852000 | tf_op jit(solution)/shard_map/ppermute | solution.py:32
  256.5 2.9 collective-permute-done.40.refs_9_
  260.2 14.3 %weights_backward.1 = bf16[4,22,64,256]{3,2,1,0:T(8,128)(2,1)} custom-call(bf16[13,256,256]{2,1,0:T(8,128)(2,1)} %copy-done.7, bf16[2,256,256]{2,1,0:T(8,128)(2,1)} %copy-done.8, bf16[2,256,256]{2,1,0:T(8,128)(2,1)} %get-tuple-element.133.refs_1_, bf16[2,256,256]{2,1,0:T(8,128)(2,1)} %add_convert_fusion.2.refs_2_, bf16[4,416,256]{2,1,0:T(8,128)(2,1)} %copy-done.6, ...), custom_call_target="tpu_custom_call" | custom-call | tf_op jit(solution)/shard_map/weights_backward/pallas_call | solution.py:618
  275.7 18.3 %features_backward.1 = bf16[8,352,256]{2,1,0:T(8,128)(2,1)} custom-call(s32[1]{0:T(128)} %bitcast.1.h_ref, f32[256,256]{1,0:T(8,128)} %fusion.12.start_ref, bf16[24,256,256]{2,1,0:T(8,128)(2,1)} %copy-done.2, bf16[352,512]{1,0:T(8,128)(2,1)} %constant.110.clone.place_ref, bf16[2,256,256]{2,1,0:T(8,128)(2,1)} %copy-done.8, ...), custom_call_target="tpu_custom_call" | custom-call | tf_op jit(solution)/shard_map/features_backward/pallas_call | solution.py:670
  294.0 3.7 all-to-all-start.1
  300.0 17.4 %all-to-all-done.1.pieces_ref = bf16[8,352,256]{2,1,0:T(8,128)(2,1)S(1)} async-done(((bf16[8,352,256]{2,1,0:T(8,128)(2,1)}), bf16[8,352,256]{2,1,0:T(8,128)(2,1)S(1)}, u32[]{:S(2)}, u32[]{:S(2)}) %all-to-all-start.1) | async-done | bytes 1441824 | tf_op jit(solution)/shard_map/all_to_all | solution.py:1128
  317.3 2.9 unchoose.1
  324.1 13.0 %collective-permute-start.48 = (f32[144,256]{1,0:T(8,128)S(1)}, f32[144,256]{1,0:T(8,128)S(1)}, u32[]{:S(2)}, u32[]{:S(2)}) collective-permute-start(f32[144,256]{1,0:T(8,128)S(1)} %get-tuple-element.110), channel_id=1, source_target_pairs={{0,2},{1,3},{2,0},{3,1},{4,6},{5,7},{6,4},{7,5},{8,10},{9,11},{10,... | collective-permute-start | bytes 442376 | tf_op jit(solution)/shard_map/ppermute | solution.py:32
  337.6 3.4 collective-permute-start.44
  342.3 8.2 %collective-permute-start.46 = (bf16[130,2304]{1,0:T(8,128)(2,1)}, bf16[130,2304]{1,0:T(8,128)(2,1)S(1)}, u32[]{:S(2)}, u32[]{:S(2)}) collective-permute-start(bf16[130,2304]{1,0:T(8,128)(2,1)} %get-tuple-element.81), channel_id=1, source_target_pairs={{1,2},{2,1},{3,0},{5,6},{6,5},{7,4},{9,10},{10,9},{11,8},{13,14},{... | collective-permute-start | bytes 1797128 | tf_op jit(solution)/shard_map/ppermute | solution.py:32
  351.4 7.2 %collective-permute-done.49 = f32[144,256]{1,0:T(8,128)S(1)} collective-permute-done((f32[144,256]{1,0:T(8,128)S(1)}, f32[144,256]{1,0:T(8,128)S(1)}, u32[]{:S(2)}, u32[]{:S(2)}) %collective-permute-start.49) | collective-permute-done | bytes 147488 | tf_op jit(solution)/shard_map/ppermute | solution.py:32
  362.0 6.8 %reduce-scatter.3.cloned.1.call-done = bf16[1,22,64,256]{3,2,1,0:T(8,128)(2,1)} async-done(((bf16[4,22,64,256]{3,2,1,0:T(8,128)(2,1)}), bf16[1,22,64,256]{3,2,1,0:T(8,128)(2,1)}) %reduce-scatter.3.cloned.1.call-update) | async-done | bytes 720912 | tf_op jit(solution)/shard_map/reduce_scatter | solution.py:172
  372.7 5.3 %collective-permute-done.44.refs_1_.refs_5_ = bf16[130,2304]{1,0:T(8,128)(2,1)S(1)} collective-permute-done((bf16[130,2304]{1,0:T(8,128)(2,1)}, bf16[130,2304]{1,0:T(8,128)(2,1)S(1)}, u32[]{:S(2)}, u32[]{:S(2)}) %collective-permute-start.44) | collective-permute-done | bytes 599072 | tf_op jit(solution)/shard_map/ppermute | solution.py:32
  378.0 6.2 %collective-permute-done.45.refs_2_.refs_6_ = bf16[130,2304]{1,0:T(8,128)(2,1)S(1)} collective-permute-done((bf16[130,2304]{1,0:T(8,128)(2,1)}, bf16[130,2304]{1,0:T(8,128)(2,1)S(1)}, u32[]{:S(2)}, u32[]{:S(2)}) %collective-permute-start.45) | collective-permute-done | bytes 599072 | tf_op jit(solution)/shard_map/ppermute | solution.py:32
  384.2 27.4 %collective-permute-done.46.refs_3_.refs_7_ = bf16[130,2304]{1,0:T(8,128)(2,1)S(1)} collective-permute-done((bf16[130,2304]{1,0:T(8,128)(2,1)}, bf16[130,2304]{1,0:T(8,128)(2,1)S(1)}, u32[]{:S(2)}, u32[]{:S(2)}) %collective-permute-start.46) | collective-permute-done | bytes 599072 | tf_op jit(solution)/shard_map/ppermute | solution.py:32
  411.6 6.6 %interleave.1 = (bf16[130,4,2048]{2,1,0:T(4,128)(2,1)}, bf16[130,4,256]{2,1,0:T(4,128)(2,1)}) custom-call(s32[1]{0:T(128)} %bitcast.z_ref, bf16[130,2304]{1,0:T(8,128)(2,1)S(1)} %get-tuple-element.78.refs_0_.refs_4_, bf16[130,2304]{1,0:T(8,128)(2,1)S(1)} %collective-permute-done.44.refs_1_.refs_5_, ...), custom_call_target="tpu_custom_call" | custom-call | tf_op jit(solution)/shard_map/interleave/pallas_call | solution.py:426
  (229 shorter events, 109.6 us)
Async XLA Ops:
  10.7 46.0 %collective-permute-start.6 = (bf16[24,64,256]{2,1,0:T(8,128)(2,1)S(1)}, bf16[24,64,256]{2,1,0:T(8,128)(2,1)S(1)}, u32[]{:S(2)}, u32[]{:S(2)}) collective-permute-start(bf16[24,64,256]{2,1,0:T(8,128)(2,1)S(1)} %pack_weights.1), channel_id=1, source_target_pairs={{1,0},{2,1},{3,2},{5,4},{6,5},{7,6},{9,8},{10,9},{11,10},{13,12},{... | collective-permute-start | bytes 2359304 | tf_op jit(solution)/shard_map/ppermute | solution.py:139
  12.8 74.2 %collective-permute-start.3 = (bf16[24,64,256]{2,1,0:T(8,128)(2,1)S(1)}, bf16[24,64,256]{2,1,0:T(8,128)(2,1)}, u32[]{:S(2)}, u32[]{:S(2)}) collective-permute-start(bf16[24,64,256]{2,1,0:T(8,128)(2,1)S(1)} %pack_weights.1), channel_id=1, source_target_pairs={{0,1},{1,2},{2,3},{4,5},{5,6},{6,7},{8,9},{9,10},{10,11},{12,13},{... | collective-permute-start | bytes 2359304 | tf_op jit(solution)/shard_map/ppermute | solution.py:139
  22.4 34.2 %collective-permute-start = (bf16[130,2304]{1,0:T(8,128)(2,1)S(1)}, bf16[130,2304]{1,0:T(8,128)(2,1)S(1)}, u32[]{:S(2)}, u32[]{:S(2)}) collective-permute-start(bf16[130,2304]{1,0:T(8,128)(2,1)S(1)} %get-tuple-element.50), channel_id=1, source_target_pairs={{0,1},{1,0},{2,3},{4,5},{5,4},{6,7},{8,9},{9,8},{10,11},{12,13},{1... | collective-permute-start | bytes 1797128 | tf_op jit(solution)/shard_map/ppermute | solution.py:32
  25.2 49.8 %collective-permute-start.1 = (bf16[130,2304]{1,0:T(8,128)(2,1)S(1)}, bf16[130,2304]{1,0:T(8,128)(2,1)S(1)}, u32[]{:S(2)}, u32[]{:S(2)}) collective-permute-start(bf16[130,2304]{1,0:T(8,128)(2,1)S(1)} %get-tuple-element.51), channel_id=1, source_target_pairs={{0,2},{1,3},{2,0},{4,6},{5,7},{6,4},{8,10},{9,11},{10,8},{12,14},{... | collective-permute-start | bytes 1797128 | tf_op jit(solution)/shard_map/ppermute | solution.py:32
  26.6 60.4 %collective-permute-start.2 = (bf16[130,2304]{1,0:T(8,128)(2,1)S(1)}, bf16[130,2304]{1,0:T(8,128)(2,1)S(1)}, u32[]{:S(2)}, u32[]{:S(2)}) collective-permute-start(bf16[130,2304]{1,0:T(8,128)(2,1)S(1)} %get-tuple-element.52), channel_id=1, source_target_pairs={{0,3},{1,2},{2,1},{4,7},{5,6},{6,5},{8,11},{9,10},{10,9},{12,15},{... | collective-permute-start | bytes 1797128 | tf_op jit(solution)/shard_map/ppermute | solution.py:32
  56.7 44.5 %collective-permute-start.8 = (bf16[24,64,256]{2,1,0:T(8,128)(2,1)S(1)}, bf16[24,64,256]{2,1,0:T(8,128)(2,1)}, u32[]{:S(2)}, u32[]{:S(2)}) collective-permute-start(bf16[24,64,256]{2,1,0:T(8,128)(2,1)S(1)} %collective-permute-done.6), channel_id=1, source_target_pairs={{1,0},{2,1},{5,4},{6,5},{9,8},{10,9},{13,12},{14,13},{17,16},{18,1... | collective-permute-start | bytes 2359304 | tf_op jit(solution)/shard_map/ppermute | solution.py:139
  87.0 20.4 %collective-permute-start.4 = (bf16[24,64,256]{2,1,0:T(8,128)(2,1)}, bf16[24,64,256]{2,1,0:T(8,128)(2,1)}, u32[]{:S(2)}, u32[]{:S(2)}) collective-permute-start(bf16[24,64,256]{2,1,0:T(8,128)(2,1)} %collective-permute-done.3), channel_id=1, source_target_pairs={{1,2},{5,6},{9,10},{13,14},{17,18},{21,22},{25,26},{29,30}} | collective-permute-start | bytes 2359304 | tf_op jit(solution)/shard_map/ppermute | solution.py:139
  95.5 23.3 %all-to-all-start = ((bf16[8,352,256]{2,1,0:T(8,128)(2,1)}), bf16[8,352,256]{2,1,0:T(8,128)(2,1)S(1)}, u32[]{:S(2)}, u32[]{:S(2)}) async-start(bf16[8,352,256]{2,1,0:T(8,128)(2,1)} %copy-done.12), calls=%async_computation | async-start | bytes 2883584 | tf_op jit(solution)/shard_map/all_to_all | solution.py:922
  99.2 198.8 %reduce-scatter.5.cloned.1.call-start = ((), (), s32[]{:S(2)}) async-start(), calls=%async_computation.5 | async-start | bytes 1179648 | tf_op jit(solution)/shard_map/reduce_scatter | solution.py:1110
  99.6 20.3 %collective-permute-start.7 = (bf16[24,64,256]{2,1,0:T(8,128)(2,1)}, bf16[24,64,256]{2,1,0:T(8,128)(2,1)}, u32[]{:S(2)}, u32[]{:S(2)}) collective-permute-start(bf16[24,64,256]{2,1,0:T(8,128)(2,1)} %collective-permute-done.3), channel_id=1, source_target_pairs={{2,3},{6,7},{10,11},{14,15},{18,19},{22,23},{26,27},{30,31}} | collective-permute-start | bytes 2359304 | tf_op jit(solution)/shard_map/ppermute | solution.py:139
  101.2 19.2 %collective-permute-start.9 = (bf16[24,64,256]{2,1,0:T(8,128)(2,1)}, bf16[24,64,256]{2,1,0:T(8,128)(2,1)}, u32[]{:S(2)}, u32[]{:S(2)}) collective-permute-start(bf16[24,64,256]{2,1,0:T(8,128)(2,1)} %collective-permute-done.8), channel_id=1, source_target_pairs={{1,0},{5,4},{9,8},{13,12},{17,16},{21,20},{25,24},{29,28}} | collective-permute-start | bytes 2359304 | tf_op jit(solution)/shard_map/ppermute | solution.py:139
  107.4 13.0 %collective-permute-start.5 = (bf16[24,64,256]{2,1,0:T(8,128)(2,1)}, bf16[24,64,256]{2,1,0:T(8,128)(2,1)}, u32[]{:S(2)}, u32[]{:S(2)}) collective-permute-start(bf16[24,64,256]{2,1,0:T(8,128)(2,1)} %collective-permute-done.4), channel_id=1, source_target_pairs={{2,3},{6,7},{10,11},{14,15},{18,19},{22,23},{26,27},{30,31}} | collective-permute-start | bytes 2359304 | tf_op jit(solution)/shard_map/ppermute | solution.py:139
  140.0 29.1 %collective-permute-start.11 = (bf16[2,2,416,256]{3,2,1,0:T(8,128)(2,1)S(1)}, bf16[2,2,416,256]{3,2,1,0:T(8,128)(2,1)S(1)}, u32[]{:S(2)}, u32[]{:S(2)}) collective-permute-start(bf16[2,2,416,256]{3,2,1,0:T(8,128)(2,1)S(1)} %slice.126), channel_id=1, source_target_pairs={{0,8},{4,12},{8,0},{12,4},{16,24},{20,28},{24,16},{28,20},{1,9},{5... | collective-permute-start | bytes 2555912 | tf_op jit(solution)/shard_map/ppermute | solution.py:32
  141.9 29.0 %collective-permute-start.13 = (bf16[2,2,416,256]{3,2,1,0:T(8,128)(2,1)S(1)}, bf16[2,2,416,256]{3,2,1,0:T(8,128)(2,1)S(1)}, u32[]{:S(2)}, u32[]{:S(2)}) collective-permute-start(bf16[2,2,416,256]{3,2,1,0:T(8,128)(2,1)S(1)} %slice.222), channel_id=1, source_target_pairs={{0,16},{4,20},{8,24},{12,28},{16,0},{20,4},{24,8},{28,12},{1,17},{... | collective-permute-start | bytes 2555912 | tf_op jit(solution)/shard_map/ppermute | solution.py:32
  143.4 22.3 %collective-permute-start.21 = (bf16[256,256]{1,0:T(8,128)(2,1)S(1)}, bf16[256,256]{1,0:T(8,128)(2,1)S(1)}, u32[]{:S(2)}, u32[]{:S(2)}) collective-permute-start(bf16[256,256]{1,0:T(8,128)(2,1)S(1)} %get-tuple-element.96), channel_id=1, source_target_pairs={{0,24},{4,28},{8,16},{12,20},{16,8},{20,12},{24,0},{28,4},{1,25},{... | collective-permute-start | bytes 393224 | tf_op jit(solution)/shard_map/ppermute | solution.py:32
  143.9 24.3 %collective-permute-start.20 = (bf16[256,256]{1,0:T(8,128)(2,1)S(1)}, bf16[256,256]{1,0:T(8,128)(2,1)S(1)}, u32[]{:S(2)}, u32[]{:S(2)}) collective-permute-start(bf16[256,256]{1,0:T(8,128)(2,1)S(1)} %get-tuple-element.96), channel_id=1, source_target_pairs={{0,16},{4,20},{8,24},{12,28},{16,0},{20,4},{24,8},{28,12},{1,17},{... | collective-permute-start | bytes 393224 | tf_op jit(solution)/shard_map/ppermute | solution.py:32
  145.5 22.7 %collective-permute-start.19 = (bf16[256,256]{1,0:T(8,128)(2,1)S(1)}, bf16[256,256]{1,0:T(8,128)(2,1)S(1)}, u32[]{:S(2)}, u32[]{:S(2)}) collective-permute-start(bf16[256,256]{1,0:T(8,128)(2,1)S(1)} %get-tuple-element.96), channel_id=1, source_target_pairs={{0,8},{4,12},{8,0},{12,4},{16,24},{20,28},{24,16},{28,20},{1,9},{5... | collective-permute-start | bytes 393224 | tf_op jit(solution)/shard_map/ppermute | solution.py:32
  169.1 20.4 %collective-permute-start.22 = (bf16[4,256,256]{2,1,0:T(8,128)(2,1)}, bf16[4,256,256]{2,1,0:T(8,128)(2,1)}, u32[]{:S(2)}, u32[]{:S(2)}) collective-permute-start(bf16[4,256,256]{2,1,0:T(8,128)(2,1)} %pad_maximum_fusion.5.near_ref), channel_id=1, source_target_pairs={{0,4},{4,0},{8,12},{12,8},{16,20},{20,16},{24,28},{28,24},{1,5},{5... | collective-permute-start | bytes 1572872 | tf_op jit(solution)/shard_map/ppermute | solution.py:32
  169.3 12.3 %collective-permute-start.12 = (bf16[2,416,256]{2,1,0:T(8,128)(2,1)S(1)}, bf16[2,416,256]{2,1,0:T(8,128)(2,1)S(1)}, u32[]{:S(2)}, u32[]{:S(2)}) collective-permute-start(bf16[2,416,256]{2,1,0:T(8,128)(2,1)S(1)} %get-tuple-element.93), channel_id=1, source_target_pairs={{0,16},{4,20},{8,24},{12,28},{16,0},{20,4},{24,8},{28,12},{1,17},{... | collective-permute-start | bytes 1277960 | tf_op jit(solution)/shard_map/ppermute | solution.py:32
  171.0 12.0 %collective-permute-start.14 = (bf16[2,416,256]{2,1,0:T(8,128)(2,1)S(1)}, bf16[2,416,256]{2,1,0:T(8,128)(2,1)S(1)}, u32[]{:S(2)}, u32[]{:S(2)}) collective-permute-start(bf16[2,416,256]{2,1,0:T(8,128)(2,1)S(1)} %get-tuple-element.91), channel_id=1, source_target_pairs={{0,8},{4,12},{8,0},{12,4},{16,24},{20,28},{24,16},{28,20},{1,9},{5... | collective-permute-start | bytes 1277960 | tf_op jit(solution)/shard_map/ppermute | solution.py:32
  224.3 11.3 %collective-permute-start.36 = (bf16[2,416,256]{2,1,0:T(8,128)(2,1)S(1)}, bf16[2,416,256]{2,1,0:T(8,128)(2,1)S(1)}, u32[]{:S(2)}, u32[]{:S(2)}) collective-permute-start(bf16[2,416,256]{2,1,0:T(8,128)(2,1)S(1)} %get-tuple-element.105), channel_id=1, source_target_pairs={{0,16},{4,20},{8,24},{12,28},{16,0},{20,4},{24,8},{28,12},{1,17},{... | collective-permute-start | bytes 1277960 | tf_op jit(solution)/shard_map/ppermute | solution.py:32
  235.0 18.7 %collective-permute-start.37 = (bf16[2,2,416,256]{3,2,1,0:T(8,128)(2,1)}, bf16[2,2,416,256]{3,2,1,0:T(8,128)(2,1)}, u32[]{:S(2)}, u32[]{:S(2)}) collective-permute-start(bf16[2,2,416,256]{3,2,1,0:T(8,128)(2,1)} %pad_maximum_fusion.2), channel_id=1, source_target_pairs={{0,16},{4,20},{8,24},{12,28},{16,0},{20,4},{24,8},{28,12},{1,17},{... | collective-permute-start | bytes 2555912 | tf_op jit(solution)/shard_map/ppermute | solution.py:32
  237.5 18.5 %collective-permute-start.38 = (bf16[2,2,416,256]{3,2,1,0:T(8,128)(2,1)}, bf16[2,2,416,256]{3,2,1,0:T(8,128)(2,1)}, u32[]{:S(2)}, u32[]{:S(2)}) collective-permute-start(bf16[2,2,416,256]{3,2,1,0:T(8,128)(2,1)} %pad_maximum_fusion.3), channel_id=1, source_target_pairs={{0,8},{4,12},{8,0},{12,4},{16,24},{20,28},{24,16},{28,20},{1,9},{5... | collective-permute-start | bytes 2555912 | tf_op jit(solution)/shard_map/ppermute | solution.py:32
  237.9 130.9 %reduce-scatter.3.cloned.1.call-start = ((), (), s32[]{:S(2)}) async-start(), calls=%async_computation.4 | async-start | bytes 3604480 | tf_op jit(solution)/shard_map/reduce_scatter | solution.py:172
  237.9 18.6 %collective-permute-start.39 = (bf16[4,416,256]{2,1,0:T(8,128)(2,1)}, bf16[4,416,256]{2,1,0:T(8,128)(2,1)}, u32[]{:S(2)}, u32[]{:S(2)}) collective-permute-start(bf16[4,416,256]{2,1,0:T(8,128)(2,1)} %copy-done.6), channel_id=1, source_target_pairs={{0,4},{4,0},{8,12},{12,8},{16,20},{20,16},{24,28},{28,24},{1,5},{5... | collective-permute-start | bytes 2555912 | tf_op jit(solution)/shard_map/ppermute | solution.py:32
  294.0 23.3 %all-to-all-start.1 = ((bf16[8,352,256]{2,1,0:T(8,128)(2,1)}), bf16[8,352,256]{2,1,0:T(8,128)(2,1)S(1)}, u32[]{:S(2)}, u32[]{:S(2)}) async-start(bf16[8,352,256]{2,1,0:T(8,128)(2,1)} %features_backward.1), calls=%async_computation.1 | async-start | bytes 2883584 | tf_op jit(solution)/shard_map/all_to_all | solution.py:1128
  321.3 21.0 %collective-permute-start.47 = (f32[144,256]{1,0:T(8,128)S(1)}, f32[144,256]{1,0:T(8,128)S(1)}, u32[]{:S(2)}, u32[]{:S(2)}) collective-permute-start(f32[144,256]{1,0:T(8,128)S(1)} %get-tuple-element.111), channel_id=1, source_target_pairs={{0,1},{1,0},{2,3},{3,2},{4,5},{5,4},{6,7},{7,6},{8,9},{9,8},{10,11... | collective-permute-start | bytes 442376 | tf_op jit(solution)/shard_map/ppermute | solution.py:32
  324.1 27.3 %collective-permute-start.48 = (f32[144,256]{1,0:T(8,128)S(1)}, f32[144,256]{1,0:T(8,128)S(1)}, u32[]{:S(2)}, u32[]{:S(2)}) collective-permute-start(f32[144,256]{1,0:T(8,128)S(1)} %get-tuple-element.110), channel_id=1, source_target_pairs={{0,2},{1,3},{2,0},{3,1},{4,6},{5,7},{6,4},{7,5},{8,10},{9,11},{10,... | collective-permute-start | bytes 442376 | tf_op jit(solution)/shard_map/ppermute | solution.py:32
  337.1 21.5 %collective-permute-start.49 = (f32[144,256]{1,0:T(8,128)S(1)}, f32[144,256]{1,0:T(8,128)S(1)}, u32[]{:S(2)}, u32[]{:S(2)}) collective-permute-start(f32[144,256]{1,0:T(8,128)S(1)} %get-tuple-element.109), channel_id=1, source_target_pairs={{0,3},{1,2},{2,1},{3,0},{4,7},{5,6},{6,5},{7,4},{8,11},{9,10},{10,... | collective-permute-start | bytes 442376 | tf_op jit(solution)/shard_map/ppermute | solution.py:32
  337.6 40.4 %collective-permute-start.44 = (bf16[130,2304]{1,0:T(8,128)(2,1)}, bf16[130,2304]{1,0:T(8,128)(2,1)S(1)}, u32[]{:S(2)}, u32[]{:S(2)}) collective-permute-start(bf16[130,2304]{1,0:T(8,128)(2,1)} %get-tuple-element.79), channel_id=1, source_target_pairs={{0,1},{1,0},{3,2},{4,5},{5,4},{7,6},{8,9},{9,8},{11,10},{12,13},{1... | collective-permute-start | bytes 1797128 | tf_op jit(solution)/shard_map/ppermute | solution.py:32
  341.0 43.2 %collective-permute-start.45 = (bf16[130,2304]{1,0:T(8,128)(2,1)}, bf16[130,2304]{1,0:T(8,128)(2,1)S(1)}, u32[]{:S(2)}, u32[]{:S(2)}) collective-permute-start(bf16[130,2304]{1,0:T(8,128)(2,1)} %get-tuple-element.80), channel_id=1, source_target_pairs={{0,2},{2,0},{3,1},{4,6},{6,4},{7,5},{8,10},{10,8},{11,9},{12,14},{... | collective-permute-start | bytes 1797128 | tf_op jit(solution)/shard_map/ppermute | solution.py:32
  342.3 69.3 %collective-permute-start.46 = (bf16[130,2304]{1,0:T(8,128)(2,1)}, bf16[130,2304]{1,0:T(8,128)(2,1)S(1)}, u32[]{:S(2)}, u32[]{:S(2)}) collective-permute-start(bf16[130,2304]{1,0:T(8,128)(2,1)} %get-tuple-element.81), channel_id=1, source_target_pairs={{1,2},{2,1},{3,0},{5,6},{6,5},{7,4},{9,10},{10,9},{11,8},{13,14},{... | collective-permute-start | bytes 1797128 | tf_op jit(solution)/shard_map/ppermute | solution.py:32
  (58 other events, 849.2 us)
Sparse Core Ops, SparseCore 0:
  238.0 50.5 reduce-scatter.4
  290.9 77.8 reduce-scatter.2

commit v5 on v4

--- a/solution.py
+++ b/solution.py
@@ -1140,7 +1140,7 @@
         df, acts = interleave(got, z, blocks, rows, cols, out, [atrous])
         wide = jnp.broadcast_to(jnp.pad(sums, ((0, 4), (0, 0)))[None], (wa, 16, out))
         rest = jnp.concatenate([rest.astype(F32).reshape(wa, -1, out), wide], axis=1)
-        rest = exchange_sum(after(rest, got[0]))
+        rest = exchange_sum(rest)
         sums = rest[-16:-4]
         rest = rest[:-16].reshape(2, -1, out)
     else:

time: 431 us -> 427 us (level)
  starting transfers between devices: 92.8 us -> 76.3 us
  waiting for transfers between devices: 219 us -> 226 us
    ppermute x43, starting transfers between devices: 64.2 us -> 47.7 us  [swap(): return lax.ppermute(array, axis, pairs)]
    reduce_scatter x1, waiting for transfers between devices: 0.02 us -> 13 us  [local(): lax.psum_scatter(grad_proj, 'ha', scatter_dimension=0, tiled=False)]
    all_to_all x1, waiting for transfers between devices: 17.4 us -> 11.7 us  [local(): back = lax.all_to_all(back, 'ha', 0, 0, tiled=True)]
    ppermute x43, waiting for transfers between devices: 182 us -> 178 us  [swap(): return lax.ppermute(array, axis, pairs)]
    reduce_scatter x1, waiting for transfers between devices: 6.82 us -> 11.4 us  [line_scatter(): lax.psum_scatter(parts, 'wa', scatter_dimension=0, tiled=False).astype(F32)]
    unnamed x78 -> x76, local copies, waits for them, and re-layouts: 13 us -> 16.7 us
  transfers between devices with their start and end apart: 54 -> 54, of which waited for: 37 -> 37; matrix products, arithmetic and copies ran while one was open for 4% -> 5% of each run, Pallas kernels for 10% -> 10%
where the time goes in v5:
time: 427 us; the launch traced here: 421 us
  waiting for transfers between devices  226 us (53%)
  starting transfers between devices  76.3 us (18%)
  Pallas kernels  62.8 us (15%)
  local copies, waits for them, and re-layouts  22 us (5%)
  other arithmetic  16.2 us (4%)
  between operations  15.3 us (4%)
    ppermute x43, waiting for transfers between devices, swap(): return lax.ppermute(array, axis, pairs)  178 us
    ppermute x43, starting transfers between devices, swap(): return lax.ppermute(array, axis, pairs)  47.7 us
    ppermute x7, starting transfers between devices, neighbour(): return lax.ppermute(array, 'wa', pairs)  21 us
    pallas_call x1, Pallas kernels, features_backward(): pl.pallas_call(kernel, out_shape=jax.ShapeDtypeStruct((ha, fit, deep), BF...  18.7 us
    unnamed x76, local copies, waits for them, and re-layouts  16.7 us
    pallas_call x1, Pallas kernels, weights_backward(): pl.pallas_call(kernel, out_shape=jax.ShapeDtypeStruct(shape, BF16), grid=...  14.3 us
    reduce_scatter x1, waiting for transfers between devices, local(): lax.psum_scatter(grad_proj, 'ha', scatter_dimension=0, tiled=False)  13 us
    all_to_all x1, waiting for transfers between devices, local(): back = lax.all_to_all(back, 'ha', 0, 0, tiled=True)  11.7 us
  transfers between devices with their start and end apart: 54, of which 37 were waited for; matrix products, arithmetic and copies ran while one was open for 5% of the time, Pallas kernels for 10%

profile of v5, /device:TPU:8, one launch (start us, length us, event | category | flops | bytes accessed | tf_op | source)
XLA Modules:
  0.0 421.4 jit_solution(5710653090982212924)
XLA Ops:
  12.8 3.9 collective-permute-start.3
  19.3 3.2 extract.1
  26.6 5.1 %collective-permute-start.2 = (bf16[130,2304]{1,0:T(8,128)(2,1)S(1)}, bf16[130,2304]{1,0:T(8,128)(2,1)S(1)}, u32[]{:S(2)}, u32[]{:S(2)}) collective-permute-start(bf16[130,2304]{1,0:T(8,128)(2,1)S(1)} %get-tuple-element.51), channel_id=1, source_target_pairs={{0,3},{1,2},{2,1},{4,7},{5,6},{6,5},{8,11},{9,10},{10,9},{12,15},{... | collective-permute-start | bytes 1797128 | tf_op jit(solution)/shard_map/ppermute | solution.py:32
  31.7 25.0 %collective-permute-done.refs_1_ = bf16[130,2304]{1,0:T(8,128)(2,1)S(1)} collective-permute-done((bf16[130,2304]{1,0:T(8,128)(2,1)S(1)}, bf16[130,2304]{1,0:T(8,128)(2,1)S(1)}, u32[]{:S(2)}, u32[]{:S(2)}) %collective-permute-start) | collective-permute-done | bytes 599072 | tf_op jit(solution)/shard_map/ppermute | solution.py:32
  56.7 4.4 %collective-permute-start.8 = (bf16[24,64,256]{2,1,0:T(8,128)(2,1)S(1)}, bf16[24,64,256]{2,1,0:T(8,128)(2,1)}, u32[]{:S(2)}, u32[]{:S(2)}) collective-permute-start(bf16[24,64,256]{2,1,0:T(8,128)(2,1)S(1)} %collective-permute-done.6), channel_id=1, source_target_pairs={{1,0},{2,1},{5,4},{6,5},{9,8},{10,9},{13,12},{14,13},{17,16},{18,1... | collective-permute-start | bytes 2359304 | tf_op jit(solution)/shard_map/ppermute | solution.py:139
  61.1 13.9 %collective-permute-done.1.refs_2_ = bf16[130,2304]{1,0:T(8,128)(2,1)S(1)} collective-permute-done((bf16[130,2304]{1,0:T(8,128)(2,1)S(1)}, bf16[130,2304]{1,0:T(8,128)(2,1)S(1)}, u32[]{:S(2)}, u32[]{:S(2)}) %collective-permute-start.1) | collective-permute-done | bytes 599072 | tf_op jit(solution)/shard_map/ppermute | solution.py:32
  75.0 12.0 %collective-permute-done.2.refs_3_ = bf16[130,2304]{1,0:T(8,128)(2,1)S(1)} collective-permute-done((bf16[130,2304]{1,0:T(8,128)(2,1)S(1)}, bf16[130,2304]{1,0:T(8,128)(2,1)S(1)}, u32[]{:S(2)}, u32[]{:S(2)}) %collective-permute-start.2) | collective-permute-done | bytes 599072 | tf_op jit(solution)/shard_map/ppermute | solution.py:32
  87.0 5.4 %collective-permute-start.4 = (bf16[24,64,256]{2,1,0:T(8,128)(2,1)}, bf16[24,64,256]{2,1,0:T(8,128)(2,1)}, u32[]{:S(2)}, u32[]{:S(2)}) collective-permute-start(bf16[24,64,256]{2,1,0:T(8,128)(2,1)} %collective-permute-done.3), channel_id=1, source_target_pairs={{1,2},{5,6},{9,10},{13,14},{17,18},{21,22},{25,26},{29,30}} | collective-permute-start | bytes 2359304 | tf_op jit(solution)/shard_map/ppermute | solution.py:139
  95.5 3.7 all-to-all-start
  103.3 4.1 collective-permute-done.4
  111.0 7.8 %all-to-all-done.raw_ref = bf16[8,352,256]{2,1,0:T(8,128)(2,1)S(1)} async-done(((bf16[8,352,256]{2,1,0:T(8,128)(2,1)}), bf16[8,352,256]{2,1,0:T(8,128)(2,1)S(1)}, u32[]{:S(2)}, u32[]{:S(2)}) %all-to-all-start) | async-done | bytes 1441824 | tf_op jit(solution)/shard_map/all_to_all | solution.py:922
  123.8 9.1 %forward.1 = (bf16[4,4,416,256]{3,2,1,0:T(8,128)(2,1)S(1)}, bf16[4,4,416,256]{3,2,1,0:T(8,128)(2,1)S(1)}) custom-call(bf16[13,256,256]{2,1,0:T(8,128)(2,1)S(1)} %get-tuple-element.53.x_ref, bf16[24,256,256]{2,1,0:T(8,128)(2,1)S(1)} %pad_maximum_fusion.w_ref, bf16[2,256,256]{2,1,0:T(8,128)(2,1)S(1)} %get-tuple-element.130.refs_0_, ...), custom_call_target="tpu_custom_call" | custom-call | tf_op jit(solution)/shard_map/forward/pallas_call | solution.py:546
  133.0 6.0 %collective-permute-done.10 = bf16[4,4,416,256]{3,2,1,0:T(8,128)(2,1)S(1)} collective-permute-done((bf16[4,4,416,256]{3,2,1,0:T(8,128)(2,1)S(1)}, bf16[4,4,416,256]{3,2,1,0:T(8,128)(2,1)S(1)}, u32[]{:S(2)}, u32[]{:S(2)}) %collective-permute-start.10) | collective-permute-done | bytes 3407904 | tf_op jit(solution)/shard_map/ppermute | solution.py:32
  146.9 18.8 %collective-permute-done.21 = bf16[256,256]{1,0:T(8,128)(2,1)S(1)} collective-permute-done((bf16[256,256]{1,0:T(8,128)(2,1)S(1)}, bf16[256,256]{1,0:T(8,128)(2,1)S(1)}, u32[]{:S(2)}, u32[]{:S(2)}) %collective-permute-start.21) | collective-permute-done | bytes 131104 | tf_op jit(solution)/shard_map/ppermute | solution.py:32
  172.1 9.5 %collective-permute-done.12.low_last = bf16[2,416,256]{2,1,0:T(8,128)(2,1)S(1)} collective-permute-done((bf16[2,416,256]{2,1,0:T(8,128)(2,1)S(1)}, bf16[2,416,256]{2,1,0:T(8,128)(2,1)S(1)}, u32[]{:S(2)}, u32[]{:S(2)}) %collective-permute-start.12) | collective-permute-done | bytes 426016 | tf_op jit(solution)/shard_map/ppermute | solution.py:32
  224.8 9.2 %collective-permute-done.35.refs_4_ = bf16[2,416,256]{2,1,0:T(8,128)(2,1)S(1)} collective-permute-done((bf16[2,416,256]{2,1,0:T(8,128)(2,1)S(1)}, bf16[2,416,256]{2,1,0:T(8,128)(2,1)S(1)}, u32[]{:S(2)}, u32[]{:S(2)}) %collective-permute-start.35) | collective-permute-done | bytes 426016 | tf_op jit(solution)/shard_map/ppermute | solution.py:32
  238.0 15.8 %collective-permute-done.37.refs_6_ = bf16[2,2,416,256]{3,2,1,0:T(8,128)(2,1)} collective-permute-done((bf16[2,2,416,256]{3,2,1,0:T(8,128)(2,1)}, bf16[2,2,416,256]{3,2,1,0:T(8,128)(2,1)}, u32[]{:S(2)}, u32[]{:S(2)}) %collective-permute-start.37) | collective-permute-done | bytes 852000 | tf_op jit(solution)/shard_map/ppermute | solution.py:32
  256.5 2.9 collective-permute-done.40.refs_9_
  260.2 14.3 %weights_backward.1 = bf16[4,22,64,256]{3,2,1,0:T(8,128)(2,1)} custom-call(bf16[13,256,256]{2,1,0:T(8,128)(2,1)} %copy-done.7, bf16[2,256,256]{2,1,0:T(8,128)(2,1)} %copy-done.8, bf16[2,256,256]{2,1,0:T(8,128)(2,1)} %get-tuple-element.131.refs_1_, bf16[2,256,256]{2,1,0:T(8,128)(2,1)} %add_convert_fusion.2.refs_2_, bf16[4,416,256]{2,1,0:T(8,128)(2,1)} %copy-done.6, ...), custom_call_target="tpu_custom_call" | custom-call | tf_op jit(solution)/shard_map/weights_backward/pallas_call | solution.py:618
  275.6 13.0 %reduce-scatter.5.cloned.1.call-done = bf16[1,256,256]{2,1,0:T(8,128)(2,1)} async-done(((bf16[8,256,256]{2,1,0:T(8,128)(2,1)}), bf16[1,256,256]{2,1,0:T(8,128)(2,1)}) %reduce-scatter.5.cloned.1.call-update) | async-done | bytes 131088 | tf_op jit(solution)/shard_map/reduce_scatter | solution.py:1110
  294.8 18.7 %features_backward.1 = bf16[8,352,256]{2,1,0:T(8,128)(2,1)} custom-call(s32[1]{0:T(128)} %bitcast.1.h_ref, f32[256,256]{1,0:T(8,128)} %fusion.21.start_ref, bf16[24,256,256]{2,1,0:T(8,128)(2,1)} %copy-done.2, bf16[352,512]{1,0:T(8,128)(2,1)} %constant.110.clone.place_ref, bf16[2,256,256]{2,1,0:T(8,128)(2,1)} %copy-done.8, ...), custom_call_target="tpu_custom_call" | custom-call | tf_op jit(solution)/shard_map/features_backward/pallas_call | solution.py:670
  313.6 3.7 all-to-all-start.1
  317.9 3.6 collective-permute-done.49
  325.1 11.7 %all-to-all-done.1.pieces_ref = bf16[8,352,256]{2,1,0:T(8,128)(2,1)S(1)} async-done(((bf16[8,352,256]{2,1,0:T(8,128)(2,1)}), bf16[8,352,256]{2,1,0:T(8,128)(2,1)S(1)}, u32[]{:S(2)}, u32[]{:S(2)}) %all-to-all-start.1) | async-done | bytes 1441824 | tf_op jit(solution)/shard_map/all_to_all | solution.py:1128
  336.9 2.9 unchoose.1
  339.8 3.3 collective-permute-start.44
  344.4 4.6 %collective-permute-start.46 = (bf16[130,2304]{1,0:T(8,128)(2,1)}, bf16[130,2304]{1,0:T(8,128)(2,1)S(1)}, u32[]{:S(2)}, u32[]{:S(2)}) collective-permute-start(bf16[130,2304]{1,0:T(8,128)(2,1)} %get-tuple-element.80), channel_id=1, source_target_pairs={{1,2},{2,1},{3,0},{5,6},{6,5},{7,4},{9,10},{10,9},{11,8},{13,14},{... | collective-permute-start | bytes 1797128 | tf_op jit(solution)/shard_map/ppermute | solution.py:32
  349.0 11.4 %reduce-scatter.3.cloned.1.call-done = bf16[1,22,64,256]{3,2,1,0:T(8,128)(2,1)} async-done(((bf16[4,22,64,256]{3,2,1,0:T(8,128)(2,1)}), bf16[1,22,64,256]{3,2,1,0:T(8,128)(2,1)}) %reduce-scatter.3.cloned.1.call-update) | async-done | bytes 720912 | tf_op jit(solution)/shard_map/reduce_scatter | solution.py:172
  369.0 2.9 collective-permute-done.44.refs_1_.refs_5_
  372.0 7.1 %collective-permute-done.45.refs_2_.refs_6_ = bf16[130,2304]{1,0:T(8,128)(2,1)S(1)} collective-permute-done((bf16[130,2304]{1,0:T(8,128)(2,1)}, bf16[130,2304]{1,0:T(8,128)(2,1)S(1)}, u32[]{:S(2)}, u32[]{:S(2)}) %collective-permute-start.45) | collective-permute-done | bytes 599072 | tf_op jit(solution)/shard_map/ppermute | solution.py:32
  379.1 28.6 %collective-permute-done.46.refs_3_.refs_7_ = bf16[130,2304]{1,0:T(8,128)(2,1)S(1)} collective-permute-done((bf16[130,2304]{1,0:T(8,128)(2,1)}, bf16[130,2304]{1,0:T(8,128)(2,1)S(1)}, u32[]{:S(2)}, u32[]{:S(2)}) %collective-permute-start.46) | collective-permute-done | bytes 599072 | tf_op jit(solution)/shard_map/ppermute | solution.py:32
  407.7 6.6 %interleave.1 = (bf16[130,4,2048]{2,1,0:T(4,128)(2,1)}, bf16[130,4,256]{2,1,0:T(4,128)(2,1)}) custom-call(s32[1]{0:T(128)} %bitcast.z_ref, bf16[130,2304]{1,0:T(8,128)(2,1)S(1)} %get-tuple-element.77.refs_0_.refs_4_, bf16[130,2304]{1,0:T(8,128)(2,1)S(1)} %collective-permute-done.44.refs_1_.refs_5_, ...), custom_call_target="tpu_custom_call" | custom-call | tf_op jit(solution)/shard_map/interleave/pallas_call | solution.py:426
  (226 shorter events, 113.7 us)
Async XLA Ops:
  10.7 46.0 %collective-permute-start.6 = (bf16[24,64,256]{2,1,0:T(8,128)(2,1)S(1)}, bf16[24,64,256]{2,1,0:T(8,128)(2,1)S(1)}, u32[]{:S(2)}, u32[]{:S(2)}) collective-permute-start(bf16[24,64,256]{2,1,0:T(8,128)(2,1)S(1)} %pack_weights.1), channel_id=1, source_target_pairs={{1,0},{2,1},{3,2},{5,4},{6,5},{7,6},{9,8},{10,9},{11,10},{13,12},{... | collective-permute-start | bytes 2359304 | tf_op jit(solution)/shard_map/ppermute | solution.py:139
  12.8 74.2 %collective-permute-start.3 = (bf16[24,64,256]{2,1,0:T(8,128)(2,1)S(1)}, bf16[24,64,256]{2,1,0:T(8,128)(2,1)}, u32[]{:S(2)}, u32[]{:S(2)}) collective-permute-start(bf16[24,64,256]{2,1,0:T(8,128)(2,1)S(1)} %pack_weights.1), channel_id=1, source_target_pairs={{0,1},{1,2},{2,3},{4,5},{5,6},{6,7},{8,9},{9,10},{10,11},{12,13},{... | collective-permute-start | bytes 2359304 | tf_op jit(solution)/shard_map/ppermute | solution.py:139
  22.4 34.2 %collective-permute-start = (bf16[130,2304]{1,0:T(8,128)(2,1)S(1)}, bf16[130,2304]{1,0:T(8,128)(2,1)S(1)}, u32[]{:S(2)}, u32[]{:S(2)}) collective-permute-start(bf16[130,2304]{1,0:T(8,128)(2,1)S(1)} %get-tuple-element.49), channel_id=1, source_target_pairs={{0,1},{1,0},{2,3},{4,5},{5,4},{6,7},{8,9},{9,8},{10,11},{12,13},{1... | collective-permute-start | bytes 1797128 | tf_op jit(solution)/shard_map/ppermute | solution.py:32
  25.2 49.8 %collective-permute-start.1 = (bf16[130,2304]{1,0:T(8,128)(2,1)S(1)}, bf16[130,2304]{1,0:T(8,128)(2,1)S(1)}, u32[]{:S(2)}, u32[]{:S(2)}) collective-permute-start(bf16[130,2304]{1,0:T(8,128)(2,1)S(1)} %get-tuple-element.50), channel_id=1, source_target_pairs={{0,2},{1,3},{2,0},{4,6},{5,7},{6,4},{8,10},{9,11},{10,8},{12,14},{... | collective-permute-start | bytes 1797128 | tf_op jit(solution)/shard_map/ppermute | solution.py:32
  26.6 60.4 %collective-permute-start.2 = (bf16[130,2304]{1,0:T(8,128)(2,1)S(1)}, bf16[130,2304]{1,0:T(8,128)(2,1)S(1)}, u32[]{:S(2)}, u32[]{:S(2)}) collective-permute-start(bf16[130,2304]{1,0:T(8,128)(2,1)S(1)} %get-tuple-element.51), channel_id=1, source_target_pairs={{0,3},{1,2},{2,1},{4,7},{5,6},{6,5},{8,11},{9,10},{10,9},{12,15},{... | collective-permute-start | bytes 1797128 | tf_op jit(solution)/shard_map/ppermute | solution.py:32
  56.7 44.4 %collective-permute-start.8 = (bf16[24,64,256]{2,1,0:T(8,128)(2,1)S(1)}, bf16[24,64,256]{2,1,0:T(8,128)(2,1)}, u32[]{:S(2)}, u32[]{:S(2)}) collective-permute-start(bf16[24,64,256]{2,1,0:T(8,128)(2,1)S(1)} %collective-permute-done.6), channel_id=1, source_target_pairs={{1,0},{2,1},{5,4},{6,5},{9,8},{10,9},{13,12},{14,13},{17,16},{18,1... | collective-permute-start | bytes 2359304 | tf_op jit(solution)/shard_map/ppermute | solution.py:139
  87.0 20.4 %collective-permute-start.4 = (bf16[24,64,256]{2,1,0:T(8,128)(2,1)}, bf16[24,64,256]{2,1,0:T(8,128)(2,1)}, u32[]{:S(2)}, u32[]{:S(2)}) collective-permute-start(bf16[24,64,256]{2,1,0:T(8,128)(2,1)} %collective-permute-done.3), channel_id=1, source_target_pairs={{1,2},{5,6},{9,10},{13,14},{17,18},{21,22},{25,26},{29,30}} | collective-permute-start | bytes 2359304 | tf_op jit(solution)/shard_map/ppermute | solution.py:139
  95.5 23.3 %all-to-all-start = ((bf16[8,352,256]{2,1,0:T(8,128)(2,1)}), bf16[8,352,256]{2,1,0:T(8,128)(2,1)S(1)}, u32[]{:S(2)}, u32[]{:S(2)}) async-start(bf16[8,352,256]{2,1,0:T(8,128)(2,1)} %copy-done.12), calls=%async_computation | async-start | bytes 2883584 | tf_op jit(solution)/shard_map/all_to_all | solution.py:922
  99.2 189.4 %reduce-scatter.5.cloned.1.call-start = ((), (), s32[]{:S(2)}) async-start(), calls=%async_computation.5 | async-start | bytes 1179648 | tf_op jit(solution)/shard_map/reduce_scatter | solution.py:1110
  99.6 20.3 %collective-permute-start.7 = (bf16[24,64,256]{2,1,0:T(8,128)(2,1)}, bf16[24,64,256]{2,1,0:T(8,128)(2,1)}, u32[]{:S(2)}, u32[]{:S(2)}) collective-permute-start(bf16[24,64,256]{2,1,0:T(8,128)(2,1)} %collective-permute-done.3), channel_id=1, source_target_pairs={{2,3},{6,7},{10,11},{14,15},{18,19},{22,23},{26,27},{30,31}} | collective-permute-start | bytes 2359304 | tf_op jit(solution)/shard_map/ppermute | solution.py:139
  101.1 19.2 %collective-permute-start.9 = (bf16[24,64,256]{2,1,0:T(8,128)(2,1)}, bf16[24,64,256]{2,1,0:T(8,128)(2,1)}, u32[]{:S(2)}, u32[]{:S(2)}) collective-permute-start(bf16[24,64,256]{2,1,0:T(8,128)(2,1)} %collective-permute-done.8), channel_id=1, source_target_pairs={{1,0},{5,4},{9,8},{13,12},{17,16},{21,20},{25,24},{29,28}} | collective-permute-start | bytes 2359304 | tf_op jit(solution)/shard_map/ppermute | solution.py:139
  107.4 13.0 %collective-permute-start.5 = (bf16[24,64,256]{2,1,0:T(8,128)(2,1)}, bf16[24,64,256]{2,1,0:T(8,128)(2,1)}, u32[]{:S(2)}, u32[]{:S(2)}) collective-permute-start(bf16[24,64,256]{2,1,0:T(8,128)(2,1)} %collective-permute-done.4), channel_id=1, source_target_pairs={{2,3},{6,7},{10,11},{14,15},{18,19},{22,23},{26,27},{30,31}} | collective-permute-start | bytes 2359304 | tf_op jit(solution)/shard_map/ppermute | solution.py:139
  140.0 29.1 %collective-permute-start.11 = (bf16[2,2,416,256]{3,2,1,0:T(8,128)(2,1)S(1)}, bf16[2,2,416,256]{3,2,1,0:T(8,128)(2,1)S(1)}, u32[]{:S(2)}, u32[]{:S(2)}) collective-permute-start(bf16[2,2,416,256]{3,2,1,0:T(8,128)(2,1)S(1)} %slice.126), channel_id=1, source_target_pairs={{0,8},{4,12},{8,0},{12,4},{16,24},{20,28},{24,16},{28,20},{1,9},{5... | collective-permute-start | bytes 2555912 | tf_op jit(solution)/shard_map/ppermute | solution.py:32
  141.8 29.0 %collective-permute-start.13 = (bf16[2,2,416,256]{3,2,1,0:T(8,128)(2,1)S(1)}, bf16[2,2,416,256]{3,2,1,0:T(8,128)(2,1)S(1)}, u32[]{:S(2)}, u32[]{:S(2)}) collective-permute-start(bf16[2,2,416,256]{3,2,1,0:T(8,128)(2,1)S(1)} %slice.222), channel_id=1, source_target_pairs={{0,16},{4,20},{8,24},{12,28},{16,0},{20,4},{24,8},{28,12},{1,17},{... | collective-permute-start | bytes 2555912 | tf_op jit(solution)/shard_map/ppermute | solution.py:32
  143.4 22.3 %collective-permute-start.21 = (bf16[256,256]{1,0:T(8,128)(2,1)S(1)}, bf16[256,256]{1,0:T(8,128)(2,1)S(1)}, u32[]{:S(2)}, u32[]{:S(2)}) collective-permute-start(bf16[256,256]{1,0:T(8,128)(2,1)S(1)} %get-tuple-element.94), channel_id=1, source_target_pairs={{0,24},{4,28},{8,16},{12,20},{16,8},{20,12},{24,0},{28,4},{1,25},{... | collective-permute-start | bytes 393224 | tf_op jit(solution)/shard_map/ppermute | solution.py:32
  143.9 24.3 %collective-permute-start.20 = (bf16[256,256]{1,0:T(8,128)(2,1)S(1)}, bf16[256,256]{1,0:T(8,128)(2,1)S(1)}, u32[]{:S(2)}, u32[]{:S(2)}) collective-permute-start(bf16[256,256]{1,0:T(8,128)(2,1)S(1)} %get-tuple-element.94), channel_id=1, source_target_pairs={{0,16},{4,20},{8,24},{12,28},{16,0},{20,4},{24,8},{28,12},{1,17},{... | collective-permute-start | bytes 393224 | tf_op jit(solution)/shard_map/ppermute | solution.py:32
  145.5 22.8 %collective-permute-start.19 = (bf16[256,256]{1,0:T(8,128)(2,1)S(1)}, bf16[256,256]{1,0:T(8,128)(2,1)S(1)}, u32[]{:S(2)}, u32[]{:S(2)}) collective-permute-start(bf16[256,256]{1,0:T(8,128)(2,1)S(1)} %get-tuple-element.94), channel_id=1, source_target_pairs={{0,8},{4,12},{8,0},{12,4},{16,24},{20,28},{24,16},{28,20},{1,9},{5... | collective-permute-start | bytes 393224 | tf_op jit(solution)/shard_map/ppermute | solution.py:32
  169.1 20.4 %collective-permute-start.22 = (bf16[4,256,256]{2,1,0:T(8,128)(2,1)}, bf16[4,256,256]{2,1,0:T(8,128)(2,1)}, u32[]{:S(2)}, u32[]{:S(2)}) collective-permute-start(bf16[4,256,256]{2,1,0:T(8,128)(2,1)} %pad_maximum_fusion.4.near_ref), channel_id=1, source_target_pairs={{0,4},{4,0},{8,12},{12,8},{16,20},{20,16},{24,28},{28,24},{1,5},{5... | collective-permute-start | bytes 1572872 | tf_op jit(solution)/shard_map/ppermute | solution.py:32
  169.3 12.3 %collective-permute-start.12 = (bf16[2,416,256]{2,1,0:T(8,128)(2,1)S(1)}, bf16[2,416,256]{2,1,0:T(8,128)(2,1)S(1)}, u32[]{:S(2)}, u32[]{:S(2)}) collective-permute-start(bf16[2,416,256]{2,1,0:T(8,128)(2,1)S(1)} %get-tuple-element.91), channel_id=1, source_target_pairs={{0,16},{4,20},{8,24},{12,28},{16,0},{20,4},{24,8},{28,12},{1,17},{... | collective-permute-start | bytes 1277960 | tf_op jit(solution)/shard_map/ppermute | solution.py:32
  171.0 12.0 %collective-permute-start.14 = (bf16[2,416,256]{2,1,0:T(8,128)(2,1)S(1)}, bf16[2,416,256]{2,1,0:T(8,128)(2,1)S(1)}, u32[]{:S(2)}, u32[]{:S(2)}) collective-permute-start(bf16[2,416,256]{2,1,0:T(8,128)(2,1)S(1)} %get-tuple-element.89), channel_id=1, source_target_pairs={{0,8},{4,12},{8,0},{12,4},{16,24},{20,28},{24,16},{28,20},{1,9},{5... | collective-permute-start | bytes 1277960 | tf_op jit(solution)/shard_map/ppermute | solution.py:32
  224.3 11.4 %collective-permute-start.36 = (bf16[2,416,256]{2,1,0:T(8,128)(2,1)S(1)}, bf16[2,416,256]{2,1,0:T(8,128)(2,1)S(1)}, u32[]{:S(2)}, u32[]{:S(2)}) collective-permute-start(bf16[2,416,256]{2,1,0:T(8,128)(2,1)S(1)} %get-tuple-element.103), channel_id=1, source_target_pairs={{0,16},{4,20},{8,24},{12,28},{16,0},{20,4},{24,8},{28,12},{1,17},{... | collective-permute-start | bytes 1277960 | tf_op jit(solution)/shard_map/ppermute | solution.py:32
  235.0 18.7 %collective-permute-start.37 = (bf16[2,2,416,256]{3,2,1,0:T(8,128)(2,1)}, bf16[2,2,416,256]{3,2,1,0:T(8,128)(2,1)}, u32[]{:S(2)}, u32[]{:S(2)}) collective-permute-start(bf16[2,2,416,256]{3,2,1,0:T(8,128)(2,1)} %pad_maximum_fusion.2), channel_id=1, source_target_pairs={{0,16},{4,20},{8,24},{12,28},{16,0},{20,4},{24,8},{28,12},{1,17},{... | collective-permute-start | bytes 2555912 | tf_op jit(solution)/shard_map/ppermute | solution.py:32
  237.4 18.5 %collective-permute-start.38 = (bf16[2,2,416,256]{3,2,1,0:T(8,128)(2,1)}, bf16[2,2,416,256]{3,2,1,0:T(8,128)(2,1)}, u32[]{:S(2)}, u32[]{:S(2)}) collective-permute-start(bf16[2,2,416,256]{3,2,1,0:T(8,128)(2,1)} %pad_maximum_fusion.3), channel_id=1, source_target_pairs={{0,8},{4,12},{8,0},{12,4},{16,24},{20,28},{24,16},{28,20},{1,9},{5... | collective-permute-start | bytes 2555912 | tf_op jit(solution)/shard_map/ppermute | solution.py:32
  237.8 122.6 %reduce-scatter.3.cloned.1.call-start = ((), (), s32[]{:S(2)}) async-start(), calls=%async_computation.4 | async-start | bytes 3604480 | tf_op jit(solution)/shard_map/reduce_scatter | solution.py:172
  237.9 18.6 %collective-permute-start.39 = (bf16[4,416,256]{2,1,0:T(8,128)(2,1)}, bf16[4,416,256]{2,1,0:T(8,128)(2,1)}, u32[]{:S(2)}, u32[]{:S(2)}) collective-permute-start(bf16[4,416,256]{2,1,0:T(8,128)(2,1)} %copy-done.6), channel_id=1, source_target_pairs={{0,4},{4,0},{8,12},{12,8},{16,20},{20,16},{24,28},{28,24},{1,5},{5... | collective-permute-start | bytes 2555912 | tf_op jit(solution)/shard_map/ppermute | solution.py:32
  290.3 27.6 %collective-permute-start.47 = (f32[144,256]{1,0:T(8,128)}, f32[144,256]{1,0:T(8,128)}, u32[]{:S(2)}, u32[]{:S(2)}) collective-permute-start(f32[144,256]{1,0:T(8,128)} %get-tuple-element.108), channel_id=1, source_target_pairs={{0,1},{1,0},{2,3},{3,2},{4,5},{5,4},{6,7},{7,6},{8,9},{9,8},{10,11... | collective-permute-start | bytes 442376 | tf_op jit(solution)/shard_map/ppermute | solution.py:32
  290.9 27.1 %collective-permute-start.48 = (f32[144,256]{1,0:T(8,128)}, f32[144,256]{1,0:T(8,128)}, u32[]{:S(2)}, u32[]{:S(2)}) collective-permute-start(f32[144,256]{1,0:T(8,128)} %get-tuple-element.109), channel_id=1, source_target_pairs={{0,2},{1,3},{2,0},{3,1},{4,6},{5,7},{6,4},{7,5},{8,10},{9,11},{10,... | collective-permute-start | bytes 442376 | tf_op jit(solution)/shard_map/ppermute | solution.py:32
  293.3 28.3 %collective-permute-start.49 = (f32[144,256]{1,0:T(8,128)S(1)}, f32[144,256]{1,0:T(8,128)}, u32[]{:S(2)}, u32[]{:S(2)}) collective-permute-start(f32[144,256]{1,0:T(8,128)S(1)} %get-tuple-element.107), channel_id=1, source_target_pairs={{0,3},{1,2},{2,1},{3,0},{4,7},{5,6},{6,5},{7,4},{8,11},{9,10},{10,... | collective-permute-start | bytes 442376 | tf_op jit(solution)/shard_map/ppermute | solution.py:32
  313.6 23.3 %all-to-all-start.1 = ((bf16[8,352,256]{2,1,0:T(8,128)(2,1)}), bf16[8,352,256]{2,1,0:T(8,128)(2,1)S(1)}, u32[]{:S(2)}, u32[]{:S(2)}) async-start(bf16[8,352,256]{2,1,0:T(8,128)(2,1)} %features_backward.1), calls=%async_computation.1 | async-start | bytes 2883584 | tf_op jit(solution)/shard_map/all_to_all | solution.py:1128
  339.8 32.2 %collective-permute-start.44 = (bf16[130,2304]{1,0:T(8,128)(2,1)}, bf16[130,2304]{1,0:T(8,128)(2,1)S(1)}, u32[]{:S(2)}, u32[]{:S(2)}) collective-permute-start(bf16[130,2304]{1,0:T(8,128)(2,1)} %get-tuple-element.78), channel_id=1, source_target_pairs={{0,1},{1,0},{3,2},{4,5},{5,4},{7,6},{8,9},{9,8},{11,10},{12,13},{1... | collective-permute-start | bytes 1797128 | tf_op jit(solution)/shard_map/ppermute | solution.py:32
  343.1 36.0 %collective-permute-start.45 = (bf16[130,2304]{1,0:T(8,128)(2,1)}, bf16[130,2304]{1,0:T(8,128)(2,1)S(1)}, u32[]{:S(2)}, u32[]{:S(2)}) collective-permute-start(bf16[130,2304]{1,0:T(8,128)(2,1)} %get-tuple-element.79), channel_id=1, source_target_pairs={{0,2},{2,0},{3,1},{4,6},{6,4},{7,5},{8,10},{10,8},{11,9},{12,14},{... | collective-permute-start | bytes 1797128 | tf_op jit(solution)/shard_map/ppermute | solution.py:32
  344.4 63.4 %collective-permute-start.46 = (bf16[130,2304]{1,0:T(8,128)(2,1)}, bf16[130,2304]{1,0:T(8,128)(2,1)S(1)}, u32[]{:S(2)}, u32[]{:S(2)}) collective-permute-start(bf16[130,2304]{1,0:T(8,128)(2,1)} %get-tuple-element.80), channel_id=1, source_target_pairs={{1,2},{2,1},{3,0},{5,6},{6,5},{7,4},{9,10},{10,9},{11,8},{13,14},{... | collective-permute-start | bytes 1797128 | tf_op jit(solution)/shard_map/ppermute | solution.py:32
  (57 other events, 815.0 us)
Sparse Core Ops, SparseCore 0:
  237.9 50.5 reduce-scatter.4
  290.9 69.4 reduce-scatter.2

commit v6 on v5

--- a/solution.py
+++ b/solution.py
@@ -409,19 +409,23 @@
     lanes = 2 * out
 
     def kernel(z_ref, *refs):
-        df_ref, act_ref, held_ref = refs[-3:]
-
-        def place(parts, wide):
-            for k in range(micro):
-                part = jnp.where(z_ref[0] < blocks, parts[k][...], jnp.zeros((), BF16))
-                held_ref[z_ref[0] ^ k, :, :wide] = part
-            return jnp.stack([held_ref[m, :, :wide] for m in range(micro)], axis=1)
+        df_ref, act_ref = refs[-2:]
+
+        def place(parts, to_ref):
+            for v in range(micro):
+
+                @pl.when(z_ref[0] == v)
+                def _():
+                    if v < blocks:
+                        to_ref[...] = jnp.stack([parts[m ^ v][...] for m in range(micro)], axis=1)
+                    else:
+                        to_ref[...] = jnp.zeros(to_ref.shape, BF16)
 
         @pl.when(pl.program_id(0) == 0)
         def _():
-            act_ref[...] = place(refs[micro : 2 * micro], out)
-
-        df_ref[...] = place(refs[:micro], lanes)
+            place(refs[micro : 2 * micro], act_ref)
+
+        place(refs[:micro], df_ref)
 
     df, act = pl.pallas_call(
         kernel,
@@ -435,7 +439,6 @@
             pl.BlockSpec((size, micro, lanes), lambda i: (0, 0, i)),
             pl.BlockSpec((size, micro, out), lambda i: (0, 0, 0)),
         ],
-        scratch_shapes=[pltpu.VMEM((micro, size, lanes), BF16)],
         compiler_params=PARAMS,
         name="interleave",
     )(z.reshape(1), *got, *got, *others)

time: 427 us -> 426 us (level)
  no operation moved by 1% of the time
where the time goes in v6:
time: 426 us; the launch traced here: 420 us
  waiting for transfers between devices  226 us (53%)
  starting transfers between devices  76.3 us (18%)
  Pallas kernels  61.3 us (14%)
  local copies, waits for them, and re-layouts  22 us (5%)
  other arithmetic  16.2 us (4%)
  between operations  15.3 us (4%)
    ppermute x43, waiting for transfers between devices, swap(): return lax.ppermute(array, axis, pairs)  178 us
    ppermute x43, starting transfers between devices, swap(): return lax.ppermute(array, axis, pairs)  47.7 us
    ppermute x7, starting transfers between devices, neighbour(): return lax.ppermute(array, 'wa', pairs)  21 us
    pallas_call x1, Pallas kernels, features_backward(): pl.pallas_call(kernel, out_shape=jax.ShapeDtypeStruct((ha, fit, deep), BF...  18.7 us
    unnamed x76, local copies, waits for them, and re-layouts  16.7 us
    pallas_call x1, Pallas kernels, weights_backward(): pl.pallas_call(kernel, out_shape=jax.ShapeDtypeStruct(shape, BF16), grid=...  14.3 us
    reduce_scatter x1, waiting for transfers between devices, local(): lax.psum_scatter(grad_proj, 'ha', scatter_dimension=0, tiled=False)  13 us
    all_to_all x1, waiting for transfers between devices, local(): back = lax.all_to_all(back, 'ha', 0, 0, tiled=True)  11.7 us
  transfers between devices with their start and end apart: 54, of which 37 were waited for; matrix products, arithmetic and copies ran while one was open for 5% of the time, Pallas kernels for 10%

profile of v6, /device:TPU:8, one launch (start us, length us, event | category | flops | bytes accessed | tf_op | source)
XLA Modules:
  0.0 419.9 jit_solution(326727244259499747)
XLA Ops:
  12.8 3.9 collective-permute-start.3
  19.3 3.2 extract.1
  26.6 5.1 %collective-permute-start.2 = (bf16[130,2304]{1,0:T(8,128)(2,1)S(1)}, bf16[130,2304]{1,0:T(8,128)(2,1)S(1)}, u32[]{:S(2)}, u32[]{:S(2)}) collective-permute-start(bf16[130,2304]{1,0:T(8,128)(2,1)S(1)} %get-tuple-element.51), channel_id=1, source_target_pairs={{0,3},{1,2},{2,1},{4,7},{5,6},{6,5},{8,11},{9,10},{10,9},{12,15},{... | collective-permute-start | bytes 1797128 | tf_op jit(solution)/shard_map/ppermute | solution.py:32
  31.7 25.0 %collective-permute-done.refs_1_ = bf16[130,2304]{1,0:T(8,128)(2,1)S(1)} collective-permute-done((bf16[130,2304]{1,0:T(8,128)(2,1)S(1)}, bf16[130,2304]{1,0:T(8,128)(2,1)S(1)}, u32[]{:S(2)}, u32[]{:S(2)}) %collective-permute-start) | collective-permute-done | bytes 599072 | tf_op jit(solution)/shard_map/ppermute | solution.py:32
  56.7 4.4 %collective-permute-start.8 = (bf16[24,64,256]{2,1,0:T(8,128)(2,1)S(1)}, bf16[24,64,256]{2,1,0:T(8,128)(2,1)}, u32[]{:S(2)}, u32[]{:S(2)}) collective-permute-start(bf16[24,64,256]{2,1,0:T(8,128)(2,1)S(1)} %collective-permute-done.6), channel_id=1, source_target_pairs={{1,0},{2,1},{5,4},{6,5},{9,8},{10,9},{13,12},{14,13},{17,16},{18,1... | collective-permute-start | bytes 2359304 | tf_op jit(solution)/shard_map/ppermute | solution.py:139
  61.1 13.9 %collective-permute-done.1.refs_2_ = bf16[130,2304]{1,0:T(8,128)(2,1)S(1)} collective-permute-done((bf16[130,2304]{1,0:T(8,128)(2,1)S(1)}, bf16[130,2304]{1,0:T(8,128)(2,1)S(1)}, u32[]{:S(2)}, u32[]{:S(2)}) %collective-permute-start.1) | collective-permute-done | bytes 599072 | tf_op jit(solution)/shard_map/ppermute | solution.py:32
  75.0 12.0 %collective-permute-done.2.refs_3_ = bf16[130,2304]{1,0:T(8,128)(2,1)S(1)} collective-permute-done((bf16[130,2304]{1,0:T(8,128)(2,1)S(1)}, bf16[130,2304]{1,0:T(8,128)(2,1)S(1)}, u32[]{:S(2)}, u32[]{:S(2)}) %collective-permute-start.2) | collective-permute-done | bytes 599072 | tf_op jit(solution)/shard_map/ppermute | solution.py:32
  87.0 5.4 %collective-permute-start.4 = (bf16[24,64,256]{2,1,0:T(8,128)(2,1)}, bf16[24,64,256]{2,1,0:T(8,128)(2,1)}, u32[]{:S(2)}, u32[]{:S(2)}) collective-permute-start(bf16[24,64,256]{2,1,0:T(8,128)(2,1)} %collective-permute-done.3), channel_id=1, source_target_pairs={{1,2},{5,6},{9,10},{13,14},{17,18},{21,22},{25,26},{29,30}} | collective-permute-start | bytes 2359304 | tf_op jit(solution)/shard_map/ppermute | solution.py:139
  95.5 3.7 all-to-all-start
  103.3 4.1 collective-permute-done.4
  111.0 7.8 %all-to-all-done.raw_ref = bf16[8,352,256]{2,1,0:T(8,128)(2,1)S(1)} async-done(((bf16[8,352,256]{2,1,0:T(8,128)(2,1)}), bf16[8,352,256]{2,1,0:T(8,128)(2,1)S(1)}, u32[]{:S(2)}, u32[]{:S(2)}) %all-to-all-start) | async-done | bytes 1441824 | tf_op jit(solution)/shard_map/all_to_all | solution.py:925
  123.8 9.1 %forward.1 = (bf16[4,4,416,256]{3,2,1,0:T(8,128)(2,1)S(1)}, bf16[4,4,416,256]{3,2,1,0:T(8,128)(2,1)S(1)}) custom-call(bf16[13,256,256]{2,1,0:T(8,128)(2,1)S(1)} %get-tuple-element.53.x_ref, bf16[24,256,256]{2,1,0:T(8,128)(2,1)S(1)} %pad_maximum_fusion.w_ref, bf16[2,256,256]{2,1,0:T(8,128)(2,1)S(1)} %get-tuple-element.130.refs_0_, ...), custom_call_target="tpu_custom_call" | custom-call | tf_op jit(solution)/shard_map/forward/pallas_call | solution.py:549
  133.0 6.0 %collective-permute-done.10 = bf16[4,4,416,256]{3,2,1,0:T(8,128)(2,1)S(1)} collective-permute-done((bf16[4,4,416,256]{3,2,1,0:T(8,128)(2,1)S(1)}, bf16[4,4,416,256]{3,2,1,0:T(8,128)(2,1)S(1)}, u32[]{:S(2)}, u32[]{:S(2)}) %collective-permute-start.10) | collective-permute-done | bytes 3407904 | tf_op jit(solution)/shard_map/ppermute | solution.py:32
  146.9 18.8 %collective-permute-done.21 = bf16[256,256]{1,0:T(8,128)(2,1)S(1)} collective-permute-done((bf16[256,256]{1,0:T(8,128)(2,1)S(1)}, bf16[256,256]{1,0:T(8,128)(2,1)S(1)}, u32[]{:S(2)}, u32[]{:S(2)}) %collective-permute-start.21) | collective-permute-done | bytes 131104 | tf_op jit(solution)/shard_map/ppermute | solution.py:32
  172.1 9.5 %collective-permute-done.12.low_last = bf16[2,416,256]{2,1,0:T(8,128)(2,1)S(1)} collective-permute-done((bf16[2,416,256]{2,1,0:T(8,128)(2,1)S(1)}, bf16[2,416,256]{2,1,0:T(8,128)(2,1)S(1)}, u32[]{:S(2)}, u32[]{:S(2)}) %collective-permute-start.12) | collective-permute-done | bytes 426016 | tf_op jit(solution)/shard_map/ppermute | solution.py:32
  224.8 9.2 %collective-permute-done.35.refs_4_ = bf16[2,416,256]{2,1,0:T(8,128)(2,1)S(1)} collective-permute-done((bf16[2,416,256]{2,1,0:T(8,128)(2,1)S(1)}, bf16[2,416,256]{2,1,0:T(8,128)(2,1)S(1)}, u32[]{:S(2)}, u32[]{:S(2)}) %collective-permute-start.35) | collective-permute-done | bytes 426016 | tf_op jit(solution)/shard_map/ppermute | solution.py:32
  238.0 15.8 %collective-permute-done.37.refs_6_ = bf16[2,2,416,256]{3,2,1,0:T(8,128)(2,1)} collective-permute-done((bf16[2,2,416,256]{3,2,1,0:T(8,128)(2,1)}, bf16[2,2,416,256]{3,2,1,0:T(8,128)(2,1)}, u32[]{:S(2)}, u32[]{:S(2)}) %collective-permute-start.37) | collective-permute-done | bytes 852000 | tf_op jit(solution)/shard_map/ppermute | solution.py:32
  256.5 2.9 collective-permute-done.40.refs_9_
  260.2 14.3 %weights_backward.1 = bf16[4,22,64,256]{3,2,1,0:T(8,128)(2,1)} custom-call(bf16[13,256,256]{2,1,0:T(8,128)(2,1)} %copy-done.7, bf16[2,256,256]{2,1,0:T(8,128)(2,1)} %copy-done.8, bf16[2,256,256]{2,1,0:T(8,128)(2,1)} %get-tuple-element.131.refs_1_, bf16[2,256,256]{2,1,0:T(8,128)(2,1)} %add_convert_fusion.2.refs_2_, bf16[4,416,256]{2,1,0:T(8,128)(2,1)} %copy-done.6, ...), custom_call_target="tpu_custom_call" | custom-call | tf_op jit(solution)/shard_map/weights_backward/pallas_call | solution.py:621
  275.6 13.0 %reduce-scatter.5.cloned.1.call-done = bf16[1,256,256]{2,1,0:T(8,128)(2,1)} async-done(((bf16[8,256,256]{2,1,0:T(8,128)(2,1)}), bf16[1,256,256]{2,1,0:T(8,128)(2,1)}) %reduce-scatter.5.cloned.1.call-update) | async-done | bytes 131088 | tf_op jit(solution)/shard_map/reduce_scatter | solution.py:1113
  294.8 18.7 %features_backward.1 = bf16[8,352,256]{2,1,0:T(8,128)(2,1)} custom-call(s32[1]{0:T(128)} %bitcast.1.h_ref, f32[256,256]{1,0:T(8,128)} %fusion.21.start_ref, bf16[24,256,256]{2,1,0:T(8,128)(2,1)} %copy-done.2, bf16[352,512]{1,0:T(8,128)(2,1)} %constant.110.clone.place_ref, bf16[2,256,256]{2,1,0:T(8,128)(2,1)} %copy-done.8, ...), custom_call_target="tpu_custom_call" | custom-call | tf_op jit(solution)/shard_map/features_backward/pallas_call | solution.py:673
  313.6 3.7 all-to-all-start.1
  317.9 3.6 collective-permute-done.49
  325.1 11.7 %all-to-all-done.1.pieces_ref = bf16[8,352,256]{2,1,0:T(8,128)(2,1)S(1)} async-done(((bf16[8,352,256]{2,1,0:T(8,128)(2,1)}), bf16[8,352,256]{2,1,0:T(8,128)(2,1)S(1)}, u32[]{:S(2)}, u32[]{:S(2)}) %all-to-all-start.1) | async-done | bytes 1441824 | tf_op jit(solution)/shard_map/all_to_all | solution.py:1131
  336.9 2.9 unchoose.1
  339.8 3.3 collective-permute-start.44
  344.4 4.6 %collective-permute-start.46 = (bf16[130,2304]{1,0:T(8,128)(2,1)}, bf16[130,2304]{1,0:T(8,128)(2,1)S(1)}, u32[]{:S(2)}, u32[]{:S(2)}) collective-permute-start(bf16[130,2304]{1,0:T(8,128)(2,1)} %get-tuple-element.80), channel_id=1, source_target_pairs={{1,2},{2,1},{3,0},{5,6},{6,5},{7,4},{9,10},{10,9},{11,8},{13,14},{... | collective-permute-start | bytes 1797128 | tf_op jit(solution)/shard_map/ppermute | solution.py:32
  349.0 11.4 %reduce-scatter.3.cloned.1.call-done = bf16[1,22,64,256]{3,2,1,0:T(8,128)(2,1)} async-done(((bf16[4,22,64,256]{3,2,1,0:T(8,128)(2,1)}), bf16[1,22,64,256]{3,2,1,0:T(8,128)(2,1)}) %reduce-scatter.3.cloned.1.call-update) | async-done | bytes 720912 | tf_op jit(solution)/shard_map/reduce_scatter | solution.py:172
  369.0 2.9 collective-permute-done.44.refs_1_.refs_5_
  372.0 7.1 %collective-permute-done.45.refs_2_.refs_6_ = bf16[130,2304]{1,0:T(8,128)(2,1)S(1)} collective-permute-done((bf16[130,2304]{1,0:T(8,128)(2,1)}, bf16[130,2304]{1,0:T(8,128)(2,1)S(1)}, u32[]{:S(2)}, u32[]{:S(2)}) %collective-permute-start.45) | collective-permute-done | bytes 599072 | tf_op jit(solution)/shard_map/ppermute | solution.py:32
  379.1 28.6 %collective-permute-done.46.refs_3_.refs_7_ = bf16[130,2304]{1,0:T(8,128)(2,1)S(1)} collective-permute-done((bf16[130,2304]{1,0:T(8,128)(2,1)}, bf16[130,2304]{1,0:T(8,128)(2,1)S(1)}, u32[]{:S(2)}, u32[]{:S(2)}) %collective-permute-start.46) | collective-permute-done | bytes 599072 | tf_op jit(solution)/shard_map/ppermute | solution.py:32
  407.7 5.1 %interleave.1 = (bf16[130,4,2048]{2,1,0:T(4,128)(2,1)}, bf16[130,4,256]{2,1,0:T(4,128)(2,1)}) custom-call(s32[1]{0:T(128)} %bitcast.z_ref, bf16[130,2304]{1,0:T(8,128)(2,1)S(1)} %get-tuple-element.77.refs_0_.refs_4_, bf16[130,2304]{1,0:T(8,128)(2,1)S(1)} %collective-permute-done.44.refs_1_.refs_5_, ...), custom_call_target="tpu_custom_call" | custom-call | tf_op jit(solution)/shard_map/interleave/pallas_call | solution.py:430
  (226 shorter events, 113.7 us)
Async XLA Ops:
  10.7 46.0 %collective-permute-start.6 = (bf16[24,64,256]{2,1,0:T(8,128)(2,1)S(1)}, bf16[24,64,256]{2,1,0:T(8,128)(2,1)S(1)}, u32[]{:S(2)}, u32[]{:S(2)}) collective-permute-start(bf16[24,64,256]{2,1,0:T(8,128)(2,1)S(1)} %pack_weights.1), channel_id=1, source_target_pairs={{1,0},{2,1},{3,2},{5,4},{6,5},{7,6},{9,8},{10,9},{11,10},{13,12},{... | collective-permute-start | bytes 2359304 | tf_op jit(solution)/shard_map/ppermute | solution.py:139
  12.8 74.2 %collective-permute-start.3 = (bf16[24,64,256]{2,1,0:T(8,128)(2,1)S(1)}, bf16[24,64,256]{2,1,0:T(8,128)(2,1)}, u32[]{:S(2)}, u32[]{:S(2)}) collective-permute-start(bf16[24,64,256]{2,1,0:T(8,128)(2,1)S(1)} %pack_weights.1), channel_id=1, source_target_pairs={{0,1},{1,2},{2,3},{4,5},{5,6},{6,7},{8,9},{9,10},{10,11},{12,13},{... | collective-permute-start | bytes 2359304 | tf_op jit(solution)/shard_map/ppermute | solution.py:139
  22.4 34.2 %collective-permute-start = (bf16[130,2304]{1,0:T(8,128)(2,1)S(1)}, bf16[130,2304]{1,0:T(8,128)(2,1)S(1)}, u32[]{:S(2)}, u32[]{:S(2)}) collective-permute-start(bf16[130,2304]{1,0:T(8,128)(2,1)S(1)} %get-tuple-element.49), channel_id=1, source_target_pairs={{0,1},{1,0},{2,3},{4,5},{5,4},{6,7},{8,9},{9,8},{10,11},{12,13},{1... | collective-permute-start | bytes 1797128 | tf_op jit(solution)/shard_map/ppermute | solution.py:32
  25.2 49.8 %collective-permute-start.1 = (bf16[130,2304]{1,0:T(8,128)(2,1)S(1)}, bf16[130,2304]{1,0:T(8,128)(2,1)S(1)}, u32[]{:S(2)}, u32[]{:S(2)}) collective-permute-start(bf16[130,2304]{1,0:T(8,128)(2,1)S(1)} %get-tuple-element.50), channel_id=1, source_target_pairs={{0,2},{1,3},{2,0},{4,6},{5,7},{6,4},{8,10},{9,11},{10,8},{12,14},{... | collective-permute-start | bytes 1797128 | tf_op jit(solution)/shard_map/ppermute | solution.py:32
  26.6 60.4 %collective-permute-start.2 = (bf16[130,2304]{1,0:T(8,128)(2,1)S(1)}, bf16[130,2304]{1,0:T(8,128)(2,1)S(1)}, u32[]{:S(2)}, u32[]{:S(2)}) collective-permute-start(bf16[130,2304]{1,0:T(8,128)(2,1)S(1)} %get-tuple-element.51), channel_id=1, source_target_pairs={{0,3},{1,2},{2,1},{4,7},{5,6},{6,5},{8,11},{9,10},{10,9},{12,15},{... | collective-permute-start | bytes 1797128 | tf_op jit(solution)/shard_map/ppermute | solution.py:32
  56.7 44.4 %collective-permute-start.8 = (bf16[24,64,256]{2,1,0:T(8,128)(2,1)S(1)}, bf16[24,64,256]{2,1,0:T(8,128)(2,1)}, u32[]{:S(2)}, u32[]{:S(2)}) collective-permute-start(bf16[24,64,256]{2,1,0:T(8,128)(2,1)S(1)} %collective-permute-done.6), channel_id=1, source_target_pairs={{1,0},{2,1},{5,4},{6,5},{9,8},{10,9},{13,12},{14,13},{17,16},{18,1... | collective-permute-start | bytes 2359304 | tf_op jit(solution)/shard_map/ppermute | solution.py:139
  87.0 20.4 %collective-permute-start.4 = (bf16[24,64,256]{2,1,0:T(8,128)(2,1)}, bf16[24,64,256]{2,1,0:T(8,128)(2,1)}, u32[]{:S(2)}, u32[]{:S(2)}) collective-permute-start(bf16[24,64,256]{2,1,0:T(8,128)(2,1)} %collective-permute-done.3), channel_id=1, source_target_pairs={{1,2},{5,6},{9,10},{13,14},{17,18},{21,22},{25,26},{29,30}} | collective-permute-start | bytes 2359304 | tf_op jit(solution)/shard_map/ppermute | solution.py:139
  95.5 23.3 %all-to-all-start = ((bf16[8,352,256]{2,1,0:T(8,128)(2,1)}), bf16[8,352,256]{2,1,0:T(8,128)(2,1)S(1)}, u32[]{:S(2)}, u32[]{:S(2)}) async-start(bf16[8,352,256]{2,1,0:T(8,128)(2,1)} %copy-done.12), calls=%async_computation | async-start | bytes 2883584 | tf_op jit(solution)/shard_map/all_to_all | solution.py:925
  99.2 189.4 %reduce-scatter.5.cloned.1.call-start = ((), (), s32[]{:S(2)}) async-start(), calls=%async_computation.5 | async-start | bytes 1179648 | tf_op jit(solution)/shard_map/reduce_scatter | solution.py:1113
  99.6 20.3 %collective-permute-start.7 = (bf16[24,64,256]{2,1,0:T(8,128)(2,1)}, bf16[24,64,256]{2,1,0:T(8,128)(2,1)}, u32[]{:S(2)}, u32[]{:S(2)}) collective-permute-start(bf16[24,64,256]{2,1,0:T(8,128)(2,1)} %collective-permute-done.3), channel_id=1, source_target_pairs={{2,3},{6,7},{10,11},{14,15},{18,19},{22,23},{26,27},{30,31}} | collective-permute-start | bytes 2359304 | tf_op jit(solution)/shard_map/ppermute | solution.py:139
  101.1 19.2 %collective-permute-start.9 = (bf16[24,64,256]{2,1,0:T(8,128)(2,1)}, bf16[24,64,256]{2,1,0:T(8,128)(2,1)}, u32[]{:S(2)}, u32[]{:S(2)}) collective-permute-start(bf16[24,64,256]{2,1,0:T(8,128)(2,1)} %collective-permute-done.8), channel_id=1, source_target_pairs={{1,0},{5,4},{9,8},{13,12},{17,16},{21,20},{25,24},{29,28}} | collective-permute-start | bytes 2359304 | tf_op jit(solution)/shard_map/ppermute | solution.py:139
  107.4 13.0 %collective-permute-start.5 = (bf16[24,64,256]{2,1,0:T(8,128)(2,1)}, bf16[24,64,256]{2,1,0:T(8,128)(2,1)}, u32[]{:S(2)}, u32[]{:S(2)}) collective-permute-start(bf16[24,64,256]{2,1,0:T(8,128)(2,1)} %collective-permute-done.4), channel_id=1, source_target_pairs={{2,3},{6,7},{10,11},{14,15},{18,19},{22,23},{26,27},{30,31}} | collective-permute-start | bytes 2359304 | tf_op jit(solution)/shard_map/ppermute | solution.py:139
  140.0 29.1 %collective-permute-start.11 = (bf16[2,2,416,256]{3,2,1,0:T(8,128)(2,1)S(1)}, bf16[2,2,416,256]{3,2,1,0:T(8,128)(2,1)S(1)}, u32[]{:S(2)}, u32[]{:S(2)}) collective-permute-start(bf16[2,2,416,256]{3,2,1,0:T(8,128)(2,1)S(1)} %slice.126), channel_id=1, source_target_pairs={{0,8},{4,12},{8,0},{12,4},{16,24},{20,28},{24,16},{28,20},{1,9},{5... | collective-permute-start | bytes 2555912 | tf_op jit(solution)/shard_map/ppermute | solution.py:32
  141.8 29.0 %collective-permute-start.13 = (bf16[2,2,416,256]{3,2,1,0:T(8,128)(2,1)S(1)}, bf16[2,2,416,256]{3,2,1,0:T(8,128)(2,1)S(1)}, u32[]{:S(2)}, u32[]{:S(2)}) collective-permute-start(bf16[2,2,416,256]{3,2,1,0:T(8,128)(2,1)S(1)} %slice.222), channel_id=1, source_target_pairs={{0,16},{4,20},{8,24},{12,28},{16,0},{20,4},{24,8},{28,12},{1,17},{... | collective-permute-start | bytes 2555912 | tf_op jit(solution)/shard_map/ppermute | solution.py:32
  143.4 22.3 %collective-permute-start.21 = (bf16[256,256]{1,0:T(8,128)(2,1)S(1)}, bf16[256,256]{1,0:T(8,128)(2,1)S(1)}, u32[]{:S(2)}, u32[]{:S(2)}) collective-permute-start(bf16[256,256]{1,0:T(8,128)(2,1)S(1)} %get-tuple-element.94), channel_id=1, source_target_pairs={{0,24},{4,28},{8,16},{12,20},{16,8},{20,12},{24,0},{28,4},{1,25},{... | collective-permute-start | bytes 393224 | tf_op jit(solution)/shard_map/ppermute | solution.py:32
  143.9 24.3 %collective-permute-start.20 = (bf16[256,256]{1,0:T(8,128)(2,1)S(1)}, bf16[256,256]{1,0:T(8,128)(2,1)S(1)}, u32[]{:S(2)}, u32[]{:S(2)}) collective-permute-start(bf16[256,256]{1,0:T(8,128)(2,1)S(1)} %get-tuple-element.94), channel_id=1, source_target_pairs={{0,16},{4,20},{8,24},{12,28},{16,0},{20,4},{24,8},{28,12},{1,17},{... | collective-permute-start | bytes 393224 | tf_op jit(solution)/shard_map/ppermute | solution.py:32
  145.5 22.8 %collective-permute-start.19 = (bf16[256,256]{1,0:T(8,128)(2,1)S(1)}, bf16[256,256]{1,0:T(8,128)(2,1)S(1)}, u32[]{:S(2)}, u32[]{:S(2)}) collective-permute-start(bf16[256,256]{1,0:T(8,128)(2,1)S(1)} %get-tuple-element.94), channel_id=1, source_target_pairs={{0,8},{4,12},{8,0},{12,4},{16,24},{20,28},{24,16},{28,20},{1,9},{5... | collective-permute-start | bytes 393224 | tf_op jit(solution)/shard_map/ppermute | solution.py:32
  169.1 20.4 %collective-permute-start.22 = (bf16[4,256,256]{2,1,0:T(8,128)(2,1)}, bf16[4,256,256]{2,1,0:T(8,128)(2,1)}, u32[]{:S(2)}, u32[]{:S(2)}) collective-permute-start(bf16[4,256,256]{2,1,0:T(8,128)(2,1)} %pad_maximum_fusion.4.near_ref), channel_id=1, source_target_pairs={{0,4},{4,0},{8,12},{12,8},{16,20},{20,16},{24,28},{28,24},{1,5},{5... | collective-permute-start | bytes 1572872 | tf_op jit(solution)/shard_map/ppermute | solution.py:32
  169.3 12.3 %collective-permute-start.12 = (bf16[2,416,256]{2,1,0:T(8,128)(2,1)S(1)}, bf16[2,416,256]{2,1,0:T(8,128)(2,1)S(1)}, u32[]{:S(2)}, u32[]{:S(2)}) collective-permute-start(bf16[2,416,256]{2,1,0:T(8,128)(2,1)S(1)} %get-tuple-element.91), channel_id=1, source_target_pairs={{0,16},{4,20},{8,24},{12,28},{16,0},{20,4},{24,8},{28,12},{1,17},{... | collective-permute-start | bytes 1277960 | tf_op jit(solution)/shard_map/ppermute | solution.py:32
  171.0 12.0 %collective-permute-start.14 = (bf16[2,416,256]{2,1,0:T(8,128)(2,1)S(1)}, bf16[2,416,256]{2,1,0:T(8,128)(2,1)S(1)}, u32[]{:S(2)}, u32[]{:S(2)}) collective-permute-start(bf16[2,416,256]{2,1,0:T(8,128)(2,1)S(1)} %get-tuple-element.89), channel_id=1, source_target_pairs={{0,8},{4,12},{8,0},{12,4},{16,24},{20,28},{24,16},{28,20},{1,9},{5... | collective-permute-start | bytes 1277960 | tf_op jit(solution)/shard_map/ppermute | solution.py:32
  224.3 11.4 %collective-permute-start.36 = (bf16[2,416,256]{2,1,0:T(8,128)(2,1)S(1)}, bf16[2,416,256]{2,1,0:T(8,128)(2,1)S(1)}, u32[]{:S(2)}, u32[]{:S(2)}) collective-permute-start(bf16[2,416,256]{2,1,0:T(8,128)(2,1)S(1)} %get-tuple-element.103), channel_id=1, source_target_pairs={{0,16},{4,20},{8,24},{12,28},{16,0},{20,4},{24,8},{28,12},{1,17},{... | collective-permute-start | bytes 1277960 | tf_op jit(solution)/shard_map/ppermute | solution.py:32
  235.0 18.7 %collective-permute-start.37 = (bf16[2,2,416,256]{3,2,1,0:T(8,128)(2,1)}, bf16[2,2,416,256]{3,2,1,0:T(8,128)(2,1)}, u32[]{:S(2)}, u32[]{:S(2)}) collective-permute-start(bf16[2,2,416,256]{3,2,1,0:T(8,128)(2,1)} %pad_maximum_fusion.2), channel_id=1, source_target_pairs={{0,16},{4,20},{8,24},{12,28},{16,0},{20,4},{24,8},{28,12},{1,17},{... | collective-permute-start | bytes 2555912 | tf_op jit(solution)/shard_map/ppermute | solution.py:32
  237.4 18.5 %collective-permute-start.38 = (bf16[2,2,416,256]{3,2,1,0:T(8,128)(2,1)}, bf16[2,2,416,256]{3,2,1,0:T(8,128)(2,1)}, u32[]{:S(2)}, u32[]{:S(2)}) collective-permute-start(bf16[2,2,416,256]{3,2,1,0:T(8,128)(2,1)} %pad_maximum_fusion.3), channel_id=1, source_target_pairs={{0,8},{4,12},{8,0},{12,4},{16,24},{20,28},{24,16},{28,20},{1,9},{5... | collective-permute-start | bytes 2555912 | tf_op jit(solution)/shard_map/ppermute | solution.py:32
  237.8 122.6 %reduce-scatter.3.cloned.1.call-start = ((), (), s32[]{:S(2)}) async-start(), calls=%async_computation.4 | async-start | bytes 3604480 | tf_op jit(solution)/shard_map/reduce_scatter | solution.py:172
  237.9 18.6 %collective-permute-start.39 = (bf16[4,416,256]{2,1,0:T(8,128)(2,1)}, bf16[4,416,256]{2,1,0:T(8,128)(2,1)}, u32[]{:S(2)}, u32[]{:S(2)}) collective-permute-start(bf16[4,416,256]{2,1,0:T(8,128)(2,1)} %copy-done.6), channel_id=1, source_target_pairs={{0,4},{4,0},{8,12},{12,8},{16,20},{20,16},{24,28},{28,24},{1,5},{5... | collective-permute-start | bytes 2555912 | tf_op jit(solution)/shard_map/ppermute | solution.py:32
  290.3 27.6 %collective-permute-start.47 = (f32[144,256]{1,0:T(8,128)}, f32[144,256]{1,0:T(8,128)}, u32[]{:S(2)}, u32[]{:S(2)}) collective-permute-start(f32[144,256]{1,0:T(8,128)} %get-tuple-element.108), channel_id=1, source_target_pairs={{0,1},{1,0},{2,3},{3,2},{4,5},{5,4},{6,7},{7,6},{8,9},{9,8},{10,11... | collective-permute-start | bytes 442376 | tf_op jit(solution)/shard_map/ppermute | solution.py:32
  290.9 27.1 %collective-permute-start.48 = (f32[144,256]{1,0:T(8,128)}, f32[144,256]{1,0:T(8,128)}, u32[]{:S(2)}, u32[]{:S(2)}) collective-permute-start(f32[144,256]{1,0:T(8,128)} %get-tuple-element.109), channel_id=1, source_target_pairs={{0,2},{1,3},{2,0},{3,1},{4,6},{5,7},{6,4},{7,5},{8,10},{9,11},{10,... | collective-permute-start | bytes 442376 | tf_op jit(solution)/shard_map/ppermute | solution.py:32
  293.3 28.3 %collective-permute-start.49 = (f32[144,256]{1,0:T(8,128)S(1)}, f32[144,256]{1,0:T(8,128)}, u32[]{:S(2)}, u32[]{:S(2)}) collective-permute-start(f32[144,256]{1,0:T(8,128)S(1)} %get-tuple-element.107), channel_id=1, source_target_pairs={{0,3},{1,2},{2,1},{3,0},{4,7},{5,6},{6,5},{7,4},{8,11},{9,10},{10,... | collective-permute-start | bytes 442376 | tf_op jit(solution)/shard_map/ppermute | solution.py:32
  313.6 23.3 %all-to-all-start.1 = ((bf16[8,352,256]{2,1,0:T(8,128)(2,1)}), bf16[8,352,256]{2,1,0:T(8,128)(2,1)S(1)}, u32[]{:S(2)}, u32[]{:S(2)}) async-start(bf16[8,352,256]{2,1,0:T(8,128)(2,1)} %features_backward.1), calls=%async_computation.1 | async-start | bytes 2883584 | tf_op jit(solution)/shard_map/all_to_all | solution.py:1131
  339.8 32.2 %collective-permute-start.44 = (bf16[130,2304]{1,0:T(8,128)(2,1)}, bf16[130,2304]{1,0:T(8,128)(2,1)S(1)}, u32[]{:S(2)}, u32[]{:S(2)}) collective-permute-start(bf16[130,2304]{1,0:T(8,128)(2,1)} %get-tuple-element.78), channel_id=1, source_target_pairs={{0,1},{1,0},{3,2},{4,5},{5,4},{7,6},{8,9},{9,8},{11,10},{12,13},{1... | collective-permute-start | bytes 1797128 | tf_op jit(solution)/shard_map/ppermute | solution.py:32
  343.1 36.0 %collective-permute-start.45 = (bf16[130,2304]{1,0:T(8,128)(2,1)}, bf16[130,2304]{1,0:T(8,128)(2,1)S(1)}, u32[]{:S(2)}, u32[]{:S(2)}) collective-permute-start(bf16[130,2304]{1,0:T(8,128)(2,1)} %get-tuple-element.79), channel_id=1, source_target_pairs={{0,2},{2,0},{3,1},{4,6},{6,4},{7,5},{8,10},{10,8},{11,9},{12,14},{... | collective-permute-start | bytes 1797128 | tf_op jit(solution)/shard_map/ppermute | solution.py:32
  344.4 63.4 %collective-permute-start.46 = (bf16[130,2304]{1,0:T(8,128)(2,1)}, bf16[130,2304]{1,0:T(8,128)(2,1)S(1)}, u32[]{:S(2)}, u32[]{:S(2)}) collective-permute-start(bf16[130,2304]{1,0:T(8,128)(2,1)} %get-tuple-element.80), channel_id=1, source_target_pairs={{1,2},{2,1},{3,0},{5,6},{6,5},{7,4},{9,10},{10,9},{11,8},{13,14},{... | collective-permute-start | bytes 1797128 | tf_op jit(solution)/shard_map/ppermute | solution.py:32
  (57 other events, 813.6 us)
Sparse Core Ops, SparseCore 0:
  237.9 50.5 reduce-scatter.4
  290.9 69.4 reduce-scatter.2

commit v7 on v6

--- a/solution.py
+++ b/solution.py
@@ -406,7 +406,7 @@
     micro = len(got)
     size, channels = got[0].shape
     channels -= out
-    lanes = 2 * out
+    lanes = 4 * out
 
     def kernel(z_ref, *refs):
         df_ref, act_ref = refs[-2:]
@@ -663,7 +663,7 @@
                     else:
                         total_ref[pl.ds(w, count)] = part + start_ref[...][None]
 
-                in_steps(*span(-b, rate, valid), 4, columns)
+                in_steps(*span(-b, rate, valid), 7, columns)
         held_ref[valid * prows :] = jnp.zeros((high - valid * prows, deep), BF16)
         for k in range(ha):
             block = total_ref[:, k * prows : (k + 1) * prows, :].astype(BF16)

time: 426 us -> 425 us (level)
  no operation moved by 1% of the time
where the time goes in v7:
time: 425 us; the launch traced here: 419 us
  waiting for transfers between devices  227 us (53%)
  starting transfers between devices  76.3 us (18%)
  Pallas kernels  60.7 us (14%)
  local copies, waits for them, and re-layouts  22 us (5%)
  other arithmetic  16.2 us (4%)
  between operations  15.3 us (4%)
    ppermute x43, waiting for transfers between devices, swap(): return lax.ppermute(array, axis, pairs)  178 us
    ppermute x43, starting transfers between devices, swap(): return lax.ppermute(array, axis, pairs)  47.7 us
    ppermute x7, starting transfers between devices, neighbour(): return lax.ppermute(array, 'wa', pairs)  21 us
    pallas_call x1, Pallas kernels, features_backward(): pl.pallas_call(kernel, out_shape=jax.ShapeDtypeStruct((ha, fit, deep), BF...  18.5 us
    unnamed x76, local copies, waits for them, and re-layouts  16.7 us
    pallas_call x1, Pallas kernels, weights_backward(): pl.pallas_call(kernel, out_shape=jax.ShapeDtypeStruct(shape, BF16), grid=...  14.3 us
    reduce_scatter x1, waiting for transfers between devices, local(): lax.psum_scatter(grad_proj, 'ha', scatter_dimension=0, tiled=False)  13 us
    reduce_scatter x1, waiting for transfers between devices, line_scatter(): lax.psum_scatter(parts, 'wa', scatter_dimension=0, tiled=False).astype(F32)  11.8 us
  transfers between devices with their start and end apart: 54, of which 37 were waited for; matrix products, arithmetic and copies ran while one was open for 5% of the time, Pallas kernels for 10%

profile of v7, /device:TPU:8, one launch (start us, length us, event | category | flops | bytes accessed | tf_op | source)
XLA Modules:
  0.0 419.5 jit_solution(16829038427638112034)
XLA Ops:
  12.8 3.9 collective-permute-start.3
  19.3 3.2 extract.1
  22.4 2.8 collective-permute-start
  26.6 5.1 %collective-permute-start.2 = (bf16[130,2304]{1,0:T(8,128)(2,1)S(1)}, bf16[130,2304]{1,0:T(8,128)(2,1)S(1)}, u32[]{:S(2)}, u32[]{:S(2)}) collective-permute-start(bf16[130,2304]{1,0:T(8,128)(2,1)S(1)} %get-tuple-element.51), channel_id=1, source_target_pairs={{0,3},{1,2},{2,1},{4,7},{5,6},{6,5},{8,11},{9,10},{10,9},{12,15},{... | collective-permute-start | bytes 1797128 | tf_op jit(solution)/shard_map/ppermute | solution.py:32
  31.7 25.0 %collective-permute-done.refs_1_ = bf16[130,2304]{1,0:T(8,128)(2,1)S(1)} collective-permute-done((bf16[130,2304]{1,0:T(8,128)(2,1)S(1)}, bf16[130,2304]{1,0:T(8,128)(2,1)S(1)}, u32[]{:S(2)}, u32[]{:S(2)}) %collective-permute-start) | collective-permute-done | bytes 599072 | tf_op jit(solution)/shard_map/ppermute | solution.py:32
  56.7 4.4 %collective-permute-start.8 = (bf16[24,64,256]{2,1,0:T(8,128)(2,1)S(1)}, bf16[24,64,256]{2,1,0:T(8,128)(2,1)}, u32[]{:S(2)}, u32[]{:S(2)}) collective-permute-start(bf16[24,64,256]{2,1,0:T(8,128)(2,1)S(1)} %collective-permute-done.6), channel_id=1, source_target_pairs={{1,0},{2,1},{5,4},{6,5},{9,8},{10,9},{13,12},{14,13},{17,16},{18,1... | collective-permute-start | bytes 2359304 | tf_op jit(solution)/shard_map/ppermute | solution.py:139
  61.1 13.9 %collective-permute-done.1.refs_2_ = bf16[130,2304]{1,0:T(8,128)(2,1)S(1)} collective-permute-done((bf16[130,2304]{1,0:T(8,128)(2,1)S(1)}, bf16[130,2304]{1,0:T(8,128)(2,1)S(1)}, u32[]{:S(2)}, u32[]{:S(2)}) %collective-permute-start.1) | collective-permute-done | bytes 599072 | tf_op jit(solution)/shard_map/ppermute | solution.py:32
  75.0 12.0 %collective-permute-done.2.refs_3_ = bf16[130,2304]{1,0:T(8,128)(2,1)S(1)} collective-permute-done((bf16[130,2304]{1,0:T(8,128)(2,1)S(1)}, bf16[130,2304]{1,0:T(8,128)(2,1)S(1)}, u32[]{:S(2)}, u32[]{:S(2)}) %collective-permute-start.2) | collective-permute-done | bytes 599072 | tf_op jit(solution)/shard_map/ppermute | solution.py:32
  87.0 5.4 %collective-permute-start.4 = (bf16[24,64,256]{2,1,0:T(8,128)(2,1)}, bf16[24,64,256]{2,1,0:T(8,128)(2,1)}, u32[]{:S(2)}, u32[]{:S(2)}) collective-permute-start(bf16[24,64,256]{2,1,0:T(8,128)(2,1)} %collective-permute-done.3), channel_id=1, source_target_pairs={{1,2},{5,6},{9,10},{13,14},{17,18},{21,22},{25,26},{29,30}} | collective-permute-start | bytes 2359304 | tf_op jit(solution)/shard_map/ppermute | solution.py:139
  95.5 3.7 all-to-all-start
  103.3 4.1 collective-permute-done.4
  111.0 7.8 %all-to-all-done.raw_ref = bf16[8,352,256]{2,1,0:T(8,128)(2,1)S(1)} async-done(((bf16[8,352,256]{2,1,0:T(8,128)(2,1)}), bf16[8,352,256]{2,1,0:T(8,128)(2,1)S(1)}, u32[]{:S(2)}, u32[]{:S(2)}) %all-to-all-start) | async-done | bytes 1441824 | tf_op jit(solution)/shard_map/all_to_all | solution.py:925
  123.8 9.1 %forward.1 = (bf16[4,4,416,256]{3,2,1,0:T(8,128)(2,1)S(1)}, bf16[4,4,416,256]{3,2,1,0:T(8,128)(2,1)S(1)}) custom-call(bf16[13,256,256]{2,1,0:T(8,128)(2,1)S(1)} %get-tuple-element.53.x_ref, bf16[24,256,256]{2,1,0:T(8,128)(2,1)S(1)} %pad_maximum_fusion.w_ref, bf16[2,256,256]{2,1,0:T(8,128)(2,1)S(1)} %get-tuple-element.130.refs_0_, ...), custom_call_target="tpu_custom_call" | custom-call | tf_op jit(solution)/shard_map/forward/pallas_call | solution.py:549
  133.0 6.0 %collective-permute-done.10 = bf16[4,4,416,256]{3,2,1,0:T(8,128)(2,1)S(1)} collective-permute-done((bf16[4,4,416,256]{3,2,1,0:T(8,128)(2,1)S(1)}, bf16[4,4,416,256]{3,2,1,0:T(8,128)(2,1)S(1)}, u32[]{:S(2)}, u32[]{:S(2)}) %collective-permute-start.10) | collective-permute-done | bytes 3407904 | tf_op jit(solution)/shard_map/ppermute | solution.py:32
  146.9 18.8 %collective-permute-done.21 = bf16[256,256]{1,0:T(8,128)(2,1)S(1)} collective-permute-done((bf16[256,256]{1,0:T(8,128)(2,1)S(1)}, bf16[256,256]{1,0:T(8,128)(2,1)S(1)}, u32[]{:S(2)}, u32[]{:S(2)}) %collective-permute-start.21) | collective-permute-done | bytes 131104 | tf_op jit(solution)/shard_map/ppermute | solution.py:32
  172.1 9.5 %collective-permute-done.12.low_last = bf16[2,416,256]{2,1,0:T(8,128)(2,1)S(1)} collective-permute-done((bf16[2,416,256]{2,1,0:T(8,128)(2,1)S(1)}, bf16[2,416,256]{2,1,0:T(8,128)(2,1)S(1)}, u32[]{:S(2)}, u32[]{:S(2)}) %collective-permute-start.12) | collective-permute-done | bytes 426016 | tf_op jit(solution)/shard_map/ppermute | solution.py:32
  224.7 9.2 %collective-permute-done.35.refs_4_ = bf16[2,416,256]{2,1,0:T(8,128)(2,1)S(1)} collective-permute-done((bf16[2,416,256]{2,1,0:T(8,128)(2,1)S(1)}, bf16[2,416,256]{2,1,0:T(8,128)(2,1)S(1)}, u32[]{:S(2)}, u32[]{:S(2)}) %collective-permute-start.35) | collective-permute-done | bytes 426016 | tf_op jit(solution)/shard_map/ppermute | solution.py:32
  237.9 15.8 %collective-permute-done.37.refs_6_ = bf16[2,2,416,256]{3,2,1,0:T(8,128)(2,1)} collective-permute-done((bf16[2,2,416,256]{3,2,1,0:T(8,128)(2,1)}, bf16[2,2,416,256]{3,2,1,0:T(8,128)(2,1)}, u32[]{:S(2)}, u32[]{:S(2)}) %collective-permute-start.37) | collective-permute-done | bytes 852000 | tf_op jit(solution)/shard_map/ppermute | solution.py:32
  256.4 2.9 collective-permute-done.40.refs_9_
  260.1 14.3 %weights_backward.1 = bf16[4,22,64,256]{3,2,1,0:T(8,128)(2,1)} custom-call(bf16[13,256,256]{2,1,0:T(8,128)(2,1)} %copy-done.7, bf16[2,256,256]{2,1,0:T(8,128)(2,1)} %copy-done.8, bf16[2,256,256]{2,1,0:T(8,128)(2,1)} %get-tuple-element.131.refs_1_, bf16[2,256,256]{2,1,0:T(8,128)(2,1)} %add_convert_fusion.2.refs_2_, bf16[4,416,256]{2,1,0:T(8,128)(2,1)} %copy-done.6, ...), custom_call_target="tpu_custom_call" | custom-call | tf_op jit(solution)/shard_map/weights_backward/pallas_call | solution.py:621
  275.5 13.0 %reduce-scatter.5.cloned.1.call-done = bf16[1,256,256]{2,1,0:T(8,128)(2,1)} async-done(((bf16[8,256,256]{2,1,0:T(8,128)(2,1)}), bf16[1,256,256]{2,1,0:T(8,128)(2,1)}) %reduce-scatter.5.cloned.1.call-update) | async-done | bytes 131088 | tf_op jit(solution)/shard_map/reduce_scatter | solution.py:1113
  294.8 18.5 %features_backward.1 = bf16[8,352,256]{2,1,0:T(8,128)(2,1)} custom-call(s32[1]{0:T(128)} %bitcast.1.h_ref, f32[256,256]{1,0:T(8,128)} %fusion.21.start_ref, bf16[24,256,256]{2,1,0:T(8,128)(2,1)} %copy-done.2, bf16[352,512]{1,0:T(8,128)(2,1)} %constant.110.clone.place_ref, bf16[2,256,256]{2,1,0:T(8,128)(2,1)} %copy-done.8, ...), custom_call_target="tpu_custom_call" | custom-call | tf_op jit(solution)/shard_map/features_backward/pallas_call | solution.py:673
  313.3 3.7 all-to-all-start.1
  317.6 3.9 collective-permute-done.49
  325.1 11.5 %all-to-all-done.1.pieces_ref = bf16[8,352,256]{2,1,0:T(8,128)(2,1)S(1)} async-done(((bf16[8,352,256]{2,1,0:T(8,128)(2,1)}), bf16[8,352,256]{2,1,0:T(8,128)(2,1)S(1)}, u32[]{:S(2)}, u32[]{:S(2)}) %all-to-all-start.1) | async-done | bytes 1441824 | tf_op jit(solution)/shard_map/all_to_all | solution.py:1131
  336.6 2.9 unchoose.1
  339.4 3.4 collective-permute-start.44
  344.1 4.6 %collective-permute-start.46 = (bf16[130,2304]{1,0:T(8,128)(2,1)}, bf16[130,2304]{1,0:T(8,128)(2,1)S(1)}, u32[]{:S(2)}, u32[]{:S(2)}) collective-permute-start(bf16[130,2304]{1,0:T(8,128)(2,1)} %get-tuple-element.80), channel_id=1, source_target_pairs={{1,2},{2,1},{3,0},{5,6},{6,5},{7,4},{9,10},{10,9},{11,8},{13,14},{... | collective-permute-start | bytes 1797128 | tf_op jit(solution)/shard_map/ppermute | solution.py:32
  348.7 11.8 %reduce-scatter.3.cloned.1.call-done = bf16[1,22,64,256]{3,2,1,0:T(8,128)(2,1)} async-done(((bf16[4,22,64,256]{3,2,1,0:T(8,128)(2,1)}), bf16[1,22,64,256]{3,2,1,0:T(8,128)(2,1)}) %reduce-scatter.3.cloned.1.call-update) | async-done | bytes 720912 | tf_op jit(solution)/shard_map/reduce_scatter | solution.py:172
  371.9 7.2 %collective-permute-done.45.refs_2_.refs_6_ = bf16[130,2304]{1,0:T(8,128)(2,1)S(1)} collective-permute-done((bf16[130,2304]{1,0:T(8,128)(2,1)}, bf16[130,2304]{1,0:T(8,128)(2,1)S(1)}, u32[]{:S(2)}, u32[]{:S(2)}) %collective-permute-start.45) | collective-permute-done | bytes 599072 | tf_op jit(solution)/shard_map/ppermute | solution.py:32
  379.0 28.6 %collective-permute-done.46.refs_3_.refs_7_ = bf16[130,2304]{1,0:T(8,128)(2,1)S(1)} collective-permute-done((bf16[130,2304]{1,0:T(8,128)(2,1)}, bf16[130,2304]{1,0:T(8,128)(2,1)S(1)}, u32[]{:S(2)}, u32[]{:S(2)}) %collective-permute-start.46) | collective-permute-done | bytes 599072 | tf_op jit(solution)/shard_map/ppermute | solution.py:32
  407.7 4.7 %interleave.1 = (bf16[130,4,2048]{2,1,0:T(4,128)(2,1)}, bf16[130,4,256]{2,1,0:T(4,128)(2,1)}) custom-call(s32[1]{0:T(128)} %bitcast.z_ref, bf16[130,2304]{1,0:T(8,128)(2,1)S(1)} %get-tuple-element.77.refs_0_.refs_4_, bf16[130,2304]{1,0:T(8,128)(2,1)S(1)} %collective-permute-done.44.refs_1_.refs_5_, ...), custom_call_target="tpu_custom_call" | custom-call | tf_op jit(solution)/shard_map/interleave/pallas_call | solution.py:430
  (226 shorter events, 113.8 us)
Async XLA Ops:
  10.7 46.0 %collective-permute-start.6 = (bf16[24,64,256]{2,1,0:T(8,128)(2,1)S(1)}, bf16[24,64,256]{2,1,0:T(8,128)(2,1)S(1)}, u32[]{:S(2)}, u32[]{:S(2)}) collective-permute-start(bf16[24,64,256]{2,1,0:T(8,128)(2,1)S(1)} %pack_weights.1), channel_id=1, source_target_pairs={{1,0},{2,1},{3,2},{5,4},{6,5},{7,6},{9,8},{10,9},{11,10},{13,12},{... | collective-permute-start | bytes 2359304 | tf_op jit(solution)/shard_map/ppermute | solution.py:139
  12.8 74.2 %collective-permute-start.3 = (bf16[24,64,256]{2,1,0:T(8,128)(2,1)S(1)}, bf16[24,64,256]{2,1,0:T(8,128)(2,1)}, u32[]{:S(2)}, u32[]{:S(2)}) collective-permute-start(bf16[24,64,256]{2,1,0:T(8,128)(2,1)S(1)} %pack_weights.1), channel_id=1, source_target_pairs={{0,1},{1,2},{2,3},{4,5},{5,6},{6,7},{8,9},{9,10},{10,11},{12,13},{... | collective-permute-start | bytes 2359304 | tf_op jit(solution)/shard_map/ppermute | solution.py:139
  22.4 34.2 %collective-permute-start = (bf16[130,2304]{1,0:T(8,128)(2,1)S(1)}, bf16[130,2304]{1,0:T(8,128)(2,1)S(1)}, u32[]{:S(2)}, u32[]{:S(2)}) collective-permute-start(bf16[130,2304]{1,0:T(8,128)(2,1)S(1)} %get-tuple-element.49), channel_id=1, source_target_pairs={{0,1},{1,0},{2,3},{4,5},{5,4},{6,7},{8,9},{9,8},{10,11},{12,13},{1... | collective-permute-start | bytes 1797128 | tf_op jit(solution)/shard_map/ppermute | solution.py:32
  25.2 49.8 %collective-permute-start.1 = (bf16[130,2304]{1,0:T(8,128)(2,1)S(1)}, bf16[130,2304]{1,0:T(8,128)(2,1)S(1)}, u32[]{:S(2)}, u32[]{:S(2)}) collective-permute-start(bf16[130,2304]{1,0:T(8,128)(2,1)S(1)} %get-tuple-element.50), channel_id=1, source_target_pairs={{0,2},{1,3},{2,0},{4,6},{5,7},{6,4},{8,10},{9,11},{10,8},{12,14},{... | collective-permute-start | bytes 1797128 | tf_op jit(solution)/shard_map/ppermute | solution.py:32
  26.6 60.4 %collective-permute-start.2 = (bf16[130,2304]{1,0:T(8,128)(2,1)S(1)}, bf16[130,2304]{1,0:T(8,128)(2,1)S(1)}, u32[]{:S(2)}, u32[]{:S(2)}) collective-permute-start(bf16[130,2304]{1,0:T(8,128)(2,1)S(1)} %get-tuple-element.51), channel_id=1, source_target_pairs={{0,3},{1,2},{2,1},{4,7},{5,6},{6,5},{8,11},{9,10},{10,9},{12,15},{... | collective-permute-start | bytes 1797128 | tf_op jit(solution)/shard_map/ppermute | solution.py:32
  56.7 44.4 %collective-permute-start.8 = (bf16[24,64,256]{2,1,0:T(8,128)(2,1)S(1)}, bf16[24,64,256]{2,1,0:T(8,128)(2,1)}, u32[]{:S(2)}, u32[]{:S(2)}) collective-permute-start(bf16[24,64,256]{2,1,0:T(8,128)(2,1)S(1)} %collective-permute-done.6), channel_id=1, source_target_pairs={{1,0},{2,1},{5,4},{6,5},{9,8},{10,9},{13,12},{14,13},{17,16},{18,1... | collective-permute-start | bytes 2359304 | tf_op jit(solution)/shard_map/ppermute | solution.py:139
  87.0 20.4 %collective-permute-start.4 = (bf16[24,64,256]{2,1,0:T(8,128)(2,1)}, bf16[24,64,256]{2,1,0:T(8,128)(2,1)}, u32[]{:S(2)}, u32[]{:S(2)}) collective-permute-start(bf16[24,64,256]{2,1,0:T(8,128)(2,1)} %collective-permute-done.3), channel_id=1, source_target_pairs={{1,2},{5,6},{9,10},{13,14},{17,18},{21,22},{25,26},{29,30}} | collective-permute-start | bytes 2359304 | tf_op jit(solution)/shard_map/ppermute | solution.py:139
  95.5 23.3 %all-to-all-start = ((bf16[8,352,256]{2,1,0:T(8,128)(2,1)}), bf16[8,352,256]{2,1,0:T(8,128)(2,1)S(1)}, u32[]{:S(2)}, u32[]{:S(2)}) async-start(bf16[8,352,256]{2,1,0:T(8,128)(2,1)} %copy-done.12), calls=%async_computation | async-start | bytes 2883584 | tf_op jit(solution)/shard_map/all_to_all | solution.py:925
  99.2 189.3 %reduce-scatter.5.cloned.1.call-start = ((), (), s32[]{:S(2)}) async-start(), calls=%async_computation.5 | async-start | bytes 1179648 | tf_op jit(solution)/shard_map/reduce_scatter | solution.py:1113
  99.6 20.3 %collective-permute-start.7 = (bf16[24,64,256]{2,1,0:T(8,128)(2,1)}, bf16[24,64,256]{2,1,0:T(8,128)(2,1)}, u32[]{:S(2)}, u32[]{:S(2)}) collective-permute-start(bf16[24,64,256]{2,1,0:T(8,128)(2,1)} %collective-permute-done.3), channel_id=1, source_target_pairs={{2,3},{6,7},{10,11},{14,15},{18,19},{22,23},{26,27},{30,31}} | collective-permute-start | bytes 2359304 | tf_op jit(solution)/shard_map/ppermute | solution.py:139
  101.1 19.2 %collective-permute-start.9 = (bf16[24,64,256]{2,1,0:T(8,128)(2,1)}, bf16[24,64,256]{2,1,0:T(8,128)(2,1)}, u32[]{:S(2)}, u32[]{:S(2)}) collective-permute-start(bf16[24,64,256]{2,1,0:T(8,128)(2,1)} %collective-permute-done.8), channel_id=1, source_target_pairs={{1,0},{5,4},{9,8},{13,12},{17,16},{21,20},{25,24},{29,28}} | collective-permute-start | bytes 2359304 | tf_op jit(solution)/shard_map/ppermute | solution.py:139
  107.4 13.0 %collective-permute-start.5 = (bf16[24,64,256]{2,1,0:T(8,128)(2,1)}, bf16[24,64,256]{2,1,0:T(8,128)(2,1)}, u32[]{:S(2)}, u32[]{:S(2)}) collective-permute-start(bf16[24,64,256]{2,1,0:T(8,128)(2,1)} %collective-permute-done.4), channel_id=1, source_target_pairs={{2,3},{6,7},{10,11},{14,15},{18,19},{22,23},{26,27},{30,31}} | collective-permute-start | bytes 2359304 | tf_op jit(solution)/shard_map/ppermute | solution.py:139
  140.0 29.1 %collective-permute-start.11 = (bf16[2,2,416,256]{3,2,1,0:T(8,128)(2,1)S(1)}, bf16[2,2,416,256]{3,2,1,0:T(8,128)(2,1)S(1)}, u32[]{:S(2)}, u32[]{:S(2)}) collective-permute-start(bf16[2,2,416,256]{3,2,1,0:T(8,128)(2,1)S(1)} %slice.126), channel_id=1, source_target_pairs={{0,8},{4,12},{8,0},{12,4},{16,24},{20,28},{24,16},{28,20},{1,9},{5... | collective-permute-start | bytes 2555912 | tf_op jit(solution)/shard_map/ppermute | solution.py:32
  141.8 29.0 %collective-permute-start.13 = (bf16[2,2,416,256]{3,2,1,0:T(8,128)(2,1)S(1)}, bf16[2,2,416,256]{3,2,1,0:T(8,128)(2,1)S(1)}, u32[]{:S(2)}, u32[]{:S(2)}) collective-permute-start(bf16[2,2,416,256]{3,2,1,0:T(8,128)(2,1)S(1)} %slice.222), channel_id=1, source_target_pairs={{0,16},{4,20},{8,24},{12,28},{16,0},{20,4},{24,8},{28,12},{1,17},{... | collective-permute-start | bytes 2555912 | tf_op jit(solution)/shard_map/ppermute | solution.py:32
  143.4 22.3 %collective-permute-start.21 = (bf16[256,256]{1,0:T(8,128)(2,1)S(1)}, bf16[256,256]{1,0:T(8,128)(2,1)S(1)}, u32[]{:S(2)}, u32[]{:S(2)}) collective-permute-start(bf16[256,256]{1,0:T(8,128)(2,1)S(1)} %get-tuple-element.94), channel_id=1, source_target_pairs={{0,24},{4,28},{8,16},{12,20},{16,8},{20,12},{24,0},{28,4},{1,25},{... | collective-permute-start | bytes 393224 | tf_op jit(solution)/shard_map/ppermute | solution.py:32
  143.9 24.3 %collective-permute-start.20 = (bf16[256,256]{1,0:T(8,128)(2,1)S(1)}, bf16[256,256]{1,0:T(8,128)(2,1)S(1)}, u32[]{:S(2)}, u32[]{:S(2)}) collective-permute-start(bf16[256,256]{1,0:T(8,128)(2,1)S(1)} %get-tuple-element.94), channel_id=1, source_target_pairs={{0,16},{4,20},{8,24},{12,28},{16,0},{20,4},{24,8},{28,12},{1,17},{... | collective-permute-start | bytes 393224 | tf_op jit(solution)/shard_map/ppermute | solution.py:32
  145.5 22.7 %collective-permute-start.19 = (bf16[256,256]{1,0:T(8,128)(2,1)S(1)}, bf16[256,256]{1,0:T(8,128)(2,1)S(1)}, u32[]{:S(2)}, u32[]{:S(2)}) collective-permute-start(bf16[256,256]{1,0:T(8,128)(2,1)S(1)} %get-tuple-element.94), channel_id=1, source_target_pairs={{0,8},{4,12},{8,0},{12,4},{16,24},{20,28},{24,16},{28,20},{1,9},{5... | collective-permute-start | bytes 393224 | tf_op jit(solution)/shard_map/ppermute | solution.py:32
  169.1 20.4 %collective-permute-start.22 = (bf16[4,256,256]{2,1,0:T(8,128)(2,1)}, bf16[4,256,256]{2,1,0:T(8,128)(2,1)}, u32[]{:S(2)}, u32[]{:S(2)}) collective-permute-start(bf16[4,256,256]{2,1,0:T(8,128)(2,1)} %pad_maximum_fusion.4.near_ref), channel_id=1, source_target_pairs={{0,4},{4,0},{8,12},{12,8},{16,20},{20,16},{24,28},{28,24},{1,5},{5... | collective-permute-start | bytes 1572872 | tf_op jit(solution)/shard_map/ppermute | solution.py:32
  169.3 12.3 %collective-permute-start.12 = (bf16[2,416,256]{2,1,0:T(8,128)(2,1)S(1)}, bf16[2,416,256]{2,1,0:T(8,128)(2,1)S(1)}, u32[]{:S(2)}, u32[]{:S(2)}) collective-permute-start(bf16[2,416,256]{2,1,0:T(8,128)(2,1)S(1)} %get-tuple-element.91), channel_id=1, source_target_pairs={{0,16},{4,20},{8,24},{12,28},{16,0},{20,4},{24,8},{28,12},{1,17},{... | collective-permute-start | bytes 1277960 | tf_op jit(solution)/shard_map/ppermute | solution.py:32
  171.0 12.0 %collective-permute-start.14 = (bf16[2,416,256]{2,1,0:T(8,128)(2,1)S(1)}, bf16[2,416,256]{2,1,0:T(8,128)(2,1)S(1)}, u32[]{:S(2)}, u32[]{:S(2)}) collective-permute-start(bf16[2,416,256]{2,1,0:T(8,128)(2,1)S(1)} %get-tuple-element.89), channel_id=1, source_target_pairs={{0,8},{4,12},{8,0},{12,4},{16,24},{20,28},{24,16},{28,20},{1,9},{5... | collective-permute-start | bytes 1277960 | tf_op jit(solution)/shard_map/ppermute | solution.py:32
  224.3 11.4 %collective-permute-start.36 = (bf16[2,416,256]{2,1,0:T(8,128)(2,1)S(1)}, bf16[2,416,256]{2,1,0:T(8,128)(2,1)S(1)}, u32[]{:S(2)}, u32[]{:S(2)}) collective-permute-start(bf16[2,416,256]{2,1,0:T(8,128)(2,1)S(1)} %get-tuple-element.103), channel_id=1, source_target_pairs={{0,16},{4,20},{8,24},{12,28},{16,0},{20,4},{24,8},{28,12},{1,17},{... | collective-permute-start | bytes 1277960 | tf_op jit(solution)/shard_map/ppermute | solution.py:32
  235.0 18.7 %collective-permute-start.37 = (bf16[2,2,416,256]{3,2,1,0:T(8,128)(2,1)}, bf16[2,2,416,256]{3,2,1,0:T(8,128)(2,1)}, u32[]{:S(2)}, u32[]{:S(2)}) collective-permute-start(bf16[2,2,416,256]{3,2,1,0:T(8,128)(2,1)} %pad_maximum_fusion.2), channel_id=1, source_target_pairs={{0,16},{4,20},{8,24},{12,28},{16,0},{20,4},{24,8},{28,12},{1,17},{... | collective-permute-start | bytes 2555912 | tf_op jit(solution)/shard_map/ppermute | solution.py:32
  237.4 18.5 %collective-permute-start.38 = (bf16[2,2,416,256]{3,2,1,0:T(8,128)(2,1)}, bf16[2,2,416,256]{3,2,1,0:T(8,128)(2,1)}, u32[]{:S(2)}, u32[]{:S(2)}) collective-permute-start(bf16[2,2,416,256]{3,2,1,0:T(8,128)(2,1)} %pad_maximum_fusion.3), channel_id=1, source_target_pairs={{0,8},{4,12},{8,0},{12,4},{16,24},{20,28},{24,16},{28,20},{1,9},{5... | collective-permute-start | bytes 2555912 | tf_op jit(solution)/shard_map/ppermute | solution.py:32
  237.8 122.7 %reduce-scatter.3.cloned.1.call-start = ((), (), s32[]{:S(2)}) async-start(), calls=%async_computation.4 | async-start | bytes 3604480 | tf_op jit(solution)/shard_map/reduce_scatter | solution.py:172
  237.8 18.6 %collective-permute-start.39 = (bf16[4,416,256]{2,1,0:T(8,128)(2,1)}, bf16[4,416,256]{2,1,0:T(8,128)(2,1)}, u32[]{:S(2)}, u32[]{:S(2)}) collective-permute-start(bf16[4,416,256]{2,1,0:T(8,128)(2,1)} %copy-done.6), channel_id=1, source_target_pairs={{0,4},{4,0},{8,12},{12,8},{16,20},{20,16},{24,28},{28,24},{1,5},{5... | collective-permute-start | bytes 2555912 | tf_op jit(solution)/shard_map/ppermute | solution.py:32
  290.3 27.4 %collective-permute-start.47 = (f32[144,256]{1,0:T(8,128)}, f32[144,256]{1,0:T(8,128)}, u32[]{:S(2)}, u32[]{:S(2)}) collective-permute-start(f32[144,256]{1,0:T(8,128)} %get-tuple-element.108), channel_id=1, source_target_pairs={{0,1},{1,0},{2,3},{3,2},{4,5},{5,4},{6,7},{7,6},{8,9},{9,8},{10,11... | collective-permute-start | bytes 442376 | tf_op jit(solution)/shard_map/ppermute | solution.py:32
  290.8 26.8 %collective-permute-start.48 = (f32[144,256]{1,0:T(8,128)}, f32[144,256]{1,0:T(8,128)}, u32[]{:S(2)}, u32[]{:S(2)}) collective-permute-start(f32[144,256]{1,0:T(8,128)} %get-tuple-element.109), channel_id=1, source_target_pairs={{0,2},{1,3},{2,0},{3,1},{4,6},{5,7},{6,4},{7,5},{8,10},{9,11},{10,... | collective-permute-start | bytes 442376 | tf_op jit(solution)/shard_map/ppermute | solution.py:32
  293.2 28.3 %collective-permute-start.49 = (f32[144,256]{1,0:T(8,128)S(1)}, f32[144,256]{1,0:T(8,128)}, u32[]{:S(2)}, u32[]{:S(2)}) collective-permute-start(f32[144,256]{1,0:T(8,128)S(1)} %get-tuple-element.107), channel_id=1, source_target_pairs={{0,3},{1,2},{2,1},{3,0},{4,7},{5,6},{6,5},{7,4},{8,11},{9,10},{10,... | collective-permute-start | bytes 442376 | tf_op jit(solution)/shard_map/ppermute | solution.py:32
  313.3 23.3 %all-to-all-start.1 = ((bf16[8,352,256]{2,1,0:T(8,128)(2,1)}), bf16[8,352,256]{2,1,0:T(8,128)(2,1)S(1)}, u32[]{:S(2)}, u32[]{:S(2)}) async-start(bf16[8,352,256]{2,1,0:T(8,128)(2,1)} %features_backward.1), calls=%async_computation.1 | async-start | bytes 2883584 | tf_op jit(solution)/shard_map/all_to_all | solution.py:1131
  339.4 32.4 %collective-permute-start.44 = (bf16[130,2304]{1,0:T(8,128)(2,1)}, bf16[130,2304]{1,0:T(8,128)(2,1)S(1)}, u32[]{:S(2)}, u32[]{:S(2)}) collective-permute-start(bf16[130,2304]{1,0:T(8,128)(2,1)} %get-tuple-element.78), channel_id=1, source_target_pairs={{0,1},{1,0},{3,2},{4,5},{5,4},{7,6},{8,9},{9,8},{11,10},{12,13},{1... | collective-permute-start | bytes 1797128 | tf_op jit(solution)/shard_map/ppermute | solution.py:32
  342.8 36.2 %collective-permute-start.45 = (bf16[130,2304]{1,0:T(8,128)(2,1)}, bf16[130,2304]{1,0:T(8,128)(2,1)S(1)}, u32[]{:S(2)}, u32[]{:S(2)}) collective-permute-start(bf16[130,2304]{1,0:T(8,128)(2,1)} %get-tuple-element.79), channel_id=1, source_target_pairs={{0,2},{2,0},{3,1},{4,6},{6,4},{7,5},{8,10},{10,8},{11,9},{12,14},{... | collective-permute-start | bytes 1797128 | tf_op jit(solution)/shard_map/ppermute | solution.py:32
  344.1 63.6 %collective-permute-start.46 = (bf16[130,2304]{1,0:T(8,128)(2,1)}, bf16[130,2304]{1,0:T(8,128)(2,1)S(1)}, u32[]{:S(2)}, u32[]{:S(2)}) collective-permute-start(bf16[130,2304]{1,0:T(8,128)(2,1)} %get-tuple-element.80), channel_id=1, source_target_pairs={{1,2},{2,1},{3,0},{5,6},{6,5},{7,4},{9,10},{10,9},{11,8},{13,14},{... | collective-permute-start | bytes 1797128 | tf_op jit(solution)/shard_map/ppermute | solution.py:32
  (57 other events, 812.9 us)
Sparse Core Ops, SparseCore 0:
  237.9 50.5 reduce-scatter.4
  290.8 69.6 reduce-scatter.2
